TPU v7x, 32 devices: a whole 2x2x4 slice. The times are simulated.
32 devices in a mesh: gx: 4 (over y, core), gy: 4 (over z), gz: 2 (over x).
Axes of the slice: x: 2, y: 2, z: 4, core: 2. Of those that a mesh axis runs over, the one named last changes fastest.
Arguments:
- positions: float32 [4, 4, 2, 3, 512], P('gx', 'gy', 'gz'), may hold values from 0 to 1
- attributes: bfloat16 [4, 4, 2, 512, 128], P('gx', 'gy', 'gz'), may hold values from -6 to 6
- edge_center: int32 [4, 4, 2, 6144], P('gx', 'gy', 'gz'), may hold values from 0 to 511
- edge_other: int32 [4, 4, 2, 6144], P('gx', 'gy', 'gz'), may hold values from 0 to 2687
- edge_count: int32 [4, 4, 2], P('gx', 'gy', 'gz'), may hold values from 1536 to 6144, as said below
- rim_rows: int32 [4, 4, 2, 8, 128], P('gx', 'gy', 'gz'), may hold values from 0 to 511
- z_rows: int32 [4, 4, 2, 128], P('gx', 'gy', 'gz'), may hold values from 0 to 2559
- w_emb: bfloat16 [128, 256], replicated, may hold values from -0.5 to 0.5
- w_rbf: float32 [8, 256], replicated, may hold values from -2 to 2
- w_chan: bfloat16 [256, 64], replicated, may hold values from -0.375 to 0.375
- w_lat: bfloat16 [256, 256], replicated, may hold values from -0.375 to 0.375
- w_ten: bfloat16 [192, 256], replicated, may hold values from -0.4375 to 0.4375
- w_out: float32 [256], replicated, may hold values from -0.375 to 0.375
Outputs:
- atom_energy: float32 [4, 4, 2, 512], P('gx', 'gy', 'gz')
- forces: float32 [4, 4, 2, 3, 512], P('gx', 'gy', 'gz')
Inputs may be any that keep to these rules, and one draw needn't show every extreme that they name: `edge_count`: a multiple of 128; a device's edge slots below its count are live; some device has 6144.
All inputs are finite; a program needn't handle non-finite values.
Results may differ from a plain program's by a relative error of at most 0.005.
Values may be sent and summed in bfloat16 or wider, within the bound.
No kernel may reach another device: no remote copies, remote signals or barrier semaphores. Data moves between devices by JAX's collectives and lax.ppermute only.
A program may use at most 64 MiB of HBM per device.

v0:
```python
import collections

import jax
import jax.numpy as jnp
from jax import lax
from jax.experimental import pallas as pl
from jax.experimental.pallas import tpu as pltpu
from jax.sharding import PartitionSpec as P

f32 = jnp.float32
bf16 = jnp.bfloat16
LANES = 128
PARTS = 16
BLOCK = 512
WINDOW = 768
ROOT3 = 3.0**0.5
BANDS = (0, 1, 1, 1, 2, 2, 2, 2, 2)

rim_cells = [(0, 0), (0, 1), (0, 2), (1, 0), (1, 2), (2, 0), (2, 1), (2, 2)]
cycle_cells = [(p, q) for p in range(5) for q in range(5) if p in (0, 4) or q in (0, 4)]


def source_of(position):
    if position == 0:
        return (-1, 2)
    if position == 4:
        return (1, 0)
    return (0, position - 1)


routes = {}
for _cycle, (_p, _q) in enumerate(cycle_cells):
    (_sx, _a), (_sy, _b) = source_of(_p), source_of(_q)
    routes.setdefault((_sx, _sy), []).append((_cycle, rim_cells.index((_a, _b))))
sides = [(0, -1), (0, 1), (-1, 0), (1, 0)]


def dot(a, b):
    return lax.dot_general(a, b, (((1,), (0,)), ((), ())), preferred_element_type=f32)


def dot_t(a, b):
    return lax.dot_general(a, b, (((1,), (1,)), ((), ())), preferred_element_type=f32)


def rows_of(shape):
    return lax.broadcasted_iota(jnp.int32, shape, 0)


def one_hot(index, size):
    return jnp.where(rows_of((size, index.shape[1])) == index, 1.0, 0.0)


def halves(values):
    upper = values.astype(bf16).astype(f32)
    return upper, values - upper


def masked(hot_low, high16, value):
    mask = jnp.where(high16 == value, 1.0, 0.0).astype(bf16)
    size, lanes = hot_low.shape
    return (hot_low.reshape(size // 16, 16, lanes) * mask[None]).reshape(size, lanes)


def half_silu(x):
    half = 0.5 * x
    return (0.5 * (half * (1.0 + jnp.tanh(half)))).astype(bf16)


def pack_kernel(pos_ref, attr_ref, picks_ref, own_ref, *rest):
    sends, parts = rest[:4], rest[4]
    atoms, width = attr_ref.shape
    eye = jnp.where(
        rows_of((width, width)) == lax.broadcasted_iota(jnp.int32, (width, width), 1), 1.0, 0.0
    ).astype(bf16)
    own_ref[0:width, :] = dot_t(eye, attr_ref[...]).astype(bf16)
    parts[...] = jnp.zeros_like(parts)
    for d in range(3):
        parts[d : d + 1, :], parts[3 + d : 4 + d, :] = halves(pos_ref[d])
    own_ref[width : width + PARTS, :] = parts[...].astype(bf16)
    packed = own_ref[...]
    for rim in range(8):
        hot = one_hot(picks_ref[rim : rim + 1, :], atoms).astype(bf16)
        cell = dot(packed, hot).astype(bf16)
        for way, send in zip(sides, sends):
            for slot, (_, source) in enumerate(routes[way]):
                if source == rim:
                    send[:, slot * LANES : (slot + 1) * LANES] = cell


def corner_kernel(minus_ref, plus_ref, to_plus_ref, to_minus_ref):
    first, last = slice(0, LANES), slice(2 * LANES, 3 * LANES)
    for slot, ref in enumerate((minus_ref, plus_ref)):
        lanes = slice(slot * LANES, (slot + 1) * LANES)
        to_plus_ref[:, lanes] = ref[:, last]
        to_minus_ref[:, lanes] = ref[:, first]


def slab_kernel(own_ref, picks_ref, *rest):
    got, corners, (inner_ref, send_ref, parts) = rest[:4], rest[4:6], rest[6:]
    atoms = own_ref.shape[1]
    height = own_ref.shape[0]
    width = height - PARTS
    inner_len = inner_ref.shape[1]
    inner_ref[:, 0:atoms] = own_ref[...]
    parts[...] = jnp.zeros_like(parts)
    parts[0:6, 0:atoms] = own_ref[width:height, :].astype(f32)[0:6]
    arrivals = []
    for way, ref in zip(sides, got):
        for slot, (cycle, _) in enumerate(routes[way]):
            arrivals.append((way, ref, slot, cycle))
    for sx, ref in zip((-1, 1), corners):
        for slot, sy in enumerate((-1, 1)):
            arrivals.append(((sx, sy), ref, slot, routes[(sx, sy)][0][0]))
    for way, ref, slot, cycle in arrivals:
        lanes = slice(slot * LANES, (slot + 1) * LANES)
        into = slice(atoms + cycle * LANES, atoms + (cycle + 1) * LANES)
        inner_ref[0:width, into] = ref[0:width, lanes]
        arrived = ref[width:height, lanes].astype(f32)
        joined = arrived[0:3] + arrived[3:6]
        axis = rows_of((3, LANES))
        shift = jnp.where(axis == 0, float(way[0]), jnp.where(axis == 1, float(way[1]), 0.0))
        upper, lower = halves(joined + shift)
        parts[0:3, into] = upper
        parts[3:6, into] = lower
    inner_ref[width:height, :] = parts[...].astype(bf16)
    hot = one_hot(picks_ref[8:9, :], inner_len).astype(bf16)
    send_ref[...] = dot(inner_ref[...], hot).astype(bf16)


def unit(size):
    lanes = lax.broadcasted_iota(jnp.int32, (size, size), 1)
    return jnp.where(rows_of((size, size)) == lanes, 1.0, 0.0)


def weights_kernel(
    stacked_ref,
    small_ref,
    emb_t_ref,
    rad_ref,
    chan_ref,
    w_chan_t_ref,
    lat_t_ref,
    ten_t_ref,
    back_ref,
    out_ref,
    rbf_ref,
    scratch,
):
    features = stacked_ref.shape[1]
    width = emb_t_ref.shape[1]
    inner = back_ref.shape[0]
    w_emb = stacked_ref[0:width]
    w_back = stacked_ref[width : width + inner]
    w_chan_t = stacked_ref[width + inner :]
    eye = unit(features)
    eye_b = eye.astype(bf16)
    emb_t_ref[...] = dot_t(eye_b, w_emb).astype(bf16)
    chan_ref[...] = dot_t(eye_b, w_chan_t).astype(bf16)
    w_chan_t_ref[...] = w_chan_t
    turned = (0.5 * dot_t(eye_b, w_back)).astype(bf16)
    lat_t_ref[...] = turned[:, 0:features]
    ten_t_ref[...] = turned[:, features:]
    back_ref[...] = w_back
    column = jnp.sum(eye * small_ref[8:9, :], axis=1, keepdims=True)
    out_ref[...] = jnp.broadcast_to(column, out_ref.shape)
    upper, lower = halves(0.5 * small_ref[0:8, :])
    rbf_ref[...] = jnp.concatenate([upper, lower], axis=0).astype(bf16)
    scratch[...] = jnp.zeros_like(scratch)
    for start, value in ((0, upper), (8, upper), (16, lower), (24, lower)):
        scratch[start : start + 8, :] = value
    rad_ref[...] = dot_t(eye_b, scratch[...].astype(bf16)).astype(bf16)


def embed_kernel(inner_ref, w_emb_ref, feat_ref, place_ref):
    width = w_emb_ref.shape[1]
    inner_len = inner_ref.shape[1]
    for first in range(0, inner_len, 512):
        raw = dot(w_emb_ref[...], inner_ref[0:width, first : first + 512])
        feat_ref[:, first : first + 512] = half_silu(raw)
    parts = inner_ref[width:, :].astype(f32)
    place_ref[...] = jnp.zeros_like(place_ref)
    for high in range(inner_len // LANES):
        place_ref[0:6, high, :] = parts[0:6, high * LANES : (high + 1) * LANES]


def bucket_kernel(count_ref, ends_ref, center_ref, other_ref, meta_ref, marks_s, rows_s, low_s):
    lines = ends_ref.shape[0] // 2
    keys = marks_s.shape[0] // lines
    groups = keys // 2
    count = count_ref[0]
    c, o = ends_ref[0:lines, :], ends_ref[lines:, :]
    shape = (lines, LANES)
    order = rows_of(shape) * LANES + lax.broadcasted_iota(jnp.int32, shape, 1)
    key = lax.shift_right_logical(c, 8) * groups + lax.shift_right_logical(o, 8)
    key = jnp.where(order < count, key, -1)
    for k in range(keys):
        marks_s[k * lines : (k + 1) * lines, :] = jnp.where(key == k, 1.0, 0.0).astype(bf16)
    square = (LANES, LANES)
    tri = jnp.where(rows_of(square) < lax.broadcasted_iota(jnp.int32, square, 1), 1.0, 0.0)
    tri = tri.astype(bf16)
    tall = (lines, lines)
    below = jnp.where(lax.broadcasted_iota(jnp.int32, tall, 1) < rows_of(tall), 1.0, 0.0)
    marks = marks_s[...]
    inside = dot(marks, tri)
    totals = dot(marks, jnp.ones(square, bf16))
    lane = lax.broadcasted_iota(jnp.int32, shape, 1)
    by_key = jnp.zeros(shape, f32)
    for k in range(keys):
        by_key = jnp.where(lane == k, totals[k * lines : (k + 1) * lines], by_key)
    before = dot(below.astype(bf16), by_key.astype(bf16))
    everything = jnp.broadcast_to(jnp.sum(by_key, axis=0, keepdims=True), (16, LANES))
    upper, lower = halves(everything)
    start = (dot(upper.astype(bf16), tri) + dot(lower.astype(bf16), tri))[0:1]
    row_lane = lane[0:1]
    first = jnp.sum(jnp.where(row_lane < groups, everything[0:1], 0.0), axis=1, keepdims=True)
    second = jnp.sum(jnp.where(row_lane >= groups, everything[0:1], 0.0), axis=1, keepdims=True)
    first_blocks = jnp.floor((first + (BLOCK - 1)) * (1.0 / BLOCK))
    blocks = first_blocks + jnp.floor((second + (BLOCK - 1)) * (1.0 / BLOCK))
    start = start + jnp.where(row_lane >= groups, first_blocks * BLOCK - first, 0.0)
    offset = before + start
    slot = jnp.full(shape, -1.0, f32)
    for k in range(keys):
        place = inside[k * lines : (k + 1) * lines] + offset[:, k : k + 1]
        slot = jnp.where(key == k, place, slot)
    slot = slot.astype(jnp.int32)
    slot_high = lax.shift_right_arithmetic(slot, 7)
    slot_low = lax.bitwise_and(slot, LANES - 1)
    highs = center_ref.shape[0]
    values = [
        jnp.ones(shape, f32),
        lax.bitwise_and(c, 255).astype(f32),
        lax.shift_right_logical(o, 7).astype(f32),
        lax.bitwise_and(o, LANES - 1).astype(f32),
    ]
    for line in range(lines):
        lanes = slice(line * LANES, (line + 1) * LANES)
        high = one_hot(slot_high[line : line + 1], highs)
        rows_s[:, lanes] = jnp.concatenate(
            [high * value[line : line + 1] for value in values], axis=0
        ).astype(bf16)
        low_s[:, lanes] = one_hot(slot_low[line : line + 1], LANES).astype(bf16)
    placed = dot_t(rows_s[...], low_s[...])
    center = placed[highs : 2 * highs] + placed[0:highs] - 1.0
    other = placed[2 * highs : 3 * highs] * float(LANES) + placed[3 * highs :]
    center_ref[...] = center.astype(jnp.int32)
    other_ref[...] = other.astype(jnp.int32)
    group = jnp.floor(other * (1.0 / 256.0))
    none = float(groups)
    low = jnp.min(jnp.where(center >= 0.0, group, none), axis=1, keepdims=True)
    high = jnp.max(jnp.where(center >= 0.0, group, -1.0), axis=1, keepdims=True)
    block = lax.broadcasted_iota(jnp.int32, (highs, LANES), 1)
    line_of = rows_of((highs, LANES)) // (BLOCK // LANES) == block
    low = jnp.min(jnp.where(line_of, low, none), axis=0, keepdims=True)
    high = jnp.max(jnp.where(line_of, high, -1.0), axis=0, keepdims=True)
    low = jnp.where(high < 0.0, 0.0, low)
    high = jnp.where(high < 0.0, 0.0, high)
    meta_ref[0:1, :] = jnp.broadcast_to(first_blocks, (1, LANES)).astype(jnp.int32)
    meta_ref[1:2, :] = jnp.broadcast_to(blocks, (1, LANES)).astype(jnp.int32)
    meta_ref[2:3, :] = low.astype(jnp.int32)
    meta_ref[3:4, :] = high.astype(jnp.int32)


def harmonic_rows(x, y, z):
    return [
        None,
        x,
        y,
        z,
        ROOT3 * x * y,
        ROOT3 * y * z,
        ROOT3 * z * x,
        0.5 * ROOT3 * (x * x - y * y),
        0.5 * (3.0 * z * z - 1.0),
    ]


def fold8(values):
    return jnp.sum(values.reshape(values.shape[0] // 8, 8, values.shape[1]), axis=0)


FIELDS = (
    ["hot", "extra", "center_hot", "low_o", "latent", "slope", "chan"]
    + ["geo", "dlat", "dharm", "tensor", "acc_o", "acc_c"]
)
Scratch = collections.namedtuple("Scratch", FIELDS)


def edge_kernel(
    meta_ref,
    lift_ref,
    centers_ref,
    others_ref,
    feat_in_ref,
    place_in_ref,
    slab_ref,
    w_emb_ref,
    w_rad_ref,
    w_chan_t_ref,
    w_chan_ref,
    w_lat_t_ref,
    w_ten_t_ref,
    w_back_ref,
    w_out_ref,
    w_rbf_ref,
    grad_ref,
    slab_grad_ref,
    energy_ref,
    feat,
    feat_c,
    place,
    place_b,
    own_b,
    tensor_b,
    *scratch,
):
    names = len(scratch) // 2
    even, odd = (Scratch(*scratch[side * names : (side + 1) * names]) for side in range(2))
    eb = centers_ref.shape[2]
    width = w_emb_ref.shape[1]
    features = feat_in_ref.shape[0]
    inner_len = feat_in_ref.shape[1]
    table = inner_len + LANES
    highs = table // LANES
    span = tensor_b.shape[2]
    halves_n = tensor_b.shape[0]
    chans = w_chan_t_ref.shape[0]
    hpad = place_in_ref.shape[1]
    first_blocks = meta_ref[0, 0]
    total_blocks = meta_ref[1, 0]
    pairs = total_blocks // 2

    feat[:, 0:inner_len] = feat_in_ref[...]
    raw = dot(w_emb_ref[...], slab_ref[0:width, :])
    feat[:, inner_len:table] = half_silu(raw)
    feat[:, table:] = jnp.zeros((features, feat.shape[1] - table), bf16)
    for half in range(halves_n):
        feat_c[half, :, 0:span] = feat_in_ref[:, half * span : (half + 1) * span]
        feat_c[half, :, span:] = w_rad_ref[...]
    place[...] = place_in_ref[...]
    arrived = slab_ref[width:, :].astype(f32)
    joined = arrived[0:3] + arrived[3:6]
    joined = joined + jnp.where(rows_of((3, LANES)) == 2, lift_ref[0], 0.0)
    upper, lower = halves(joined)
    place[0:3, highs - 1, :] = upper
    place[3:6, highs - 1, :] = lower
    place_b[...] = place[...].reshape(6 * hpad, LANES).astype(bf16)
    own_b[...] = place[:, 0:8, :].reshape(48, LANES).astype(bf16)
    for own in (even, odd):
        own.hot[WINDOW + span + 32 :, :] = jnp.zeros((LANES - 32, eb), bf16)
        for ref in (own.extra, own.tensor, own.acc_o, own.acc_c):
            ref[...] = jnp.zeros_like(ref)

    def half_of(b):
        return jnp.where(b >= first_blocks, 1, 0)

    def each_block(run):
        def step(pair, carry):
            run([(even, 2 * pair, pair), (odd, 2 * pair + 1, pair)])
            return carry

        lax.fori_loop(0, pairs, step, 0)

        @pl.when(total_blocks > 2 * pairs)
        def _():
            run([(even, 2 * pairs, pairs)])

    def prepare(side):
        own_s, b, at = side
        hot = own_s.hot
        slot_c = centers_ref[b]
        o = others_ref[b]
        live = jnp.where(slot_c >= 0, 1.0, 0.0)
        c = jnp.maximum(slot_c, 0)
        half = half_of(b)
        c_high = lax.shift_right_logical(c, 7)
        o_high = lax.shift_right_logical(o, 7)
        hot_c = one_hot(lax.bitwise_and(c, LANES - 1), LANES).astype(bf16)
        hot_o = one_hot(lax.bitwise_and(o, LANES - 1), LANES).astype(bf16)
        own_s.low_o[at] = hot_o
        c_high16 = jnp.broadcast_to(c_high, (16, eb))
        o_high16 = jnp.broadcast_to(o_high, (16, eb))
        shift = 2 * meta_ref[2, b]
        for high in range(WINDOW // LANES):
            rows = slice(high * LANES, (high + 1) * LANES)
            hot[rows, :] = masked(hot_o, o_high16 - shift, high)
        own = jnp.concatenate(
            [masked(hot_c, c_high16, high) for high in range(span // LANES)], axis=0
        )
        own_s.center_hot[at] = own
        hot[WINDOW : WINDOW + span, :] = own

        picked = dot(place_b[...], hot_o)
        picked = (picked[0 : 3 * hpad] + picked[3 * hpad :]).reshape(3, hpad, eb)
        po = jnp.sum(picked * one_hot(o_high, hpad)[None], axis=1)
        picked = dot(own_b[...], hot_c)
        picked = (picked[0:24] + picked[24:48]).reshape(3, 8, eb)
        c_whole = c_high + half * (span // LANES)
        pc = jnp.sum(picked * one_hot(c_whole, 8)[None], axis=1)
        sep = po - pc
        rx, ry, rz = sep[0:1], sep[1:2], sep[2:3]
        squared = rx * rx + ry * ry + rz * rz
        inv_d = lax.rsqrt(squared + 0.25)
        dist = (squared + 0.25) * inv_d
        env = 1.0 / (1.0 + squared * squared * (1.0 / 16.0))
        x, y, z = rx * inv_d, ry * inv_d, rz * inv_d
        for row, value in enumerate((x, y, z, inv_d, dist, env, squared, live)):
            own_s.geo[at, row : row + 1, :] = value
        mu = 0.5 + 0.4 * rows_of((8, eb)).astype(f32)
        u = (dist - mu) * 2.0
        upper, lower = halves(jnp.exp(-(u * u)) * env)
        radial = jnp.concatenate([upper, lower], axis=0).astype(bf16)
        hot[WINDOW + span : WINDOW + span + 16, :] = radial
        hot[WINDOW + span + 16 : WINDOW + span + 32, :] = radial
        return x, y, z, live, own

    def window(group):
        return feat[:, pl.ds(pl.multiple_of(group * 256, 256), WINDOW)]

    def windows_of(side):
        b = side[1]
        return (meta_ref[3, b] - meta_ref[2, b]) // (WINDOW // 256) + 1

    def further_windows(side):
        own_s, b, _ = side
        windows = windows_of(side)

        @pl.when(windows > 1)
        def _():
            o = others_ref[b]
            hot_o = one_hot(lax.bitwise_and(o, LANES - 1), LANES).astype(bf16)
            o_high16 = jnp.broadcast_to(lax.shift_right_logical(o, 7), (16, eb))

            def add(index, carry):
                group = meta_ref[2, b] + index * (WINDOW // 256)
                hot = jnp.concatenate(
                    [
                        masked(hot_o, o_high16 - 2 * group, high)
                        for high in range(WINDOW // LANES)
                    ],
                    axis=0,
                )
                own_s.extra[...] += dot(window(group), hot)
                return carry

            lax.fori_loop(1, windows, add, 0)

    def clear_windows(side):
        @pl.when(windows_of(side) > 1)
        def _():
            side[0].extra[...] = jnp.zeros_like(side[0].extra)

    def mix(side):
        own_s, b, _ = side
        mixed = dot(window(meta_ref[2, b]), own_s.hot[0:WINDOW, :])
        mixed = mixed + dot(feat_c[half_of(b)], own_s.hot[WINDOW:, :])
        return mixed + own_s.extra[...]

    def activate(side, mixed):
        own_s, _, at = side
        up = 1.0 + jnp.tanh(mixed)
        value = mixed * up
        latent = value.astype(bf16)
        own_s.latent[at] = latent
        own_s.slope[at] = (up + value * (2.0 - up)).astype(bf16)
        return latent

    def spread(side, latent, geo):
        own_s, _, at = side
        x, y, z, live, _ = geo
        chan = dot(w_chan_t_ref[...], latent) * live
        own_s.chan[at] = chan
        return jnp.concatenate(
            [
                (chan if h is None else chan * h).astype(bf16)
                for h in harmonic_rows(x, y, z)
            ],
            axis=0,
        )

    def gather_tensor(side):
        own_s, b, at = side
        return dot(tensor_b[half_of(b)], own_s.center_hot[at])

    def add_tensor(side, products, hot):
        own_s, b, _ = side
        own_s.tensor[half_of(b)] += dot_t(products, hot)

    def first_pass(sides):
        geos, mixed = [], []
        for side in sides:
            further_windows(side)
        for side in sides:
            geos.append(prepare(side))
            mixed.append(mix(side))
        products = []
        for side, geo, values in zip(sides, geos, mixed):
            products.append(spread(side, activate(side, values), geo))
        for side, geo, values in zip(sides, geos, products):
            add_tensor(side, values, geo[4])
        for side in sides:
            clear_windows(side)

    each_block(first_pass)
    tensor_b[...] = (0.125 * (even.tensor[...] + odd.tensor[...])).astype(bf16)
    for own in (even, odd):
        own.tensor[...] = jnp.zeros_like(own.tensor)

    def invariants(side, gathered):
        geo = side[0].geo[side[2]]
        harm = harmonic_rows(geo[0:1], geo[1:2], geo[2:3])
        parts = [gathered[m * chans : (m + 1) * chans] for m in range(9)]
        bands = [parts[0], None, None]
        for m in range(1, 9):
            term = parts[m] * harm[m]
            band = BANDS[m]
            bands[band] = term if bands[band] is None else bands[band] + term
        return jnp.concatenate([band.astype(bf16) for band in bands], axis=0)

    def hidden(side, invariant):
        return dot(w_lat_t_ref[...], side[0].latent[side[2]]) + dot(w_ten_t_ref[...], invariant)

    def readout(side, pre):
        own_s, _, at = side
        geo = own_s.geo[at]
        up = 1.0 + jnp.tanh(pre)
        value = pre * up
        weight = jnp.concatenate([w_out_ref[...]] * (eb // LANES), axis=1)
        own_s.geo[at, 8:9, :] = jnp.sum(value * weight, axis=0, keepdims=True)
        scale = 0.5 * geo[5:6] * geo[7:8]
        return ((up + value * (2.0 - up)) * (weight * scale)).astype(bf16)

    def unfold(side, back, gathered):
        own_s, _, at = side
        geo = own_s.geo[at]
        harm = harmonic_rows(geo[0:1], geo[1:2], geo[2:3])
        own_s.dlat[at] = back[0:features].astype(bf16)
        dbands = [
            back[features + band * chans : features + (band + 1) * chans] for band in range(3)
        ]
        for m in range(1, 9):
            part = gathered[m * chans : (m + 1) * chans]
            own_s.dharm[at, (m - 1) * 8 : m * 8, :] = fold8(dbands[BANDS[m]] * part)
        return jnp.concatenate(
            [
                (dbands[BANDS[m]] if harm[m] is None else dbands[BANDS[m]] * harm[m]).astype(bf16)
                for m in range(9)
            ],
            axis=0,
        )

    def second_pass(sides):
        gathered = [gather_tensor(side) for side in sides]
        pre = [hidden(side, invariants(side, g)) for side, g in zip(sides, gathered)]
        back = [dot(w_back_ref[...], readout(side, values)) for side, values in zip(sides, pre)]
        for side, values, g in zip(sides, back, gathered):
            add_tensor(side, unfold(side, values, g), side[0].center_hot[side[2]])

    each_block(second_pass)
    tensor_b[...] = (0.125 * (even.tensor[...] + odd.tensor[...])).astype(bf16)

    def channels_back(side, gathered):
        own_s, _, at = side
        geo = own_s.geo[at]
        harm = harmonic_rows(geo[0:1], geo[1:2], geo[2:3])
        chan = own_s.chan[at]
        dchan = gathered[0:chans]
        dh = [None]
        for m in range(1, 9):
            part = gathered[m * chans : (m + 1) * chans]
            dchan = dchan + part * harm[m]
            total = own_s.dharm[at, (m - 1) * 8 : m * 8, :] + fold8(part * chan)
            dh.append(jnp.sum(total, axis=0, keepdims=True))
        return (dchan * geo[7:8]).astype(bf16), dh

    def radial_back(side, dchan):
        own_s, _, at = side
        dlat = own_s.dlat[at] + dot(w_chan_ref[...], dchan).astype(bf16)
        drad = dot(w_rbf_ref[...], dlat * own_s.slope[at])
        return drad[0:8] + drad[8:16]

    def finish(side, drad, dh):
        own_s, b, at = side
        geo = own_s.geo[at]
        x, y, z = geo[0:1], geo[1:2], geo[2:3]
        inv_d, dist, env, squared = geo[3:4], geo[4:5], geo[5:6], geo[6:7]
        live, summed = geo[7:8], geo[8:9]
        mu = 0.5 + 0.4 * rows_of((8, eb)).astype(f32)
        u = (dist - mu) * 2.0
        weighted = drad * jnp.exp(-(u * u))
        denv = jnp.sum(weighted, axis=0, keepdims=True) + live * summed
        ddist = -4.0 * env * jnp.sum(weighted * u, axis=0, keepdims=True)
        dx = dh[1] + ROOT3 * (y * dh[4] + z * dh[6] + x * dh[7])
        dy = dh[2] + ROOT3 * (x * dh[4] + z * dh[5] - y * dh[7])
        dz = dh[3] + ROOT3 * (y * dh[5] + x * dh[6]) + 3.0 * z * dh[8]
        ddist = ddist - (dx * x + dy * y + dz * z) * inv_d
        dsq = denv * (env * env * squared * -0.125) + ddist * (0.5 * inv_d)
        both = 2.0 * dsq * dist
        gs = [dx * inv_d + both * x, dy * inv_d + both * y, dz * inv_d + both * z]
        energy = summed * env * live

        o_high = lax.shift_right_logical(others_ref[b], 7)
        mask_o = one_hot(o_high, hpad)
        split = [halves(g) for g in gs]
        rows_o = jnp.concatenate(
            [mask_o * split[d][part] for part in range(2) for d in range(3)], axis=0
        ).astype(bf16)
        split.append(halves(energy))
        rows_c = jnp.concatenate(
            [split[d][part] for part in range(2) for d in range(4)]
            + [jnp.zeros((8, eb), f32)],
            axis=0,
        ).astype(bf16)
        own_s.acc_o[...] += dot_t(rows_o, own_s.low_o[at])
        own_s.acc_c[half_of(b)] += dot_t(rows_c, own_s.center_hot[at])

    def third_pass(sides):
        gathered = [gather_tensor(side) for side in sides]
        back = []
        for side, g in zip(sides, gathered):
            dchan, dh = channels_back(side, g)
            back.append((radial_back(side, dchan), dh))
        for side, (drad, dh) in zip(sides, back):
            finish(side, drad, dh)

    each_block(third_pass)
    sum_o = even.acc_o[...] + odd.acc_o[...]
    sum_o = sum_o[0 : 3 * hpad] + sum_o[3 * hpad :]
    for d in range(3):
        grad_ref[d] = sum_o[d * hpad : (d + 1) * hpad]
        slab_grad_ref[d : d + 1, :] = sum_o[d * hpad + highs - 1 : d * hpad + highs]
    for half in range(halves_n):
        sum_c = even.acc_c[half] + odd.acc_c[half]
        sum_c = sum_c[0:4] + sum_c[4:8]
        for part in range(span // LANES):
            high = half * (span // LANES) + part
            lanes = slice(part * LANES, (part + 1) * LANES)
            for d in range(3):
                grad_ref[d, high : high + 1, :] = (
                    sum_o[d * hpad + high : d * hpad + high + 1] - sum_c[d : d + 1, lanes]
                )
            energy_ref[:, high * LANES : (high + 1) * LANES] = sum_c[3:4, lanes]


def return_kernel(grad_ref, back_ref, picks_ref, own_ref, to_xm_ref, to_xp_ref, to_ym_ref, to_yp_ref):
    hpad = grad_ref.shape[1]
    z_rows = picks_ref[8:9, :]
    mask = one_hot(lax.shift_right_logical(z_rows, 7), hpad)
    low = one_hot(lax.bitwise_and(z_rows, LANES - 1), LANES).astype(bf16)
    pieces = [halves(back_ref[d : d + 1, :]) for d in range(3)]
    rows = jnp.concatenate(
        [mask * pieces[d][part] for part in range(2) for d in range(3)], axis=0
    ).astype(bf16)
    landed = dot_t(rows, low)
    landed = landed[0 : 3 * hpad] + landed[3 * hpad :]
    base = own_ref.shape[1] // 2
    for d in range(3):
        total = grad_ref[d] + landed[d * hpad : (d + 1) * hpad]
        own_ref[d] = total[0:8]
        for cycle, (p, q) in enumerate(cycle_cells):
            value = total[base + cycle : base + cycle + 1]
            if p in (0, 4):
                ref = to_xm_ref if p == 0 else to_xp_ref
                ref[q * 3 + d : q * 3 + d + 1, :] = value
            else:
                ref = to_ym_ref if q == 0 else to_yp_ref
                ref[(p - 1) * 3 + d : (p - 1) * 3 + d + 1, :] = value


def turn_kernel(from_xp_ref, from_xm_ref, to_ym_ref, to_yp_ref, send_ym_ref, send_yp_ref):
    for q, old, new in ((0, to_ym_ref, send_ym_ref), (4, to_yp_ref, send_yp_ref)):
        new[0:3, :] = old[0:3, :] + from_xm_ref[q * 3 : q * 3 + 3, :]
        new[3:6, :] = old[3:6, :]
        new[6:9, :] = old[6:9, :] + from_xp_ref[q * 3 : q * 3 + 3, :]


def force_kernel(
    own_ref, picks_ref, from_xp_ref, from_xm_ref, from_yp_ref, from_ym_ref, out_ref, rim_sum
):
    rim_sum[...] = jnp.zeros_like(rim_sum)
    for a, ref in ((2, from_xp_ref), (0, from_xm_ref)):
        for b in range(3):
            rim_sum[rim_cells.index((a, b)), 0:3, :] += ref[(b + 1) * 3 : (b + 2) * 3, :]
    for b, ref in ((2, from_yp_ref), (0, from_ym_ref)):
        for a in range(3):
            rim_sum[rim_cells.index((a, b)), 0:3, :] += ref[a * 3 : (a + 1) * 3, :]
    total = jnp.zeros((48, LANES), f32)
    for rim in range(8):
        index = picks_ref[rim : rim + 1, :]
        mask = one_hot(lax.shift_right_logical(index, 7), 8)
        low = one_hot(lax.bitwise_and(index, LANES - 1), LANES).astype(bf16)
        values = rim_sum[rim]
        pieces = [halves(values[d : d + 1, :]) for d in range(3)]
        rows = jnp.concatenate(
            [mask * pieces[d][part] for part in range(2) for d in range(3)], axis=0
        ).astype(bf16)
        total = total + dot_t(rows, low)
    total = total[0:24] + total[24:48]
    for d in range(3):
        for high in range(out_ref.shape[2] // LANES):
            value = own_ref[d, high : high + 1, :] + total[d * 8 + high : d * 8 + high + 1, :]
            out_ref[d, :, high * LANES : (high + 1) * LANES] = -value


def call(kernel, out_shape, args, scratch=(), smem=0, limit=12 * 1024 * 1024):
    vmem = pl.BlockSpec(memory_space=pltpu.VMEM)
    scalar = pl.BlockSpec(memory_space=pltpu.SMEM)
    return pl.pallas_call(
        kernel,
        out_shape=out_shape,
        in_specs=[scalar] * smem + [vmem] * (len(args) - smem),
        out_specs=jax.tree.map(lambda _: vmem, out_shape),
        scratch_shapes=list(scratch),
        compiler_params=pltpu.CompilerParams(vmem_limit_bytes=limit),
    )(*args)


def shifted(x, axis, step):
    count = lax.axis_size(axis)
    return lax.ppermute(x, axis, [((i + step) % count, i) for i in range(count)])


def swapped(x):
    count = lax.axis_size("gz")
    return lax.ppermute(x, "gz", [(i, i ^ 1) for i in range(count)])


def per_device(
    positions,
    attributes,
    edge_center,
    edge_other,
    edge_count,
    rim_rows,
    z_rows,
    w_emb,
    w_rbf,
    w_chan,
    w_lat,
    w_ten,
    w_out,
):
    pos = positions.reshape(3, 1, -1)
    attr = attributes[0, 0, 0]
    rim = rim_rows[0, 0, 0]
    zr = z_rows[0, 0]
    count = edge_count[0, 0]
    atoms, width = attr.shape
    edges = edge_center.shape[-1]
    features = w_emb.shape[1]
    chans = w_chan.shape[1]
    height = width + PARTS
    inner_len = atoms + 16 * LANES
    table = inner_len + LANES
    hpad = -(-(table // LANES) // 8) * 8
    eb = BLOCK
    span = 2 * LANES
    pairs = -(-(edges // eb + atoms // span - 1) // 2)
    slot_rows = -(-(2 * pairs * eb // LANES) // 8) * 8
    lift = (1 - 2 * lax.axis_index("gz")).astype(f32).reshape(1)
    big = 42 * 1024 * 1024

    shape = jax.ShapeDtypeStruct
    prepared = call(
        weights_kernel,
        (
            shape((features, width), bf16),
            shape((features, LANES), bf16),
            shape((features, chans), bf16),
            shape((chans, features), bf16),
            shape((features, features), bf16),
            shape((features, 3 * chans), bf16),
            shape((features + 3 * chans, features), bf16),
            shape((features, LANES), f32),
            shape((16, features), bf16),
        ),
        (
            jnp.concatenate([w_emb, w_lat, w_ten, w_chan.T], axis=0),
            jnp.concatenate([w_rbf, w_out[None]], axis=0),
        ),
        [pltpu.VMEM((LANES, features), f32)],
    )
    picks = jnp.concatenate([rim, zr], axis=0)
    own, *sent = call(
        pack_kernel,
        (shape((height, atoms), bf16),) + (shape((height, 3 * LANES), bf16),) * 4,
        (pos, attr, picks),
        [pltpu.VMEM((PARTS, atoms), f32)],
    )
    got = [
        shifted(x, "gx" if way[0] else "gy", way[0] + way[1]) for x, way in zip(sent, sides)
    ]
    lines = edges // LANES
    groups = -(-table // 256)
    ends = jnp.concatenate(
        [edge_center.reshape(lines, LANES), edge_other.reshape(lines, LANES)], axis=0
    )
    bucketed = call(
        bucket_kernel,
        (
            shape((slot_rows, LANES), jnp.int32),
            shape((slot_rows, LANES), jnp.int32),
            shape((4, LANES), jnp.int32),
        ),
        (count, ends),
        [
            pltpu.VMEM((2 * groups * lines, LANES), bf16),
            pltpu.VMEM((4 * slot_rows, edges), bf16),
            pltpu.VMEM((LANES, edges), bf16),
        ],
        smem=1,
        limit=24 * 1024 * 1024,
    )
    first, bucketed = lax.optimization_barrier((got[:2], bucketed))
    got = [*first, *got[2:]]
    centers, others, meta = bucketed
    centers = centers.reshape(-1, 1, eb)
    others = others.reshape(-1, 1, eb)
    to_plus, to_minus = call(
        corner_kernel,
        (shape((height, 2 * LANES), bf16),) * 2,
        (got[0], got[1]),
    )
    corners = [shifted(to_plus, "gx", -1), shifted(to_minus, "gx", 1)]
    corners, prepared = lax.optimization_barrier((corners, prepared))
    w_emb_t, w_rad, w_chan_r, w_chan_t, w_lat_t, w_ten_t, w_back, w_out_col, w_rbf2 = prepared
    inner, slab_send = call(
        slab_kernel,
        (shape((height, inner_len), bf16), shape((height, LANES), bf16)),
        (own, picks, *got, *corners),
        [pltpu.VMEM((PARTS, inner_len), f32)],
    )
    slab_got = swapped(slab_send)
    feat, place = call(
        embed_kernel,
        (shape((features, inner_len), bf16), shape((6, hpad, LANES), f32)),
        (inner, w_emb_t),
    )
    grads, slab_grad, energy = call(
        edge_kernel,
        (shape((3, hpad, LANES), f32), shape((3, LANES), f32), shape((1, atoms), f32)),
        (
            meta,
            lift,
            centers,
            others,
            feat,
            place,
            slab_got,
            w_emb_t,
            w_rad,
            w_chan_t,
            w_chan_r,
            w_lat_t,
            w_ten_t,
            w_back,
            w_out_col,
            w_rbf2,
        ),
        [
            pltpu.VMEM((features, (groups - 1) * 256 + WINDOW), bf16),
            pltpu.VMEM((atoms // span, features, span + LANES), bf16),
            pltpu.VMEM((6, hpad, LANES), f32),
            pltpu.VMEM((6 * hpad, LANES), bf16),
            pltpu.VMEM((48, LANES), bf16),
            pltpu.VMEM((atoms // span, 9 * chans, span), bf16),
        ]
        + [
            pltpu.VMEM((WINDOW + span + LANES, eb), bf16),
            pltpu.VMEM((features, eb), f32),
            pltpu.VMEM((pairs, span, eb), bf16),
            pltpu.VMEM((pairs, LANES, eb), bf16),
            pltpu.VMEM((pairs, features, eb), bf16),
            pltpu.VMEM((pairs, features, eb), bf16),
            pltpu.VMEM((pairs, chans, eb), f32),
            pltpu.VMEM((pairs, 16, eb), f32),
            pltpu.VMEM((pairs, features, eb), bf16),
            pltpu.VMEM((pairs, 64, eb), f32),
            pltpu.VMEM((atoms // span, 9 * chans, span), f32),
            pltpu.VMEM((6 * hpad, LANES), f32),
            pltpu.VMEM((atoms // span, 16, span), f32),
        ]
        * 2,
        smem=2,
        limit=big,
    )
    slab_back = swapped(slab_grad)
    along_x, along_y = shape((15, LANES), f32), shape((9, LANES), f32)
    own_grad, to_xm, to_xp, to_ym, to_yp = call(
        return_kernel,
        (shape((3, 8, LANES), f32), along_x, along_x, along_y, along_y),
        (grads, slab_back, picks),
    )
    from_xp, from_xm = shifted(to_xm, "gx", 1), shifted(to_xp, "gx", -1)
    to_ym, to_yp = call(turn_kernel, (along_y, along_y), (from_xp, from_xm, to_ym, to_yp))
    from_yp, from_ym = shifted(to_ym, "gy", 1), shifted(to_yp, "gy", -1)
    forces = call(
        force_kernel,
        shape((3, 1, atoms), f32),
        (own_grad, picks, from_xp, from_xm, from_yp, from_ym),
        [pltpu.VMEM((8, 8, LANES), f32)],
    )
    return (energy.reshape(1, 1, 1, atoms), forces.reshape(1, 1, 1, 3, atoms))


def solution(mesh):
    return jax.shard_map(
        per_device,
        mesh=mesh,
        in_specs=(
            P("gx", "gy", "gz", None, None),
            P("gx", "gy", "gz", None, None),
            P("gx", "gy", "gz", None),
            P("gx", "gy", "gz", None),
            P("gx", "gy", "gz"),
            P("gx", "gy", "gz", None, None),
            P("gx", "gy", "gz", None),
            P(),
            P(),
            P(),
            P(),
            P(),
            P(),
        ),
        out_specs=(P("gx", "gy", "gz", None), P("gx", "gy", "gz", None, None)),
        check_vma=False,
    )
```

profile of v0, /device:TPU:0, one launch (start us, length us, event | category | flops | bytes accessed | tf_op | source)
XLA Modules:
  0.0 72.8 jit_solution(18209919857826983914)
XLA Ops:
  0.6 0.7 pad_add_fusion.1.picks_ref
  1.3 0.9 %copy-done = bf16[1,1,1,512,128]{4,3,2,1,0:T(8,128)(2,1)S(1)} copy-done((bf16[1,1,1,512,128]{4,3,2,1,0:T(8,128)(2,1)S(1)}, bf16[1,1,1,512,128]{4,3,2,1,0:T(8,128)(2,1)}, u32[]{:S(2)}) %copy-start) | copy-done | bytes 131096
  2.2 0.7 copy-done.1
  3.5 3.1 %collective-permute-start = (bf16[144,384]{1,0:T(8,128)(2,1)S(1)}, bf16[144,384]{1,0:T(8,128)(2,1)S(1)}, u32[]{:S(2)}, u32[]{:S(2)}) collective-permute-start(bf16[144,384]{1,0:T(8,128)(2,1)S(1)} %get-tuple-element.51), channel_id=1, source_target_pairs={{6,0},{0,2},{2,4},{4,6},{7,1},{1,3},{3,5},{5,7},{14,8},{8,10},{10,... | collective-permute-start | bytes 331784 | tf_op jit(solution)/shard_map/ppermute | solution.py:720
  6.6 2.1 %collective-permute-start.1 = (bf16[144,384]{1,0:T(8,128)(2,1)S(1)}, bf16[144,384]{1,0:T(8,128)(2,1)S(1)}, u32[]{:S(2)}, u32[]{:S(2)}) collective-permute-start(bf16[144,384]{1,0:T(8,128)(2,1)S(1)} %get-tuple-element.52), channel_id=1, source_target_pairs={{2,0},{4,2},{6,4},{0,6},{3,1},{5,3},{7,5},{1,7},{10,8},{12,10},{14... | collective-permute-start | bytes 331784 | tf_op jit(solution)/shard_map/ppermute | solution.py:720
  8.7 1.7 %collective-permute-start.3 = (bf16[144,384]{1,0:T(8,128)(2,1)S(1)}, bf16[144,384]{1,0:T(8,128)(2,1)S(1)}, u32[]{:S(2)}, u32[]{:S(2)}) collective-permute-start(bf16[144,384]{1,0:T(8,128)(2,1)S(1)} %get-tuple-element.63), channel_id=1, source_target_pairs={{8,0},{16,8},{24,16},{0,24},{9,1},{17,9},{25,17},{1,25},{10,2},{18... | collective-permute-start | bytes 331784 | tf_op jit(solution)/shard_map/ppermute | solution.py:720
  11.1 0.8 %pad_add_fusion.ends_ref = s32[96,128]{1,0:T(8,128)S(1)} fusion(s32[48,128]{1,0:T(8,128)} %bitcast.22, s32[48,128]{1,0:T(8,128)} %bitcast.23), kind=kLoop, calls=%fused_computation.1 | loop fusion | flops 12288 | bytes 98304 | tf_op jit(solution)/shard_map/concatenate | solution.py:795
  11.9 2.5 %shard_map.141 = (s32[56,128]{1,0:T(8,128)S(1)}, s32[56,128]{1,0:T(8,128)S(1)}, s32[4,128]{1,0:T(4,128)S(1)}) custom-call(s32[1]{0:T(128)} %bitcast.16.count_ref, s32[96,128]{1,0:T(8,128)S(1)} %pad_add_fusion.ends_ref), custom_call_target="tpu_custom_call" | custom-call | tf_op jit(solution)/shard_map/pallas_call | solution.py:708
  14.3 1.0 %pad_maximum_fusion.stacked_ref = bf16[640,256]{1,0:T(8,128)(2,1)S(1)} fusion(bf16[64,256]{1,0:T(8,128)(2,1)} %bitcast.21, bf16[192,256]{1,0:T(8,128)(2,1)} %param.24, bf16[256,256]{1,0:T(8,128)(2,1)} %param.23, bf16[128,256]{1,0:T(8,128)(2,1)} %param.20), kind=kLoop, calls=%fused_computation | loop fusion | flops 1310720 | bytes 655360 | tf_op jit(solution)/shard_map/concatenate | solution.py:778
  15.5 1.7 %collective-permute-start.5 = (bf16[144,256]{1,0:T(8,128)(2,1)S(1)}, bf16[144,256]{1,0:T(8,128)(2,1)S(1)}, u32[]{:S(2)}, u32[]{:S(2)}) collective-permute-start(bf16[144,256]{1,0:T(8,128)(2,1)S(1)} %get-tuple-element.65), channel_id=1, source_target_pairs={{8,0},{16,8},{24,16},{0,24},{9,1},{17,9},{25,17},{1,25},{10,2},{18... | collective-permute-start | bytes 221192 | tf_op jit(solution)/shard_map/ppermute | solution.py:720
  17.2 0.7 pad_maximum_fusion.1.small_ref
  18.2 1.0 %collective-permute-done.4.rest_4_ = bf16[144,256]{1,0:T(8,128)(2,1)S(1)} collective-permute-done((bf16[144,256]{1,0:T(8,128)(2,1)S(1)}, bf16[144,256]{1,0:T(8,128)(2,1)S(1)}, u32[]{:S(2)}, u32[]{:S(2)}) %collective-permute-start.4) | collective-permute-done | bytes 73760 | tf_op jit(solution)/shard_map/ppermute | solution.py:720
  19.6 1.7 %collective-permute-start.6 = (bf16[144,128]{1,0:T(8,128)(2,1)S(1)}, bf16[144,128]{1,0:T(8,128)(2,1)S(1)}, u32[]{:S(2)}, u32[]{:S(2)}) collective-permute-start(bf16[144,128]{1,0:T(8,128)(2,1)S(1)} %get-tuple-element.81), channel_id=1, source_target_pairs={{0,1},{1,0},{2,3},{3,2},{4,5},{5,4},{6,7},{7,6},{8,9},{9,8},{10,11... | collective-permute-start | bytes 110600 | tf_op jit(solution)/shard_map/ppermute | solution.py:725
  21.3 0.7 %shard_map.145 = (bf16[256,2560]{1,0:T(8,128)(2,1)S(1)}, f32[6,24,128]{2,1,0:T(8,128)S(1)}) custom-call(bf16[144,2560]{1,0:T(8,128)(2,1)S(1)} %get-tuple-element.77.inner_ref, bf16[256,128]{1,0:T(8,128)(2,1)S(1)} %get-tuple-element.78.w_emb_ref), custom_call_target="tpu_custom_call" | custom-call | tf_op jit(solution)/shard_map/pallas_call | solution.py:708
  22.1 1.6 %collective-permute-done.6.slab_ref = bf16[144,128]{1,0:T(8,128)(2,1)S(1)} collective-permute-done((bf16[144,128]{1,0:T(8,128)(2,1)S(1)}, bf16[144,128]{1,0:T(8,128)(2,1)S(1)}, u32[]{:S(2)}, u32[]{:S(2)}) %collective-permute-start.6) | collective-permute-done | bytes 36896 | tf_op jit(solution)/shard_map/ppermute | solution.py:725
  23.7 24.5 %shard_map.146 = (f32[3,24,128]{2,1,0:T(8,128)S(1)}, f32[3,128]{1,0:T(4,128)S(1)}, f32[1,512]{1,0:T(1,128)}) custom-call(s32[4,128]{1,0:T(4,128)S(1)} %get-tuple-element.56.meta_ref, f32[1]{0:T(128)} %bitcast.7.lift_ref, s32[14,1,512]{2,1,0:T(1,128)S(1)} %bitcast.18, s32[14,1,512]{2,1,0:T(1,128)S(1)} %bitcast.19, ...), custom_call_target="tpu_custom_call" | custom-call | tf_op jit(solution)/shard_map/pallas_call | solution.py:708
  48.1 2.1 %collective-permute-start.7 = (f32[3,128]{1,0:T(4,128)S(1)}, f32[3,128]{1,0:T(4,128)S(1)}, u32[]{:S(2)}, u32[]{:S(2)}) collective-permute-start(f32[3,128]{1,0:T(4,128)S(1)} %get-tuple-element.92), channel_id=1, source_target_pairs={{0,1},{1,0},{2,3},{3,2},{4,5},{5,4},{6,7},{7,6},{8,9},{9,8},{10,11... | collective-permute-start | bytes 4616 | tf_op jit(solution)/shard_map/ppermute | solution.py:725
  50.2 1.6 %collective-permute-done.7.back_ref = f32[3,128]{1,0:T(4,128)S(1)} collective-permute-done((f32[3,128]{1,0:T(4,128)S(1)}, f32[3,128]{1,0:T(4,128)S(1)}, u32[]{:S(2)}, u32[]{:S(2)}) %collective-permute-start.7) | collective-permute-done | bytes 1568 | tf_op jit(solution)/shard_map/ppermute | solution.py:725
  52.0 7.9 %collective-permute-start.9 = (f32[15,128]{1,0:T(8,128)S(1)}, f32[15,128]{1,0:T(8,128)S(1)}, u32[]{:S(2)}, u32[]{:S(2)}) collective-permute-start(f32[15,128]{1,0:T(8,128)S(1)} %get-tuple-element.95), channel_id=1, source_target_pairs={{24,0},{0,8},{8,16},{16,24},{25,1},{1,9},{9,17},{17,25},{26,2},{2,... | collective-permute-start | bytes 23048 | tf_op jit(solution)/shard_map/ppermute | solution.py:720
  59.9 0.6 collective-permute-done.8.from_xp_ref
  60.8 5.7 %collective-permute-start.10 = (f32[9,128]{1,0:T(8,128)S(1)}, f32[9,128]{1,0:T(8,128)S(1)}, u32[]{:S(2)}, u32[]{:S(2)}) collective-permute-start(f32[9,128]{1,0:T(8,128)S(1)} %get-tuple-element.98), channel_id=1, source_target_pairs={{2,0},{4,2},{6,4},{0,6},{3,1},{5,3},{7,5},{1,7},{10,8},{12,10},{14... | collective-permute-start | bytes 13832 | tf_op jit(solution)/shard_map/ppermute | solution.py:720
  66.5 1.4 %collective-permute-done.10.from_yp_ref = f32[9,128]{1,0:T(8,128)S(1)} collective-permute-done((f32[9,128]{1,0:T(8,128)S(1)}, f32[9,128]{1,0:T(8,128)S(1)}, u32[]{:S(2)}, u32[]{:S(2)}) %collective-permute-start.10) | collective-permute-done | bytes 4640 | tf_op jit(solution)/shard_map/ppermute | solution.py:720
  67.9 4.1 %collective-permute-done.11.from_ym_ref = f32[9,128]{1,0:T(8,128)S(1)} collective-permute-done((f32[9,128]{1,0:T(8,128)S(1)}, f32[9,128]{1,0:T(8,128)S(1)}, u32[]{:S(2)}, u32[]{:S(2)}) %collective-permute-start.11) | collective-permute-done | bytes 4640 | tf_op jit(solution)/shard_map/ppermute | solution.py:720
  71.9 0.9 %shard_map.149 = f32[3,1,512]{2,1,0:T(1,128)} custom-call(f32[3,8,128]{2,1,0:T(8,128)S(1)} %get-tuple-element.93.own_ref, s32[9,128]{1,0:T(8,128)S(1)} %pad_add_fusion.1.picks_ref, f32[15,128]{1,0:T(8,128)S(1)} %collective-permute-done.8.from_xp_ref, f32[15,128]{1,0:T(8,128)S(1)} %collective-permute-done.9.from_xm_ref, ...), custom_call_target="tpu_custom_call" | custom-call | tf_op jit(solution)/shard_map/pallas_call | solution.py:708
  (18 shorter events, 1.9 us)
Async XLA Ops:
  1.3 0.9 %copy-start = (bf16[1,1,1,512,128]{4,3,2,1,0:T(8,128)(2,1)S(1)}, bf16[1,1,1,512,128]{4,3,2,1,0:T(8,128)(2,1)}, u32[]{:S(2)}) copy-start(bf16[1,1,1,512,128]{4,3,2,1,0:T(8,128)(2,1)} %param.14) | copy-start | bytes 393220
  2.2 0.7 copy-start.1
  3.5 11.8 %collective-permute-start = (bf16[144,384]{1,0:T(8,128)(2,1)S(1)}, bf16[144,384]{1,0:T(8,128)(2,1)S(1)}, u32[]{:S(2)}, u32[]{:S(2)}) collective-permute-start(bf16[144,384]{1,0:T(8,128)(2,1)S(1)} %get-tuple-element.51), channel_id=1, source_target_pairs={{6,0},{0,2},{2,4},{4,6},{7,1},{1,3},{3,5},{5,7},{14,8},{8,10},{10,... | collective-permute-start | bytes 331784 | tf_op jit(solution)/shard_map/ppermute | solution.py:720
  6.6 8.7 %collective-permute-start.1 = (bf16[144,384]{1,0:T(8,128)(2,1)S(1)}, bf16[144,384]{1,0:T(8,128)(2,1)S(1)}, u32[]{:S(2)}, u32[]{:S(2)}) collective-permute-start(bf16[144,384]{1,0:T(8,128)(2,1)S(1)} %get-tuple-element.52), channel_id=1, source_target_pairs={{2,0},{4,2},{6,4},{0,6},{3,1},{5,3},{7,5},{1,7},{10,8},{12,10},{14... | collective-permute-start | bytes 331784 | tf_op jit(solution)/shard_map/ppermute | solution.py:720
  8.7 10.5 %collective-permute-start.2 = (bf16[144,384]{1,0:T(8,128)(2,1)S(1)}, bf16[144,384]{1,0:T(8,128)(2,1)S(1)}, u32[]{:S(2)}, u32[]{:S(2)}) collective-permute-start(bf16[144,384]{1,0:T(8,128)(2,1)S(1)} %get-tuple-element.62), channel_id=1, source_target_pairs={{24,0},{0,8},{8,16},{16,24},{25,1},{1,9},{9,17},{17,25},{26,2},{2,... | collective-permute-start | bytes 331784 | tf_op jit(solution)/shard_map/ppermute | solution.py:720
  8.7 10.5 %collective-permute-start.3 = (bf16[144,384]{1,0:T(8,128)(2,1)S(1)}, bf16[144,384]{1,0:T(8,128)(2,1)S(1)}, u32[]{:S(2)}, u32[]{:S(2)}) collective-permute-start(bf16[144,384]{1,0:T(8,128)(2,1)S(1)} %get-tuple-element.63), channel_id=1, source_target_pairs={{8,0},{16,8},{24,16},{0,24},{9,1},{17,9},{25,17},{1,25},{10,2},{18... | collective-permute-start | bytes 331784 | tf_op jit(solution)/shard_map/ppermute | solution.py:720
  15.4 3.8 %collective-permute-start.4 = (bf16[144,256]{1,0:T(8,128)(2,1)S(1)}, bf16[144,256]{1,0:T(8,128)(2,1)S(1)}, u32[]{:S(2)}, u32[]{:S(2)}) collective-permute-start(bf16[144,256]{1,0:T(8,128)(2,1)S(1)} %get-tuple-element.64), channel_id=1, source_target_pairs={{24,0},{0,8},{8,16},{16,24},{25,1},{1,9},{9,17},{17,25},{26,2},{2,... | collective-permute-start | bytes 221192 | tf_op jit(solution)/shard_map/ppermute | solution.py:720
  15.5 3.7 %collective-permute-start.5 = (bf16[144,256]{1,0:T(8,128)(2,1)S(1)}, bf16[144,256]{1,0:T(8,128)(2,1)S(1)}, u32[]{:S(2)}, u32[]{:S(2)}) collective-permute-start(bf16[144,256]{1,0:T(8,128)(2,1)S(1)} %get-tuple-element.65), channel_id=1, source_target_pairs={{8,0},{16,8},{24,16},{0,24},{9,1},{17,9},{25,17},{1,25},{10,2},{18... | collective-permute-start | bytes 221192 | tf_op jit(solution)/shard_map/ppermute | solution.py:720
  19.6 4.0 %collective-permute-start.6 = (bf16[144,128]{1,0:T(8,128)(2,1)S(1)}, bf16[144,128]{1,0:T(8,128)(2,1)S(1)}, u32[]{:S(2)}, u32[]{:S(2)}) collective-permute-start(bf16[144,128]{1,0:T(8,128)(2,1)S(1)} %get-tuple-element.81), channel_id=1, source_target_pairs={{0,1},{1,0},{2,3},{3,2},{4,5},{5,4},{6,7},{7,6},{8,9},{9,8},{10,11... | collective-permute-start | bytes 110600 | tf_op jit(solution)/shard_map/ppermute | solution.py:725
  48.1 3.7 %collective-permute-start.7 = (f32[3,128]{1,0:T(4,128)S(1)}, f32[3,128]{1,0:T(4,128)S(1)}, u32[]{:S(2)}, u32[]{:S(2)}) collective-permute-start(f32[3,128]{1,0:T(4,128)S(1)} %get-tuple-element.92), channel_id=1, source_target_pairs={{0,1},{1,0},{2,3},{3,2},{4,5},{5,4},{6,7},{7,6},{8,9},{9,8},{10,11... | collective-permute-start | bytes 4616 | tf_op jit(solution)/shard_map/ppermute | solution.py:725
  52.0 8.6 %collective-permute-start.8 = (f32[15,128]{1,0:T(8,128)S(1)}, f32[15,128]{1,0:T(8,128)S(1)}, u32[]{:S(2)}, u32[]{:S(2)}) collective-permute-start(f32[15,128]{1,0:T(8,128)S(1)} %get-tuple-element.94), channel_id=1, source_target_pairs={{8,0},{16,8},{24,16},{0,24},{9,1},{17,9},{25,17},{1,25},{10,2},{18... | collective-permute-start | bytes 23048 | tf_op jit(solution)/shard_map/ppermute | solution.py:720
  52.0 8.7 %collective-permute-start.9 = (f32[15,128]{1,0:T(8,128)S(1)}, f32[15,128]{1,0:T(8,128)S(1)}, u32[]{:S(2)}, u32[]{:S(2)}) collective-permute-start(f32[15,128]{1,0:T(8,128)S(1)} %get-tuple-element.95), channel_id=1, source_target_pairs={{24,0},{0,8},{8,16},{16,24},{25,1},{1,9},{9,17},{17,25},{26,2},{2,... | collective-permute-start | bytes 23048 | tf_op jit(solution)/shard_map/ppermute | solution.py:720
  60.8 7.1 %collective-permute-start.10 = (f32[9,128]{1,0:T(8,128)S(1)}, f32[9,128]{1,0:T(8,128)S(1)}, u32[]{:S(2)}, u32[]{:S(2)}) collective-permute-start(f32[9,128]{1,0:T(8,128)S(1)} %get-tuple-element.98), channel_id=1, source_target_pairs={{2,0},{4,2},{6,4},{0,6},{3,1},{5,3},{7,5},{1,7},{10,8},{12,10},{14... | collective-permute-start | bytes 13832 | tf_op jit(solution)/shard_map/ppermute | solution.py:720
  66.5 5.4 %collective-permute-start.11 = (f32[9,128]{1,0:T(8,128)S(1)}, f32[9,128]{1,0:T(8,128)S(1)}, u32[]{:S(2)}, u32[]{:S(2)}) collective-permute-start(f32[9,128]{1,0:T(8,128)S(1)} %get-tuple-element.99), channel_id=1, source_target_pairs={{6,0},{0,2},{2,4},{4,6},{7,1},{1,3},{3,5},{5,7},{14,8},{8,10},{10,... | collective-permute-start | bytes 13832 | tf_op jit(solution)/shard_map/ppermute | solution.py:720
where the time goes:
time: 74.2 us; the launch traced here: 72.8 us
  Pallas kernels  30.1 us (41%)
  starting transfers between devices  26.2 us (35%)
  waiting for transfers between devices  10.4 us (14%)
  other arithmetic  3.19 us (4%)
  local copies, waits for them, and re-layouts  1.59 us (2%)
  between operations  1.37 us (2%)
    pallas_call x10, Pallas kernels, call(): pl.pallas_call(kernel, out_shape=out_shape, in_specs=[scalar] * smem + [v...  30.1 us
    ppermute x10, starting transfers between devices, shifted(): lax.ppermute(x, axis, [((i + step) % count, i) for i in range(count)])  22.4 us
    ppermute x10, waiting for transfers between devices, shifted(): lax.ppermute(x, axis, [((i + step) % count, i) for i in range(count)])  7.27 us
    ppermute x2, starting transfers between devices, swapped(): return lax.ppermute(x, 'gz', [(i, i ^ 1) for i in range(count)])  3.8 us
    ppermute x2, waiting for transfers between devices, swapped(): return lax.ppermute(x, 'gz', [(i, i ^ 1) for i in range(count)])  3.12 us
    unnamed x4, local copies, waits for them, and re-layouts  1.59 us
  transfers between devices with their start and end apart: 12, of which 7 were waited for; matrix products, arithmetic and copies ran while one was open for 3% of the time, Pallas kernels for 5%

commit v1 on v0

--- a/solution.py
+++ b/solution.py
@@ -139,8 +139,7 @@
     emb_t_ref,
     rad_ref,
     chan_ref,
-    w_chan_t_ref,
-    lat_t_ref,
+    forward_ref,
     ten_t_ref,
     back_ref,
     out_ref,
@@ -157,9 +156,10 @@
     eye_b = eye.astype(bf16)
     emb_t_ref[...] = dot_t(eye_b, w_emb).astype(bf16)
     chan_ref[...] = dot_t(eye_b, w_chan_t).astype(bf16)
-    w_chan_t_ref[...] = w_chan_t
+    chans = w_chan_t.shape[0]
+    forward_ref[0:chans, :] = w_chan_t
     turned = (0.5 * dot_t(eye_b, w_back)).astype(bf16)
-    lat_t_ref[...] = turned[:, 0:features]
+    forward_ref[chans:, :] = turned[:, 0:features]
     ten_t_ref[...] = turned[:, features:]
     back_ref[...] = w_back
     column = jnp.sum(eye * small_ref[8:9, :], axis=1, keepdims=True)
@@ -280,8 +280,8 @@
 
 
 FIELDS = (
-    ["hot", "extra", "center_hot", "low_o", "latent", "slope", "chan"]
-    + ["geo", "dlat", "dharm", "tensor", "acc_o", "acc_c"]
+    ["hot", "extra", "center_hot", "lows", "linear", "slope", "chan"]
+    + ["geo", "dlat", "dharm", "tensor", "acc"]
 )
 Scratch = collections.namedtuple("Scratch", FIELDS)
 
@@ -296,9 +296,8 @@
     slab_ref,
     w_emb_ref,
     w_rad_ref,
-    w_chan_t_ref,
+    w_forward_ref,
     w_chan_ref,
-    w_lat_t_ref,
     w_ten_t_ref,
     w_back_ref,
     w_out_ref,
@@ -310,7 +309,6 @@
     feat_c,
     place,
     place_b,
-    own_b,
     tensor_b,
     *scratch,
 ):
@@ -324,7 +322,7 @@
     highs = table // LANES
     span = tensor_b.shape[2]
     halves_n = tensor_b.shape[0]
-    chans = w_chan_t_ref.shape[0]
+    chans = w_chan_ref.shape[1]
     hpad = place_in_ref.shape[1]
     first_blocks = meta_ref[0, 0]
     total_blocks = meta_ref[1, 0]
@@ -344,11 +342,12 @@
     upper, lower = halves(joined)
     place[0:3, highs - 1, :] = upper
     place[3:6, highs - 1, :] = lower
-    place_b[...] = place[...].reshape(6 * hpad, LANES).astype(bf16)
-    own_b[...] = place[:, 0:8, :].reshape(48, LANES).astype(bf16)
+    place_b[...] = jnp.zeros_like(place_b)
+    place_b[0 : 6 * hpad, 0:LANES] = place[...].reshape(6 * hpad, LANES).astype(bf16)
+    place_b[6 * hpad :, LANES:] = place[:, 0:8, :].reshape(48, LANES).astype(bf16)
     for own in (even, odd):
         own.hot[WINDOW + span + 32 :, :] = jnp.zeros((LANES - 32, eb), bf16)
-        for ref in (own.extra, own.tensor, own.acc_o, own.acc_c):
+        for ref in (own.extra, own.tensor, own.acc):
             ref[...] = jnp.zeros_like(ref)
 
     def half_of(b):
@@ -377,7 +376,8 @@
         o_high = lax.shift_right_logical(o, 7)
         hot_c = one_hot(lax.bitwise_and(c, LANES - 1), LANES).astype(bf16)
         hot_o = one_hot(lax.bitwise_and(o, LANES - 1), LANES).astype(bf16)
-        own_s.low_o[at] = hot_o
+        lows = jnp.concatenate([hot_o, hot_c], axis=0)
+        own_s.lows[at] = lows
         c_high16 = jnp.broadcast_to(c_high, (16, eb))
         o_high16 = jnp.broadcast_to(o_high, (16, eb))
         shift = 2 * meta_ref[2, b]
@@ -390,10 +390,10 @@
         own_s.center_hot[at] = own
         hot[WINDOW : WINDOW + span, :] = own
 
-        picked = dot(place_b[...], hot_o)
-        picked = (picked[0 : 3 * hpad] + picked[3 * hpad :]).reshape(3, hpad, eb)
+        both = dot(place_b[...], lows)
+        picked = (both[0 : 3 * hpad] + both[3 * hpad : 6 * hpad]).reshape(3, hpad, eb)
         po = jnp.sum(picked * one_hot(o_high, hpad)[None], axis=1)
-        picked = dot(own_b[...], hot_c)
+        picked = both[6 * hpad :]
         picked = (picked[0:24] + picked[24:48]).reshape(3, 8, eb)
         c_whole = c_high + half * (span // LANES)
         pc = jnp.sum(picked * one_hot(c_whole, 8)[None], axis=1)
@@ -461,14 +461,15 @@
         up = 1.0 + jnp.tanh(mixed)
         value = mixed * up
         latent = value.astype(bf16)
-        own_s.latent[at] = latent
         own_s.slope[at] = (up + value * (2.0 - up)).astype(bf16)
         return latent
 
     def spread(side, latent, geo):
         own_s, _, at = side
         x, y, z, live, _ = geo
-        chan = dot(w_chan_t_ref[...], latent) * live
+        both = dot(w_forward_ref[...], latent)
+        own_s.linear[at] = both[chans:]
+        chan = both[0:chans] * live
         own_s.chan[at] = chan
         return jnp.concatenate(
             [
@@ -518,7 +519,7 @@
         return jnp.concatenate([band.astype(bf16) for band in bands], axis=0)
 
     def hidden(side, invariant):
-        return dot(w_lat_t_ref[...], side[0].latent[side[2]]) + dot(w_ten_t_ref[...], invariant)
+        return side[0].linear[side[2]] + dot(w_ten_t_ref[...], invariant)
 
     def readout(side, pre):
         own_s, _, at = side
@@ -606,13 +607,19 @@
             [mask_o * split[d][part] for part in range(2) for d in range(3)], axis=0
         ).astype(bf16)
         split.append(halves(energy))
+        values = jnp.concatenate(
+            [split[d][part] for part in range(2) for d in range(4)], axis=0
+        )
+        c_high = lax.shift_right_arithmetic(centers_ref[b], 7)
         rows_c = jnp.concatenate(
-            [split[d][part] for part in range(2) for d in range(4)]
-            + [jnp.zeros((8, eb), f32)],
+            [
+                values * jnp.where(c_high == high, 1.0, 0.0)
+                for high in range(span // LANES)
+            ],
             axis=0,
         ).astype(bf16)
-        own_s.acc_o[...] += dot_t(rows_o, own_s.low_o[at])
-        own_s.acc_c[half_of(b)] += dot_t(rows_c, own_s.center_hot[at])
+        rows = jnp.concatenate([rows_o, rows_c], axis=0)
+        own_s.acc[half_of(b)] += dot_t(rows, own_s.lows[at])
 
     def third_pass(sides):
         gathered = [gather_tensor(side) for side in sides]
@@ -624,22 +631,22 @@
             finish(side, drad, dh)
 
     each_block(third_pass)
-    sum_o = even.acc_o[...] + odd.acc_o[...]
+    acc = [even.acc[half] + odd.acc[half] for half in range(halves_n)]
+    sum_o = sum(value[0 : 6 * hpad, 0:LANES] for value in acc)
     sum_o = sum_o[0 : 3 * hpad] + sum_o[3 * hpad :]
     for d in range(3):
         grad_ref[d] = sum_o[d * hpad : (d + 1) * hpad]
         slab_grad_ref[d : d + 1, :] = sum_o[d * hpad + highs - 1 : d * hpad + highs]
     for half in range(halves_n):
-        sum_c = even.acc_c[half] + odd.acc_c[half]
-        sum_c = sum_c[0:4] + sum_c[4:8]
         for part in range(span // LANES):
             high = half * (span // LANES) + part
-            lanes = slice(part * LANES, (part + 1) * LANES)
+            base = 6 * hpad + part * 8
+            sum_c = acc[half][base : base + 4, LANES:] + acc[half][base + 4 : base + 8, LANES:]
             for d in range(3):
                 grad_ref[d, high : high + 1, :] = (
-                    sum_o[d * hpad + high : d * hpad + high + 1] - sum_c[d : d + 1, lanes]
+                    sum_o[d * hpad + high : d * hpad + high + 1] - sum_c[d : d + 1]
                 )
-            energy_ref[:, high * LANES : (high + 1) * LANES] = sum_c[3:4, lanes]
+            energy_ref[:, high * LANES : (high + 1) * LANES] = sum_c[3:4]
 
 
 def return_kernel(grad_ref, back_ref, picks_ref, own_ref, to_xm_ref, to_xp_ref, to_ym_ref, to_yp_ref):
@@ -758,28 +765,9 @@
     pairs = -(-(edges // eb + atoms // span - 1) // 2)
     slot_rows = -(-(2 * pairs * eb // LANES) // 8) * 8
     lift = (1 - 2 * lax.axis_index("gz")).astype(f32).reshape(1)
-    big = 42 * 1024 * 1024
+    big = 44 * 1024 * 1024
 
     shape = jax.ShapeDtypeStruct
-    prepared = call(
-        weights_kernel,
-        (
-            shape((features, width), bf16),
-            shape((features, LANES), bf16),
-            shape((features, chans), bf16),
-            shape((chans, features), bf16),
-            shape((features, features), bf16),
-            shape((features, 3 * chans), bf16),
-            shape((features + 3 * chans, features), bf16),
-            shape((features, LANES), f32),
-            shape((16, features), bf16),
-        ),
-        (
-            jnp.concatenate([w_emb, w_lat, w_ten, w_chan.T], axis=0),
-            jnp.concatenate([w_rbf, w_out[None]], axis=0),
-        ),
-        [pltpu.VMEM((LANES, features), f32)],
-    )
     picks = jnp.concatenate([rim, zr], axis=0)
     own, *sent = call(
         pack_kernel,
@@ -821,9 +809,28 @@
         (shape((height, 2 * LANES), bf16),) * 2,
         (got[0], got[1]),
     )
+    w_emb, w_rbf, to_plus = lax.optimization_barrier((w_emb, w_rbf, to_plus))
+    prepared = call(
+        weights_kernel,
+        (
+            shape((features, width), bf16),
+            shape((features, LANES), bf16),
+            shape((features, chans), bf16),
+            shape((chans + features, features), bf16),
+            shape((features, 3 * chans), bf16),
+            shape((features + 3 * chans, features), bf16),
+            shape((features, LANES), f32),
+            shape((16, features), bf16),
+        ),
+        (
+            jnp.concatenate([w_emb, w_lat, w_ten, w_chan.T], axis=0),
+            jnp.concatenate([w_rbf, w_out[None]], axis=0),
+        ),
+        [pltpu.VMEM((LANES, features), f32)],
+    )
     corners = [shifted(to_plus, "gx", -1), shifted(to_minus, "gx", 1)]
     corners, prepared = lax.optimization_barrier((corners, prepared))
-    w_emb_t, w_rad, w_chan_r, w_chan_t, w_lat_t, w_ten_t, w_back, w_out_col, w_rbf2 = prepared
+    w_emb_t, w_rad, w_chan_r, w_forward, w_ten_t, w_back, w_out_col, w_rbf2 = prepared
     inner, slab_send = call(
         slab_kernel,
         (shape((height, inner_len), bf16), shape((height, LANES), bf16)),
@@ -849,9 +856,8 @@
             slab_got,
             w_emb_t,
             w_rad,
-            w_chan_t,
+            w_forward,
             w_chan_r,
-            w_lat_t,
             w_ten_t,
             w_back,
             w_out_col,
@@ -861,24 +867,22 @@
             pltpu.VMEM((features, (groups - 1) * 256 + WINDOW), bf16),
             pltpu.VMEM((atoms // span, features, span + LANES), bf16),
             pltpu.VMEM((6, hpad, LANES), f32),
-            pltpu.VMEM((6 * hpad, LANES), bf16),
-            pltpu.VMEM((48, LANES), bf16),
+            pltpu.VMEM((6 * hpad + 48, 2 * LANES), bf16),
             pltpu.VMEM((atoms // span, 9 * chans, span), bf16),
         ]
         + [
             pltpu.VMEM((WINDOW + span + LANES, eb), bf16),
             pltpu.VMEM((features, eb), f32),
             pltpu.VMEM((pairs, span, eb), bf16),
-            pltpu.VMEM((pairs, LANES, eb), bf16),
-            pltpu.VMEM((pairs, features, eb), bf16),
+            pltpu.VMEM((pairs, 2 * LANES, eb), bf16),
+            pltpu.VMEM((pairs, features, eb), f32),
             pltpu.VMEM((pairs, features, eb), bf16),
             pltpu.VMEM((pairs, chans, eb), f32),
             pltpu.VMEM((pairs, 16, eb), f32),
             pltpu.VMEM((pairs, features, eb), bf16),
             pltpu.VMEM((pairs, 64, eb), f32),
             pltpu.VMEM((atoms // span, 9 * chans, span), f32),
-            pltpu.VMEM((6 * hpad, LANES), f32),
-            pltpu.VMEM((atoms // span, 16, span), f32),
+            pltpu.VMEM((atoms // span, 6 * hpad + 8 * (span // LANES), 2 * LANES), f32),
         ]
         * 2,
         smem=2,

time: 74.2 us -> 73 us (0.984); the launches traced: 72.8 us -> 72.8 us
  starting transfers between devices: 26.2 us -> 13 us
  Pallas kernels: 30.1 us -> 42.4 us
  waiting for transfers between devices: 10.4 us -> 11.3 us
    pallas_call x10, Pallas kernels: 30.1 us -> 42.4 us  [call(): pl.pallas_call(kernel, out_shape=out_shape, in_specs=[scalar] * smem + [v...]
    ppermute x10, starting transfers between devices: 22.4 us -> 11.3 us  [shifted(): lax.ppermute(x, axis, [((i + step) % count, i) for i in range(count)])]
    ppermute x2, starting transfers between devices: 3.8 us -> 1.71 us  [swapped(): return lax.ppermute(x, 'gz', [(i, i ^ 1) for i in range(count)])]
    ppermute x2, waiting for transfers between devices: 3.12 us -> 5.14 us  [swapped(): return lax.ppermute(x, 'gz', [(i, i ^ 1) for i in range(count)])]
    ppermute x10, waiting for transfers between devices: 7.27 us -> 6.13 us  [shifted(): lax.ppermute(x, axis, [((i + step) % count, i) for i in range(count)])]
  transfers between devices with their start and end apart: 12 -> 12, of which waited for: 7 -> 6; matrix products, arithmetic and copies ran while one was open for 3% -> 3% of each run, Pallas kernels for 5% -> 5%
where the time goes in v1:
time: 73 us; the launch traced here: 72.8 us
  Pallas kernels  42.4 us (58%)
  starting transfers between devices  13 us (18%)
  waiting for transfers between devices  11.3 us (15%)
  other arithmetic  3.19 us (4%)
  local copies, waits for them, and re-layouts  1.59 us (2%)
  between operations  1.4 us (2%)
    pallas_call x10, Pallas kernels, call(): pl.pallas_call(kernel, out_shape=out_shape, in_specs=[scalar] * smem + [v...  42.4 us
    ppermute x10, starting transfers between devices, shifted(): lax.ppermute(x, axis, [((i + step) % count, i) for i in range(count)])  11.3 us
    ppermute x10, waiting for transfers between devices, shifted(): lax.ppermute(x, axis, [((i + step) % count, i) for i in range(count)])  6.13 us
    ppermute x2, waiting for transfers between devices, swapped(): return lax.ppermute(x, 'gz', [(i, i ^ 1) for i in range(count)])  5.14 us
    ppermute x2, starting transfers between devices, swapped(): return lax.ppermute(x, 'gz', [(i, i ^ 1) for i in range(count)])  1.71 us
    unnamed x4, local copies, waits for them, and re-layouts  1.59 us
  transfers between devices with their start and end apart: 12, of which 6 were waited for; matrix products, arithmetic and copies ran while one was open for 3% of the time, Pallas kernels for 5%

profile of v1, /device:TPU:0, one launch (start us, length us, event | category | flops | bytes accessed | tf_op | source)
XLA Modules:
  0.0 72.8 jit_solution(2186929413911736320)
XLA Ops:
  0.6 0.7 pad_add_fusion.1.picks_ref
  1.3 0.9 %copy-done = bf16[1,1,1,512,128]{4,3,2,1,0:T(8,128)(2,1)S(1)} copy-done((bf16[1,1,1,512,128]{4,3,2,1,0:T(8,128)(2,1)S(1)}, bf16[1,1,1,512,128]{4,3,2,1,0:T(8,128)(2,1)}, u32[]{:S(2)}) %copy-start) | copy-done | bytes 131096
  2.2 0.7 copy-done.1
  2.9 0.6 shard_map.140
  3.5 3.1 %collective-permute-start = (bf16[144,384]{1,0:T(8,128)(2,1)S(1)}, bf16[144,384]{1,0:T(8,128)(2,1)S(1)}, u32[]{:S(2)}, u32[]{:S(2)}) collective-permute-start(bf16[144,384]{1,0:T(8,128)(2,1)S(1)} %get-tuple-element.52), channel_id=1, source_target_pairs={{6,0},{0,2},{2,4},{4,6},{7,1},{1,3},{3,5},{5,7},{14,8},{8,10},{10,... | collective-permute-start | bytes 331784 | tf_op jit(solution)/shard_map/ppermute | solution.py:727
  6.6 2.1 %collective-permute-start.1 = (bf16[144,384]{1,0:T(8,128)(2,1)S(1)}, bf16[144,384]{1,0:T(8,128)(2,1)S(1)}, u32[]{:S(2)}, u32[]{:S(2)}) collective-permute-start(bf16[144,384]{1,0:T(8,128)(2,1)S(1)} %get-tuple-element.53), channel_id=1, source_target_pairs={{2,0},{4,2},{6,4},{0,6},{3,1},{5,3},{7,5},{1,7},{10,8},{12,10},{14... | collective-permute-start | bytes 331784 | tf_op jit(solution)/shard_map/ppermute | solution.py:727
  8.7 1.7 %collective-permute-start.3 = (bf16[144,384]{1,0:T(8,128)(2,1)S(1)}, bf16[144,384]{1,0:T(8,128)(2,1)S(1)}, u32[]{:S(2)}, u32[]{:S(2)}) collective-permute-start(bf16[144,384]{1,0:T(8,128)(2,1)S(1)} %get-tuple-element.64), channel_id=1, source_target_pairs={{8,0},{16,8},{24,16},{0,24},{9,1},{17,9},{25,17},{1,25},{10,2},{18... | collective-permute-start | bytes 331784 | tf_op jit(solution)/shard_map/ppermute | solution.py:727
  11.1 0.8 %pad_add_fusion.ends_ref = s32[96,128]{1,0:T(8,128)S(1)} fusion(s32[48,128]{1,0:T(8,128)} %bitcast.22, s32[48,128]{1,0:T(8,128)} %bitcast.23), kind=kLoop, calls=%fused_computation.1 | loop fusion | flops 12288 | bytes 98304 | tf_op jit(solution)/shard_map/concatenate | solution.py:783
  11.9 2.5 %shard_map.141 = (s32[56,128]{1,0:T(8,128)S(1)}, s32[56,128]{1,0:T(8,128)S(1)}, s32[4,128]{1,0:T(4,128)S(1)}) custom-call(s32[1]{0:T(128)} %bitcast.16.count_ref, s32[96,128]{1,0:T(8,128)S(1)} %pad_add_fusion.ends_ref), custom_call_target="tpu_custom_call" | custom-call | tf_op jit(solution)/shard_map/pallas_call | solution.py:715
  14.5 1.7 %collective-permute-start.5 = (bf16[144,256]{1,0:T(8,128)(2,1)S(1)}, bf16[144,256]{1,0:T(8,128)(2,1)S(1)}, u32[]{:S(2)}, u32[]{:S(2)}) collective-permute-start(bf16[144,256]{1,0:T(8,128)(2,1)S(1)} %get-tuple-element.67), channel_id=1, source_target_pairs={{8,0},{16,8},{24,16},{0,24},{9,1},{17,9},{25,17},{1,25},{10,2},{18... | collective-permute-start | bytes 221192 | tf_op jit(solution)/shard_map/ppermute | solution.py:727
  16.2 1.0 %pad_maximum_fusion.stacked_ref = bf16[640,256]{1,0:T(8,128)(2,1)S(1)} fusion(bf16[64,256]{1,0:T(8,128)(2,1)} %bitcast.21, bf16[192,256]{1,0:T(8,128)(2,1)} %param.24, bf16[256,256]{1,0:T(8,128)(2,1)} %param.23, bf16[128,256]{1,0:T(8,128)(2,1)} %param.20), kind=kLoop, calls=%fused_computation | loop fusion | flops 1310720 | bytes 655360 | tf_op jit(solution)/shard_map/concatenate | solution.py:826
  17.2 0.7 pad_maximum_fusion.1.small_ref
  18.7 1.7 %collective-permute-start.6 = (bf16[144,128]{1,0:T(8,128)(2,1)S(1)}, bf16[144,128]{1,0:T(8,128)(2,1)S(1)}, u32[]{:S(2)}, u32[]{:S(2)}) collective-permute-start(bf16[144,128]{1,0:T(8,128)(2,1)S(1)} %get-tuple-element.84), channel_id=1, source_target_pairs={{0,1},{1,0},{2,3},{3,2},{4,5},{5,4},{6,7},{7,6},{8,9},{9,8},{10,11... | collective-permute-start | bytes 110600 | tf_op jit(solution)/shard_map/ppermute | solution.py:732
  20.4 0.8 %shard_map.145 = (bf16[256,2560]{1,0:T(8,128)(2,1)S(1)}, f32[6,24,128]{2,1,0:T(8,128)S(1)}) custom-call(bf16[144,2560]{1,0:T(8,128)(2,1)S(1)} %get-tuple-element.80.inner_ref, bf16[256,128]{1,0:T(8,128)(2,1)S(1)} %get-tuple-element.81.w_emb_ref), custom_call_target="tpu_custom_call" | custom-call | tf_op jit(solution)/shard_map/pallas_call | solution.py:715
  21.1 1.6 %collective-permute-done.6.slab_ref = bf16[144,128]{1,0:T(8,128)(2,1)S(1)} collective-permute-done((bf16[144,128]{1,0:T(8,128)(2,1)S(1)}, bf16[144,128]{1,0:T(8,128)(2,1)S(1)}, u32[]{:S(2)}, u32[]{:S(2)}) %collective-permute-start.6) | collective-permute-done | bytes 36896 | tf_op jit(solution)/shard_map/ppermute | solution.py:732
  22.7 36.7 %shard_map.146 = (f32[3,24,128]{2,1,0:T(8,128)S(1)}, f32[3,128]{1,0:T(4,128)S(1)}, f32[1,512]{1,0:T(1,128)}) custom-call(s32[4,128]{1,0:T(4,128)S(1)} %get-tuple-element.57.meta_ref, f32[1]{0:T(128)} %bitcast.7.lift_ref, s32[14,1,512]{2,1,0:T(1,128)S(1)} %bitcast.18, s32[14,1,512]{2,1,0:T(1,128)S(1)} %bitcast.19, ...), custom_call_target="tpu_custom_call" | custom-call | tf_op jit(solution)/shard_map/pallas_call | solution.py:715
  59.5 3.6 %collective-permute-done.7.back_ref = f32[3,128]{1,0:T(4,128)S(1)} collective-permute-done((f32[3,128]{1,0:T(4,128)S(1)}, f32[3,128]{1,0:T(4,128)S(1)}, u32[]{:S(2)}, u32[]{:S(2)}) %collective-permute-start.7) | collective-permute-done | bytes 1568 | tf_op jit(solution)/shard_map/ppermute | solution.py:732
  63.3 0.5 collective-permute-start.9
  63.8 0.9 %collective-permute-done.8.from_xp_ref = f32[15,128]{1,0:T(8,128)S(1)} collective-permute-done((f32[15,128]{1,0:T(8,128)S(1)}, f32[15,128]{1,0:T(8,128)S(1)}, u32[]{:S(2)}, u32[]{:S(2)}) %collective-permute-start.8) | collective-permute-done | bytes 7712 | tf_op jit(solution)/shard_map/ppermute | solution.py:727
  64.6 1.8 %collective-permute-done.9.from_xm_ref = f32[15,128]{1,0:T(8,128)S(1)} collective-permute-done((f32[15,128]{1,0:T(8,128)S(1)}, f32[15,128]{1,0:T(8,128)S(1)}, u32[]{:S(2)}, u32[]{:S(2)}) %collective-permute-start.9) | collective-permute-done | bytes 7712 | tf_op jit(solution)/shard_map/ppermute | solution.py:727
  66.4 2.0 %collective-permute-start.11 = (f32[9,128]{1,0:T(8,128)S(1)}, f32[9,128]{1,0:T(8,128)S(1)}, u32[]{:S(2)}, u32[]{:S(2)}) collective-permute-start(f32[9,128]{1,0:T(8,128)S(1)} %get-tuple-element.101), channel_id=1, source_target_pairs={{6,0},{0,2},{2,4},{4,6},{7,1},{1,3},{3,5},{5,7},{14,8},{8,10},{10,... | collective-permute-start | bytes 13832 | tf_op jit(solution)/shard_map/ppermute | solution.py:727
  68.4 1.6 %collective-permute-done.10.from_yp_ref = f32[9,128]{1,0:T(8,128)S(1)} collective-permute-done((f32[9,128]{1,0:T(8,128)S(1)}, f32[9,128]{1,0:T(8,128)S(1)}, u32[]{:S(2)}, u32[]{:S(2)}) %collective-permute-start.10) | collective-permute-done | bytes 4640 | tf_op jit(solution)/shard_map/ppermute | solution.py:727
  70.1 1.9 %collective-permute-done.11.from_ym_ref = f32[9,128]{1,0:T(8,128)S(1)} collective-permute-done((f32[9,128]{1,0:T(8,128)S(1)}, f32[9,128]{1,0:T(8,128)S(1)}, u32[]{:S(2)}, u32[]{:S(2)}) %collective-permute-start.11) | collective-permute-done | bytes 4640 | tf_op jit(solution)/shard_map/ppermute | solution.py:727
  71.9 0.9 %shard_map.149 = f32[3,1,512]{2,1,0:T(1,128)} custom-call(f32[3,8,128]{2,1,0:T(8,128)S(1)} %get-tuple-element.95.own_ref, s32[9,128]{1,0:T(8,128)S(1)} %pad_add_fusion.1.picks_ref, f32[15,128]{1,0:T(8,128)S(1)} %collective-permute-done.8.from_xp_ref, f32[15,128]{1,0:T(8,128)S(1)} %collective-permute-done.9.from_xm_ref, ...), custom_call_target="tpu_custom_call" | custom-call | tf_op jit(solution)/shard_map/pallas_call | solution.py:715
  (18 shorter events, 1.1 us)
Async XLA Ops:
  1.3 0.9 %copy-start = (bf16[1,1,1,512,128]{4,3,2,1,0:T(8,128)(2,1)S(1)}, bf16[1,1,1,512,128]{4,3,2,1,0:T(8,128)(2,1)}, u32[]{:S(2)}) copy-start(bf16[1,1,1,512,128]{4,3,2,1,0:T(8,128)(2,1)} %param.14) | copy-start | bytes 393220
  2.2 0.7 copy-start.1
  3.5 10.8 %collective-permute-start = (bf16[144,384]{1,0:T(8,128)(2,1)S(1)}, bf16[144,384]{1,0:T(8,128)(2,1)S(1)}, u32[]{:S(2)}, u32[]{:S(2)}) collective-permute-start(bf16[144,384]{1,0:T(8,128)(2,1)S(1)} %get-tuple-element.52), channel_id=1, source_target_pairs={{6,0},{0,2},{2,4},{4,6},{7,1},{1,3},{3,5},{5,7},{14,8},{8,10},{10,... | collective-permute-start | bytes 331784 | tf_op jit(solution)/shard_map/ppermute | solution.py:727
  6.6 7.7 %collective-permute-start.1 = (bf16[144,384]{1,0:T(8,128)(2,1)S(1)}, bf16[144,384]{1,0:T(8,128)(2,1)S(1)}, u32[]{:S(2)}, u32[]{:S(2)}) collective-permute-start(bf16[144,384]{1,0:T(8,128)(2,1)S(1)} %get-tuple-element.53), channel_id=1, source_target_pairs={{2,0},{4,2},{6,4},{0,6},{3,1},{5,3},{7,5},{1,7},{10,8},{12,10},{14... | collective-permute-start | bytes 331784 | tf_op jit(solution)/shard_map/ppermute | solution.py:727
  8.7 9.6 %collective-permute-start.2 = (bf16[144,384]{1,0:T(8,128)(2,1)S(1)}, bf16[144,384]{1,0:T(8,128)(2,1)S(1)}, u32[]{:S(2)}, u32[]{:S(2)}) collective-permute-start(bf16[144,384]{1,0:T(8,128)(2,1)S(1)} %get-tuple-element.63), channel_id=1, source_target_pairs={{24,0},{0,8},{8,16},{16,24},{25,1},{1,9},{9,17},{17,25},{26,2},{2,... | collective-permute-start | bytes 331784 | tf_op jit(solution)/shard_map/ppermute | solution.py:727
  8.7 9.6 %collective-permute-start.3 = (bf16[144,384]{1,0:T(8,128)(2,1)S(1)}, bf16[144,384]{1,0:T(8,128)(2,1)S(1)}, u32[]{:S(2)}, u32[]{:S(2)}) collective-permute-start(bf16[144,384]{1,0:T(8,128)(2,1)S(1)} %get-tuple-element.64), channel_id=1, source_target_pairs={{8,0},{16,8},{24,16},{0,24},{9,1},{17,9},{25,17},{1,25},{10,2},{18... | collective-permute-start | bytes 331784 | tf_op jit(solution)/shard_map/ppermute | solution.py:727
  14.4 3.8 %collective-permute-start.4 = (bf16[144,256]{1,0:T(8,128)(2,1)S(1)}, bf16[144,256]{1,0:T(8,128)(2,1)S(1)}, u32[]{:S(2)}, u32[]{:S(2)}) collective-permute-start(bf16[144,256]{1,0:T(8,128)(2,1)S(1)} %get-tuple-element.66), channel_id=1, source_target_pairs={{24,0},{0,8},{8,16},{16,24},{25,1},{1,9},{9,17},{17,25},{26,2},{2,... | collective-permute-start | bytes 221192 | tf_op jit(solution)/shard_map/ppermute | solution.py:727
  14.5 3.8 %collective-permute-start.5 = (bf16[144,256]{1,0:T(8,128)(2,1)S(1)}, bf16[144,256]{1,0:T(8,128)(2,1)S(1)}, u32[]{:S(2)}, u32[]{:S(2)}) collective-permute-start(bf16[144,256]{1,0:T(8,128)(2,1)S(1)} %get-tuple-element.67), channel_id=1, source_target_pairs={{8,0},{16,8},{24,16},{0,24},{9,1},{17,9},{25,17},{1,25},{10,2},{18... | collective-permute-start | bytes 221192 | tf_op jit(solution)/shard_map/ppermute | solution.py:727
  18.7 4.0 %collective-permute-start.6 = (bf16[144,128]{1,0:T(8,128)(2,1)S(1)}, bf16[144,128]{1,0:T(8,128)(2,1)S(1)}, u32[]{:S(2)}, u32[]{:S(2)}) collective-permute-start(bf16[144,128]{1,0:T(8,128)(2,1)S(1)} %get-tuple-element.84), channel_id=1, source_target_pairs={{0,1},{1,0},{2,3},{3,2},{4,5},{5,4},{6,7},{7,6},{8,9},{9,8},{10,11... | collective-permute-start | bytes 110600 | tf_op jit(solution)/shard_map/ppermute | solution.py:732
  59.5 3.6 %collective-permute-start.7 = (f32[3,128]{1,0:T(4,128)S(1)}, f32[3,128]{1,0:T(4,128)S(1)}, u32[]{:S(2)}, u32[]{:S(2)}) collective-permute-start(f32[3,128]{1,0:T(4,128)S(1)} %get-tuple-element.94), channel_id=1, source_target_pairs={{0,1},{1,0},{2,3},{3,2},{4,5},{5,4},{6,7},{7,6},{8,9},{9,8},{10,11... | collective-permute-start | bytes 4616 | tf_op jit(solution)/shard_map/ppermute | solution.py:732
  63.2 1.4 %collective-permute-start.8 = (f32[15,128]{1,0:T(8,128)S(1)}, f32[15,128]{1,0:T(8,128)S(1)}, u32[]{:S(2)}, u32[]{:S(2)}) collective-permute-start(f32[15,128]{1,0:T(8,128)S(1)} %get-tuple-element.96), channel_id=1, source_target_pairs={{8,0},{16,8},{24,16},{0,24},{9,1},{17,9},{25,17},{1,25},{10,2},{18... | collective-permute-start | bytes 23048 | tf_op jit(solution)/shard_map/ppermute | solution.py:727
  63.3 3.1 %collective-permute-start.9 = (f32[15,128]{1,0:T(8,128)S(1)}, f32[15,128]{1,0:T(8,128)S(1)}, u32[]{:S(2)}, u32[]{:S(2)}) collective-permute-start(f32[15,128]{1,0:T(8,128)S(1)} %get-tuple-element.97), channel_id=1, source_target_pairs={{24,0},{0,8},{8,16},{16,24},{25,1},{1,9},{9,17},{17,25},{26,2},{2,... | collective-permute-start | bytes 23048 | tf_op jit(solution)/shard_map/ppermute | solution.py:727
  66.4 3.7 %collective-permute-start.10 = (f32[9,128]{1,0:T(8,128)S(1)}, f32[9,128]{1,0:T(8,128)S(1)}, u32[]{:S(2)}, u32[]{:S(2)}) collective-permute-start(f32[9,128]{1,0:T(8,128)S(1)} %get-tuple-element.100), channel_id=1, source_target_pairs={{2,0},{4,2},{6,4},{0,6},{3,1},{5,3},{7,5},{1,7},{10,8},{12,10},{14... | collective-permute-start | bytes 13832 | tf_op jit(solution)/shard_map/ppermute | solution.py:727
  66.4 5.5 %collective-permute-start.11 = (f32[9,128]{1,0:T(8,128)S(1)}, f32[9,128]{1,0:T(8,128)S(1)}, u32[]{:S(2)}, u32[]{:S(2)}) collective-permute-start(f32[9,128]{1,0:T(8,128)S(1)} %get-tuple-element.101), channel_id=1, source_target_pairs={{6,0},{0,2},{2,4},{4,6},{7,1},{1,3},{3,5},{5,7},{14,8},{8,10},{10,... | collective-permute-start | bytes 13832 | tf_op jit(solution)/shard_map/ppermute | solution.py:727

commit v2 on v1

--- a/solution.py
+++ b/solution.py
@@ -139,8 +139,8 @@
     emb_t_ref,
     rad_ref,
     chan_ref,
-    forward_ref,
-    ten_t_ref,
+    w_chan_t_ref,
+    hidden_ref,
     back_ref,
     out_ref,
     rbf_ref,
@@ -156,11 +156,9 @@
     eye_b = eye.astype(bf16)
     emb_t_ref[...] = dot_t(eye_b, w_emb).astype(bf16)
     chan_ref[...] = dot_t(eye_b, w_chan_t).astype(bf16)
-    chans = w_chan_t.shape[0]
-    forward_ref[0:chans, :] = w_chan_t
+    w_chan_t_ref[...] = w_chan_t
     turned = (0.5 * dot_t(eye_b, w_back)).astype(bf16)
-    forward_ref[chans:, :] = turned[:, 0:features]
-    ten_t_ref[...] = turned[:, features:]
+    hidden_ref[...] = turned
     back_ref[...] = w_back
     column = jnp.sum(eye * small_ref[8:9, :], axis=1, keepdims=True)
     out_ref[...] = jnp.broadcast_to(column, out_ref.shape)
@@ -280,8 +278,8 @@
 
 
 FIELDS = (
-    ["hot", "extra", "center_hot", "lows", "linear", "slope", "chan"]
-    + ["geo", "dlat", "dharm", "tensor", "acc"]
+    ["hot", "extra", "center_hot", "lows", "latent", "slope", "chan"]
+    + ["geo", "res", "dlat", "dharm", "tensor", "acc"]
 )
 Scratch = collections.namedtuple("Scratch", FIELDS)
 
@@ -296,9 +294,9 @@
     slab_ref,
     w_emb_ref,
     w_rad_ref,
-    w_forward_ref,
+    w_chan_t_ref,
     w_chan_ref,
-    w_ten_t_ref,
+    w_hidden_ref,
     w_back_ref,
     w_out_ref,
     w_rbf_ref,
@@ -364,55 +362,70 @@
         def _():
             run([(even, 2 * pairs, pairs)])
 
+    def locate(sides):
+        for own_s, b, at in sides:
+            slot_c = centers_ref[b]
+            o = others_ref[b]
+            c = jnp.maximum(slot_c, 0)
+            c_high = lax.shift_right_logical(c, 7)
+            o_high = lax.shift_right_logical(o, 7)
+            hot_c = one_hot(lax.bitwise_and(c, LANES - 1), LANES).astype(bf16)
+            hot_o = one_hot(lax.bitwise_and(o, LANES - 1), LANES).astype(bf16)
+            lows = jnp.concatenate([hot_o, hot_c], axis=0)
+            own_s.lows[at] = lows
+            c_high16 = jnp.broadcast_to(c_high, (16, eb))
+            own_s.center_hot[at] = jnp.concatenate(
+                [masked(hot_c, c_high16, high) for high in range(span // LANES)], axis=0
+            )
+            both = dot(place_b[...], lows)
+            picked = (both[0 : 3 * hpad] + both[3 * hpad : 6 * hpad]).reshape(3, hpad, eb)
+            po = jnp.sum(picked * one_hot(o_high, hpad)[None], axis=1)
+            picked = both[6 * hpad :]
+            picked = (picked[0:24] + picked[24:48]).reshape(3, 8, eb)
+            c_whole = c_high + half_of(b) * (span // LANES)
+            pc = jnp.sum(picked * one_hot(c_whole, 8)[None], axis=1)
+            sep = po - pc
+            row = pl.ds(at, 1)
+            for d in range(3):
+                own_s.geo[d, row, :] = sep[d : d + 1]
+            own_s.geo[6, row, :] = jnp.where(slot_c >= 0, 1.0, 0.0)
+
+    each_block(locate)
+    for own in (even, odd):
+        rx, ry, rz = own.geo[0], own.geo[1], own.geo[2]
+        squared = rx * rx + ry * ry + rz * rz
+        inv_d = lax.rsqrt(squared + 0.25)
+        x, y, z = rx * inv_d, ry * inv_d, rz * inv_d
+        own.geo[3] = inv_d
+        own.geo[4] = (squared + 0.25) * inv_d
+        own.geo[5] = 1.0 / (1.0 + squared * squared * (1.0 / 16.0))
+        own.geo[7] = squared
+        for m, value in enumerate(harmonic_rows(x, y, z)[1:]):
+            own.geo[8 + m] = value
+
+    def geo_row(side, index):
+        own_s, _, at = side
+        return own_s.geo[index, pl.ds(at, 1), :]
+
+    def harmonics(side):
+        return [None] + [geo_row(side, 8 + m) for m in range(8)]
+
     def prepare(side):
         own_s, b, at = side
         hot = own_s.hot
-        slot_c = centers_ref[b]
-        o = others_ref[b]
-        live = jnp.where(slot_c >= 0, 1.0, 0.0)
-        c = jnp.maximum(slot_c, 0)
-        half = half_of(b)
-        c_high = lax.shift_right_logical(c, 7)
-        o_high = lax.shift_right_logical(o, 7)
-        hot_c = one_hot(lax.bitwise_and(c, LANES - 1), LANES).astype(bf16)
-        hot_o = one_hot(lax.bitwise_and(o, LANES - 1), LANES).astype(bf16)
-        lows = jnp.concatenate([hot_o, hot_c], axis=0)
-        own_s.lows[at] = lows
-        c_high16 = jnp.broadcast_to(c_high, (16, eb))
+        hot_o = own_s.lows[at, 0:LANES, :]
+        o_high = lax.shift_right_logical(others_ref[b], 7) - 2 * meta_ref[2, b]
         o_high16 = jnp.broadcast_to(o_high, (16, eb))
-        shift = 2 * meta_ref[2, b]
         for high in range(WINDOW // LANES):
             rows = slice(high * LANES, (high + 1) * LANES)
-            hot[rows, :] = masked(hot_o, o_high16 - shift, high)
-        own = jnp.concatenate(
-            [masked(hot_c, c_high16, high) for high in range(span // LANES)], axis=0
-        )
-        own_s.center_hot[at] = own
-        hot[WINDOW : WINDOW + span, :] = own
-
-        both = dot(place_b[...], lows)
-        picked = (both[0 : 3 * hpad] + both[3 * hpad : 6 * hpad]).reshape(3, hpad, eb)
-        po = jnp.sum(picked * one_hot(o_high, hpad)[None], axis=1)
-        picked = both[6 * hpad :]
-        picked = (picked[0:24] + picked[24:48]).reshape(3, 8, eb)
-        c_whole = c_high + half * (span // LANES)
-        pc = jnp.sum(picked * one_hot(c_whole, 8)[None], axis=1)
-        sep = po - pc
-        rx, ry, rz = sep[0:1], sep[1:2], sep[2:3]
-        squared = rx * rx + ry * ry + rz * rz
-        inv_d = lax.rsqrt(squared + 0.25)
-        dist = (squared + 0.25) * inv_d
-        env = 1.0 / (1.0 + squared * squared * (1.0 / 16.0))
-        x, y, z = rx * inv_d, ry * inv_d, rz * inv_d
-        for row, value in enumerate((x, y, z, inv_d, dist, env, squared, live)):
-            own_s.geo[at, row : row + 1, :] = value
+            hot[rows, :] = masked(hot_o, o_high16, high)
+        hot[WINDOW : WINDOW + span, :] = own_s.center_hot[at]
         mu = 0.5 + 0.4 * rows_of((8, eb)).astype(f32)
-        u = (dist - mu) * 2.0
-        upper, lower = halves(jnp.exp(-(u * u)) * env)
+        u = (geo_row(side, 4) - mu) * 2.0
+        upper, lower = halves(jnp.exp(-(u * u)) * geo_row(side, 5))
         radial = jnp.concatenate([upper, lower], axis=0).astype(bf16)
         hot[WINDOW + span : WINDOW + span + 16, :] = radial
         hot[WINDOW + span + 16 : WINDOW + span + 32, :] = radial
-        return x, y, z, live, own
 
     def window(group):
         return feat[:, pl.ds(pl.multiple_of(group * 256, 256), WINDOW)]
@@ -452,9 +465,8 @@
 
     def mix(side):
         own_s, b, _ = side
-        mixed = dot(window(meta_ref[2, b]), own_s.hot[0:WINDOW, :])
-        mixed = mixed + dot(feat_c[half_of(b)], own_s.hot[WINDOW:, :])
-        return mixed + own_s.extra[...]
+        tables = jnp.concatenate([window(meta_ref[2, b]), feat_c[half_of(b)]], axis=1)
+        return dot(tables, own_s.hot[...]) + own_s.extra[...]
 
     def activate(side, mixed):
         own_s, _, at = side
@@ -464,19 +476,13 @@
         own_s.slope[at] = (up + value * (2.0 - up)).astype(bf16)
         return latent
 
-    def spread(side, latent, geo):
+    def spread(side, latent):
         own_s, _, at = side
-        x, y, z, live, _ = geo
-        both = dot(w_forward_ref[...], latent)
-        own_s.linear[at] = both[chans:]
-        chan = both[0:chans] * live
+        own_s.latent[at] = latent
+        chan = dot(w_chan_t_ref[...], latent) * geo_row(side, 6)
         own_s.chan[at] = chan
         return jnp.concatenate(
-            [
-                (chan if h is None else chan * h).astype(bf16)
-                for h in harmonic_rows(x, y, z)
-            ],
-            axis=0,
+            [(chan if h is None else chan * h).astype(bf16) for h in harmonics(side)], axis=0
         )
 
     def gather_tensor(side):
@@ -488,17 +494,17 @@
         own_s.tensor[half_of(b)] += dot_t(products, hot)
 
     def first_pass(sides):
-        geos, mixed = [], []
         for side in sides:
             further_windows(side)
+        mixed = []
         for side in sides:
-            geos.append(prepare(side))
+            prepare(side)
             mixed.append(mix(side))
         products = []
-        for side, geo, values in zip(sides, geos, mixed):
-            products.append(spread(side, activate(side, values), geo))
-        for side, geo, values in zip(sides, geos, products):
-            add_tensor(side, values, geo[4])
+        for side, values in zip(sides, mixed):
+            products.append(spread(side, activate(side, values)))
+        for side, values in zip(sides, products):
+            add_tensor(side, values, side[0].center_hot[side[2]])
         for side in sides:
             clear_windows(side)
 
@@ -508,8 +514,7 @@
         own.tensor[...] = jnp.zeros_like(own.tensor)
 
     def invariants(side, gathered):
-        geo = side[0].geo[side[2]]
-        harm = harmonic_rows(geo[0:1], geo[1:2], geo[2:3])
+        harm = harmonics(side)
         parts = [gathered[m * chans : (m + 1) * chans] for m in range(9)]
         bands = [parts[0], None, None]
         for m in range(1, 9):
@@ -519,22 +524,21 @@
         return jnp.concatenate([band.astype(bf16) for band in bands], axis=0)
 
     def hidden(side, invariant):
-        return side[0].linear[side[2]] + dot(w_ten_t_ref[...], invariant)
+        inputs = jnp.concatenate([side[0].latent[side[2]], invariant], axis=0)
+        return dot(w_hidden_ref[...], inputs)
 
     def readout(side, pre):
         own_s, _, at = side
-        geo = own_s.geo[at]
         up = 1.0 + jnp.tanh(pre)
         value = pre * up
         weight = jnp.concatenate([w_out_ref[...]] * (eb // LANES), axis=1)
-        own_s.geo[at, 8:9, :] = jnp.sum(value * weight, axis=0, keepdims=True)
-        scale = 0.5 * geo[5:6] * geo[7:8]
+        own_s.res[10, pl.ds(at, 1), :] = jnp.sum(value * weight, axis=0, keepdims=True)
+        scale = 0.5 * geo_row(side, 5) * geo_row(side, 6)
         return ((up + value * (2.0 - up)) * (weight * scale)).astype(bf16)
 
     def unfold(side, back, gathered):
         own_s, _, at = side
-        geo = own_s.geo[at]
-        harm = harmonic_rows(geo[0:1], geo[1:2], geo[2:3])
+        harm = harmonics(side)
         own_s.dlat[at] = back[0:features].astype(bf16)
         dbands = [
             back[features + band * chans : features + (band + 1) * chans] for band in range(3)
@@ -562,75 +566,70 @@
 
     def channels_back(side, gathered):
         own_s, _, at = side
-        geo = own_s.geo[at]
-        harm = harmonic_rows(geo[0:1], geo[1:2], geo[2:3])
+        harm = harmonics(side)
         chan = own_s.chan[at]
         dchan = gathered[0:chans]
-        dh = [None]
         for m in range(1, 9):
             part = gathered[m * chans : (m + 1) * chans]
             dchan = dchan + part * harm[m]
             total = own_s.dharm[at, (m - 1) * 8 : m * 8, :] + fold8(part * chan)
-            dh.append(jnp.sum(total, axis=0, keepdims=True))
-        return (dchan * geo[7:8]).astype(bf16), dh
+            own_s.res[m - 1, pl.ds(at, 1), :] = jnp.sum(total, axis=0, keepdims=True)
+        return (dchan * geo_row(side, 6)).astype(bf16)
 
     def radial_back(side, dchan):
         own_s, _, at = side
         dlat = own_s.dlat[at] + dot(w_chan_ref[...], dchan).astype(bf16)
         drad = dot(w_rbf_ref[...], dlat * own_s.slope[at])
-        return drad[0:8] + drad[8:16]
-
-    def finish(side, drad, dh):
-        own_s, b, at = side
-        geo = own_s.geo[at]
-        x, y, z = geo[0:1], geo[1:2], geo[2:3]
-        inv_d, dist, env, squared = geo[3:4], geo[4:5], geo[5:6], geo[6:7]
-        live, summed = geo[7:8], geo[8:9]
+        drad = drad[0:8] + drad[8:16]
         mu = 0.5 + 0.4 * rows_of((8, eb)).astype(f32)
-        u = (dist - mu) * 2.0
+        u = (geo_row(side, 4) - mu) * 2.0
         weighted = drad * jnp.exp(-(u * u))
-        denv = jnp.sum(weighted, axis=0, keepdims=True) + live * summed
-        ddist = -4.0 * env * jnp.sum(weighted * u, axis=0, keepdims=True)
+        own_s.res[8, pl.ds(at, 1), :] = jnp.sum(weighted, axis=0, keepdims=True)
+        own_s.res[9, pl.ds(at, 1), :] = jnp.sum(weighted * u, axis=0, keepdims=True)
+
+    def third_pass(sides):
+        gathered = [gather_tensor(side) for side in sides]
+        for side, g in zip(sides, gathered):
+            radial_back(side, channels_back(side, g))
+
+    each_block(third_pass)
+
+    for own in (even, odd):
+        x, y, z = own.geo[8], own.geo[9], own.geo[10]
+        inv_d, dist, env = own.geo[3], own.geo[4], own.geo[5]
+        live, squared = own.geo[6], own.geo[7]
+        dh = [None] + [own.res[m] for m in range(8)]
+        summed = own.res[10]
+        denv = own.res[8] + live * summed
+        ddist = -4.0 * env * own.res[9]
         dx = dh[1] + ROOT3 * (y * dh[4] + z * dh[6] + x * dh[7])
         dy = dh[2] + ROOT3 * (x * dh[4] + z * dh[5] - y * dh[7])
         dz = dh[3] + ROOT3 * (y * dh[5] + x * dh[6]) + 3.0 * z * dh[8]
         ddist = ddist - (dx * x + dy * y + dz * z) * inv_d
         dsq = denv * (env * env * squared * -0.125) + ddist * (0.5 * inv_d)
         both = 2.0 * dsq * dist
-        gs = [dx * inv_d + both * x, dy * inv_d + both * y, dz * inv_d + both * z]
-        energy = summed * env * live
-
-        o_high = lax.shift_right_logical(others_ref[b], 7)
-        mask_o = one_hot(o_high, hpad)
-        split = [halves(g) for g in gs]
-        rows_o = jnp.concatenate(
-            [mask_o * split[d][part] for part in range(2) for d in range(3)], axis=0
-        ).astype(bf16)
-        split.append(halves(energy))
-        values = jnp.concatenate(
-            [split[d][part] for part in range(2) for d in range(4)], axis=0
-        )
-        c_high = lax.shift_right_arithmetic(centers_ref[b], 7)
-        rows_c = jnp.concatenate(
-            [
-                values * jnp.where(c_high == high, 1.0, 0.0)
-                for high in range(span // LANES)
-            ],
-            axis=0,
-        ).astype(bf16)
-        rows = jnp.concatenate([rows_o, rows_c], axis=0)
-        own_s.acc[half_of(b)] += dot_t(rows, own_s.lows[at])
-
-    def third_pass(sides):
-        gathered = [gather_tensor(side) for side in sides]
-        back = []
-        for side, g in zip(sides, gathered):
-            dchan, dh = channels_back(side, g)
-            back.append((radial_back(side, dchan), dh))
-        for side, (drad, dh) in zip(sides, back):
-            finish(side, drad, dh)
-
-    each_block(third_pass)
+        results = [dx * inv_d + both * x, dy * inv_d + both * y, dz * inv_d + both * z]
+        results.append(summed * env * live)
+        for index, value in enumerate(results):
+            own.res[index], own.res[4 + index] = halves(value)
+
+    def collect(sides):
+        for own_s, b, at in sides:
+            split = [own_s.res[index, pl.ds(at, 1), :] for index in range(8)]
+            mask_o = one_hot(lax.shift_right_logical(others_ref[b], 7), hpad)
+            values = jnp.concatenate(split, axis=0)
+            c_high = lax.shift_right_arithmetic(centers_ref[b], 7)
+            rows = jnp.concatenate(
+                [mask_o * split[4 * part + d] for part in range(2) for d in range(3)]
+                + [
+                    values * jnp.where(c_high == high, 1.0, 0.0)
+                    for high in range(span // LANES)
+                ],
+                axis=0,
+            ).astype(bf16)
+            own_s.acc[half_of(b)] += dot_t(rows, own_s.lows[at])
+
+    each_block(collect)
     acc = [even.acc[half] + odd.acc[half] for half in range(halves_n)]
     sum_o = sum(value[0 : 6 * hpad, 0:LANES] for value in acc)
     sum_o = sum_o[0 : 3 * hpad] + sum_o[3 * hpad :]
@@ -765,7 +764,7 @@
     pairs = -(-(edges // eb + atoms // span - 1) // 2)
     slot_rows = -(-(2 * pairs * eb // LANES) // 8) * 8
     lift = (1 - 2 * lax.axis_index("gz")).astype(f32).reshape(1)
-    big = 44 * 1024 * 1024
+    big = 42 * 1024 * 1024
 
     shape = jax.ShapeDtypeStruct
     picks = jnp.concatenate([rim, zr], axis=0)
@@ -816,8 +815,8 @@
             shape((features, width), bf16),
             shape((features, LANES), bf16),
             shape((features, chans), bf16),
-            shape((chans + features, features), bf16),
-            shape((features, 3 * chans), bf16),
+            shape((chans, features), bf16),
+            shape((features, features + 3 * chans), bf16),
             shape((features + 3 * chans, features), bf16),
             shape((features, LANES), f32),
             shape((16, features), bf16),
@@ -830,7 +829,7 @@
     )
     corners = [shifted(to_plus, "gx", -1), shifted(to_minus, "gx", 1)]
     corners, prepared = lax.optimization_barrier((corners, prepared))
-    w_emb_t, w_rad, w_chan_r, w_forward, w_ten_t, w_back, w_out_col, w_rbf2 = prepared
+    w_emb_t, w_rad, w_chan_r, w_chan_t, w_hidden, w_back, w_out_col, w_rbf2 = prepared
     inner, slab_send = call(
         slab_kernel,
         (shape((height, inner_len), bf16), shape((height, LANES), bf16)),
@@ -856,9 +855,9 @@
             slab_got,
             w_emb_t,
             w_rad,
-            w_forward,
+            w_chan_t,
             w_chan_r,
-            w_ten_t,
+            w_hidden,
             w_back,
             w_out_col,
             w_rbf2,
@@ -875,10 +874,11 @@
             pltpu.VMEM((features, eb), f32),
             pltpu.VMEM((pairs, span, eb), bf16),
             pltpu.VMEM((pairs, 2 * LANES, eb), bf16),
-            pltpu.VMEM((pairs, features, eb), f32),
+            pltpu.VMEM((pairs, features, eb), bf16),
             pltpu.VMEM((pairs, features, eb), bf16),
             pltpu.VMEM((pairs, chans, eb), f32),
-            pltpu.VMEM((pairs, 16, eb), f32),
+            pltpu.VMEM((16, -(-pairs // 8) * 8, eb), f32),
+            pltpu.VMEM((11, -(-pairs // 8) * 8, eb), f32),
             pltpu.VMEM((pairs, features, eb), bf16),
             pltpu.VMEM((pairs, 64, eb), f32),
             pltpu.VMEM((atoms // span, 9 * chans, span), f32),

time: 73 us -> 74.3 us (1.018)
  starting transfers between devices: 13 us -> 25.5 us
  Pallas kernels: 42.4 us -> 30.3 us
    pallas_call x10, Pallas kernels: 42.4 us -> 30.3 us  [call(): pl.pallas_call(kernel, out_shape=out_shape, in_specs=[scalar] * smem + [v...]
    ppermute x10, starting transfers between devices: 11.3 us -> 22.6 us  [shifted(): lax.ppermute(x, axis, [((i + step) % count, i) for i in range(count)])]
    ppermute x10, waiting for transfers between devices: 6.13 us -> 8.09 us  [shifted(): lax.ppermute(x, axis, [((i + step) % count, i) for i in range(count)])]
    ppermute x2, waiting for transfers between devices: 5.14 us -> 3.92 us  [swapped(): return lax.ppermute(x, 'gz', [(i, i ^ 1) for i in range(count)])]
    ppermute x2, starting transfers between devices: 1.71 us -> 2.92 us  [swapped(): return lax.ppermute(x, 'gz', [(i, i ^ 1) for i in range(count)])]
where the time goes in v2:
time: 74.3 us; the launch traced here: 74 us
  Pallas kernels  30.3 us (41%)
  starting transfers between devices  25.5 us (34%)
  waiting for transfers between devices  12 us (16%)
  other arithmetic  3.19 us (4%)
  local copies, waits for them, and re-layouts  1.59 us (2%)
  between operations  1.4 us (2%)
    pallas_call x10, Pallas kernels, call(): pl.pallas_call(kernel, out_shape=out_shape, in_specs=[scalar] * smem + [v...  30.3 us
    ppermute x10, starting transfers between devices, shifted(): lax.ppermute(x, axis, [((i + step) % count, i) for i in range(count)])  22.6 us
    ppermute x10, waiting for transfers between devices, shifted(): lax.ppermute(x, axis, [((i + step) % count, i) for i in range(count)])  8.09 us
    ppermute x2, waiting for transfers between devices, swapped(): return lax.ppermute(x, 'gz', [(i, i ^ 1) for i in range(count)])  3.92 us
    ppermute x2, starting transfers between devices, swapped(): return lax.ppermute(x, 'gz', [(i, i ^ 1) for i in range(count)])  2.92 us
    unnamed x4, local copies, waits for them, and re-layouts  1.59 us
  transfers between devices with their start and end apart: 12, of which 6 were waited for; matrix products, arithmetic and copies ran while one was open for 3% of the time, Pallas kernels for 5%

profile of v2, /device:TPU:0, one launch (start us, length us, event | category | flops | bytes accessed | tf_op | source)
XLA Modules:
  0.0 74.0 jit_solution(9121419365095176106)
XLA Ops:
  0.6 0.7 pad_add_fusion.1.picks_ref
  1.3 0.9 %copy-done = bf16[1,1,1,512,128]{4,3,2,1,0:T(8,128)(2,1)S(1)} copy-done((bf16[1,1,1,512,128]{4,3,2,1,0:T(8,128)(2,1)S(1)}, bf16[1,1,1,512,128]{4,3,2,1,0:T(8,128)(2,1)}, u32[]{:S(2)}) %copy-start) | copy-done | bytes 131096
  2.2 0.7 copy-done.1
  2.9 0.6 shard_map.140
  3.5 3.1 %collective-permute-start = (bf16[144,384]{1,0:T(8,128)(2,1)S(1)}, bf16[144,384]{1,0:T(8,128)(2,1)S(1)}, u32[]{:S(2)}, u32[]{:S(2)}) collective-permute-start(bf16[144,384]{1,0:T(8,128)(2,1)S(1)} %get-tuple-element.52), channel_id=1, source_target_pairs={{6,0},{0,2},{2,4},{4,6},{7,1},{1,3},{3,5},{5,7},{14,8},{8,10},{10,... | collective-permute-start | bytes 331784 | tf_op jit(solution)/shard_map/ppermute | solution.py:726
  6.6 2.1 %collective-permute-start.1 = (bf16[144,384]{1,0:T(8,128)(2,1)S(1)}, bf16[144,384]{1,0:T(8,128)(2,1)S(1)}, u32[]{:S(2)}, u32[]{:S(2)}) collective-permute-start(bf16[144,384]{1,0:T(8,128)(2,1)S(1)} %get-tuple-element.53), channel_id=1, source_target_pairs={{2,0},{4,2},{6,4},{0,6},{3,1},{5,3},{7,5},{1,7},{10,8},{12,10},{14... | collective-permute-start | bytes 331784 | tf_op jit(solution)/shard_map/ppermute | solution.py:726
  8.7 1.7 %collective-permute-start.3 = (bf16[144,384]{1,0:T(8,128)(2,1)S(1)}, bf16[144,384]{1,0:T(8,128)(2,1)S(1)}, u32[]{:S(2)}, u32[]{:S(2)}) collective-permute-start(bf16[144,384]{1,0:T(8,128)(2,1)S(1)} %get-tuple-element.64), channel_id=1, source_target_pairs={{8,0},{16,8},{24,16},{0,24},{9,1},{17,9},{25,17},{1,25},{10,2},{18... | collective-permute-start | bytes 331784 | tf_op jit(solution)/shard_map/ppermute | solution.py:726
  11.1 0.8 %pad_add_fusion.ends_ref = s32[96,128]{1,0:T(8,128)S(1)} fusion(s32[48,128]{1,0:T(8,128)} %bitcast.22, s32[48,128]{1,0:T(8,128)} %bitcast.23), kind=kLoop, calls=%fused_computation.1 | loop fusion | flops 12288 | bytes 98304 | tf_op jit(solution)/shard_map/concatenate | solution.py:782
  11.9 2.5 %shard_map.141 = (s32[56,128]{1,0:T(8,128)S(1)}, s32[56,128]{1,0:T(8,128)S(1)}, s32[4,128]{1,0:T(4,128)S(1)}) custom-call(s32[1]{0:T(128)} %bitcast.16.count_ref, s32[96,128]{1,0:T(8,128)S(1)} %pad_add_fusion.ends_ref), custom_call_target="tpu_custom_call" | custom-call | tf_op jit(solution)/shard_map/pallas_call | solution.py:714
  14.5 1.7 %collective-permute-start.5 = (bf16[144,256]{1,0:T(8,128)(2,1)S(1)}, bf16[144,256]{1,0:T(8,128)(2,1)S(1)}, u32[]{:S(2)}, u32[]{:S(2)}) collective-permute-start(bf16[144,256]{1,0:T(8,128)(2,1)S(1)} %get-tuple-element.67), channel_id=1, source_target_pairs={{8,0},{16,8},{24,16},{0,24},{9,1},{17,9},{25,17},{1,25},{10,2},{18... | collective-permute-start | bytes 221192 | tf_op jit(solution)/shard_map/ppermute | solution.py:726
  16.2 1.0 %pad_maximum_fusion.stacked_ref = bf16[640,256]{1,0:T(8,128)(2,1)S(1)} fusion(bf16[64,256]{1,0:T(8,128)(2,1)} %bitcast.21, bf16[192,256]{1,0:T(8,128)(2,1)} %param.24, bf16[256,256]{1,0:T(8,128)(2,1)} %param.23, bf16[128,256]{1,0:T(8,128)(2,1)} %param.20), kind=kLoop, calls=%fused_computation | loop fusion | flops 1310720 | bytes 655360 | tf_op jit(solution)/shard_map/concatenate | solution.py:825
  17.2 0.7 pad_maximum_fusion.1.small_ref
  18.7 1.7 %collective-permute-start.6 = (bf16[144,128]{1,0:T(8,128)(2,1)S(1)}, bf16[144,128]{1,0:T(8,128)(2,1)S(1)}, u32[]{:S(2)}, u32[]{:S(2)}) collective-permute-start(bf16[144,128]{1,0:T(8,128)(2,1)S(1)} %get-tuple-element.84), channel_id=1, source_target_pairs={{0,1},{1,0},{2,3},{3,2},{4,5},{5,4},{6,7},{7,6},{8,9},{9,8},{10,11... | collective-permute-start | bytes 110600 | tf_op jit(solution)/shard_map/ppermute | solution.py:731
  20.4 0.8 %shard_map.145 = (bf16[256,2560]{1,0:T(8,128)(2,1)S(1)}, f32[6,24,128]{2,1,0:T(8,128)S(1)}) custom-call(bf16[144,2560]{1,0:T(8,128)(2,1)S(1)} %get-tuple-element.80.inner_ref, bf16[256,128]{1,0:T(8,128)(2,1)S(1)} %get-tuple-element.81.w_emb_ref), custom_call_target="tpu_custom_call" | custom-call | tf_op jit(solution)/shard_map/pallas_call | solution.py:714
  21.1 1.6 %collective-permute-done.6.slab_ref = bf16[144,128]{1,0:T(8,128)(2,1)S(1)} collective-permute-done((bf16[144,128]{1,0:T(8,128)(2,1)S(1)}, bf16[144,128]{1,0:T(8,128)(2,1)S(1)}, u32[]{:S(2)}, u32[]{:S(2)}) %collective-permute-start.6) | collective-permute-done | bytes 36896 | tf_op jit(solution)/shard_map/ppermute | solution.py:731
  22.7 24.7 %shard_map.146 = (f32[3,24,128]{2,1,0:T(8,128)S(1)}, f32[3,128]{1,0:T(4,128)S(1)}, f32[1,512]{1,0:T(1,128)}) custom-call(s32[4,128]{1,0:T(4,128)S(1)} %get-tuple-element.57.meta_ref, f32[1]{0:T(128)} %bitcast.7.lift_ref, s32[14,1,512]{2,1,0:T(1,128)S(1)} %bitcast.18, s32[14,1,512]{2,1,0:T(1,128)S(1)} %bitcast.19, ...), custom_call_target="tpu_custom_call" | custom-call | tf_op jit(solution)/shard_map/pallas_call | solution.py:714
  47.4 1.2 %collective-permute-start.7 = (f32[3,128]{1,0:T(4,128)S(1)}, f32[3,128]{1,0:T(4,128)S(1)}, u32[]{:S(2)}, u32[]{:S(2)}) collective-permute-start(f32[3,128]{1,0:T(4,128)S(1)} %get-tuple-element.94), channel_id=1, source_target_pairs={{0,1},{1,0},{2,3},{3,2},{4,5},{5,4},{6,7},{7,6},{8,9},{9,8},{10,11... | collective-permute-start | bytes 4616 | tf_op jit(solution)/shard_map/ppermute | solution.py:731
  48.6 2.4 %collective-permute-done.7.back_ref = f32[3,128]{1,0:T(4,128)S(1)} collective-permute-done((f32[3,128]{1,0:T(4,128)S(1)}, f32[3,128]{1,0:T(4,128)S(1)}, u32[]{:S(2)}, u32[]{:S(2)}) %collective-permute-start.7) | collective-permute-done | bytes 1568 | tf_op jit(solution)/shard_map/ppermute | solution.py:731
  51.7 0.9 %collective-permute-done.8.from_xp_ref = f32[15,128]{1,0:T(8,128)S(1)} collective-permute-done((f32[15,128]{1,0:T(8,128)S(1)}, f32[15,128]{1,0:T(8,128)S(1)}, u32[]{:S(2)}, u32[]{:S(2)}) %collective-permute-start.8) | collective-permute-done | bytes 7712 | tf_op jit(solution)/shard_map/ppermute | solution.py:726
  52.6 1.8 %collective-permute-done.9.from_xm_ref = f32[15,128]{1,0:T(8,128)S(1)} collective-permute-done((f32[15,128]{1,0:T(8,128)S(1)}, f32[15,128]{1,0:T(8,128)S(1)}, u32[]{:S(2)}, u32[]{:S(2)}) %collective-permute-start.9) | collective-permute-done | bytes 7712 | tf_op jit(solution)/shard_map/ppermute | solution.py:726
  54.3 13.3 %collective-permute-start.10 = (f32[9,128]{1,0:T(8,128)S(1)}, f32[9,128]{1,0:T(8,128)S(1)}, u32[]{:S(2)}, u32[]{:S(2)}) collective-permute-start(f32[9,128]{1,0:T(8,128)S(1)} %get-tuple-element.100), channel_id=1, source_target_pairs={{2,0},{4,2},{6,4},{0,6},{3,1},{5,3},{7,5},{1,7},{10,8},{12,10},{14... | collective-permute-start | bytes 13832 | tf_op jit(solution)/shard_map/ppermute | solution.py:726
  67.7 1.4 %collective-permute-done.10.from_yp_ref = f32[9,128]{1,0:T(8,128)S(1)} collective-permute-done((f32[9,128]{1,0:T(8,128)S(1)}, f32[9,128]{1,0:T(8,128)S(1)}, u32[]{:S(2)}, u32[]{:S(2)}) %collective-permute-start.10) | collective-permute-done | bytes 4640 | tf_op jit(solution)/shard_map/ppermute | solution.py:726
  69.1 4.1 %collective-permute-done.11.from_ym_ref = f32[9,128]{1,0:T(8,128)S(1)} collective-permute-done((f32[9,128]{1,0:T(8,128)S(1)}, f32[9,128]{1,0:T(8,128)S(1)}, u32[]{:S(2)}, u32[]{:S(2)}) %collective-permute-start.11) | collective-permute-done | bytes 4640 | tf_op jit(solution)/shard_map/ppermute | solution.py:726
  73.1 0.9 %shard_map.149 = f32[3,1,512]{2,1,0:T(1,128)} custom-call(f32[3,8,128]{2,1,0:T(8,128)S(1)} %get-tuple-element.95.own_ref, s32[9,128]{1,0:T(8,128)S(1)} %pad_add_fusion.1.picks_ref, f32[15,128]{1,0:T(8,128)S(1)} %collective-permute-done.8.from_xp_ref, f32[15,128]{1,0:T(8,128)S(1)} %collective-permute-done.9.from_xm_ref, ...), custom_call_target="tpu_custom_call" | custom-call | tf_op jit(solution)/shard_map/pallas_call | solution.py:714
  (18 shorter events, 1.6 us)
Async XLA Ops:
  1.3 0.9 %copy-start = (bf16[1,1,1,512,128]{4,3,2,1,0:T(8,128)(2,1)S(1)}, bf16[1,1,1,512,128]{4,3,2,1,0:T(8,128)(2,1)}, u32[]{:S(2)}) copy-start(bf16[1,1,1,512,128]{4,3,2,1,0:T(8,128)(2,1)} %param.14) | copy-start | bytes 393220
  2.2 0.7 copy-start.1
  3.5 10.8 %collective-permute-start = (bf16[144,384]{1,0:T(8,128)(2,1)S(1)}, bf16[144,384]{1,0:T(8,128)(2,1)S(1)}, u32[]{:S(2)}, u32[]{:S(2)}) collective-permute-start(bf16[144,384]{1,0:T(8,128)(2,1)S(1)} %get-tuple-element.52), channel_id=1, source_target_pairs={{6,0},{0,2},{2,4},{4,6},{7,1},{1,3},{3,5},{5,7},{14,8},{8,10},{10,... | collective-permute-start | bytes 331784 | tf_op jit(solution)/shard_map/ppermute | solution.py:726
  6.6 7.7 %collective-permute-start.1 = (bf16[144,384]{1,0:T(8,128)(2,1)S(1)}, bf16[144,384]{1,0:T(8,128)(2,1)S(1)}, u32[]{:S(2)}, u32[]{:S(2)}) collective-permute-start(bf16[144,384]{1,0:T(8,128)(2,1)S(1)} %get-tuple-element.53), channel_id=1, source_target_pairs={{2,0},{4,2},{6,4},{0,6},{3,1},{5,3},{7,5},{1,7},{10,8},{12,10},{14... | collective-permute-start | bytes 331784 | tf_op jit(solution)/shard_map/ppermute | solution.py:726
  8.7 9.6 %collective-permute-start.2 = (bf16[144,384]{1,0:T(8,128)(2,1)S(1)}, bf16[144,384]{1,0:T(8,128)(2,1)S(1)}, u32[]{:S(2)}, u32[]{:S(2)}) collective-permute-start(bf16[144,384]{1,0:T(8,128)(2,1)S(1)} %get-tuple-element.63), channel_id=1, source_target_pairs={{24,0},{0,8},{8,16},{16,24},{25,1},{1,9},{9,17},{17,25},{26,2},{2,... | collective-permute-start | bytes 331784 | tf_op jit(solution)/shard_map/ppermute | solution.py:726
  8.7 9.6 %collective-permute-start.3 = (bf16[144,384]{1,0:T(8,128)(2,1)S(1)}, bf16[144,384]{1,0:T(8,128)(2,1)S(1)}, u32[]{:S(2)}, u32[]{:S(2)}) collective-permute-start(bf16[144,384]{1,0:T(8,128)(2,1)S(1)} %get-tuple-element.64), channel_id=1, source_target_pairs={{8,0},{16,8},{24,16},{0,24},{9,1},{17,9},{25,17},{1,25},{10,2},{18... | collective-permute-start | bytes 331784 | tf_op jit(solution)/shard_map/ppermute | solution.py:726
  14.4 3.8 %collective-permute-start.4 = (bf16[144,256]{1,0:T(8,128)(2,1)S(1)}, bf16[144,256]{1,0:T(8,128)(2,1)S(1)}, u32[]{:S(2)}, u32[]{:S(2)}) collective-permute-start(bf16[144,256]{1,0:T(8,128)(2,1)S(1)} %get-tuple-element.66), channel_id=1, source_target_pairs={{24,0},{0,8},{8,16},{16,24},{25,1},{1,9},{9,17},{17,25},{26,2},{2,... | collective-permute-start | bytes 221192 | tf_op jit(solution)/shard_map/ppermute | solution.py:726
  14.5 3.8 %collective-permute-start.5 = (bf16[144,256]{1,0:T(8,128)(2,1)S(1)}, bf16[144,256]{1,0:T(8,128)(2,1)S(1)}, u32[]{:S(2)}, u32[]{:S(2)}) collective-permute-start(bf16[144,256]{1,0:T(8,128)(2,1)S(1)} %get-tuple-element.67), channel_id=1, source_target_pairs={{8,0},{16,8},{24,16},{0,24},{9,1},{17,9},{25,17},{1,25},{10,2},{18... | collective-permute-start | bytes 221192 | tf_op jit(solution)/shard_map/ppermute | solution.py:726
  18.7 4.0 %collective-permute-start.6 = (bf16[144,128]{1,0:T(8,128)(2,1)S(1)}, bf16[144,128]{1,0:T(8,128)(2,1)S(1)}, u32[]{:S(2)}, u32[]{:S(2)}) collective-permute-start(bf16[144,128]{1,0:T(8,128)(2,1)S(1)} %get-tuple-element.84), channel_id=1, source_target_pairs={{0,1},{1,0},{2,3},{3,2},{4,5},{5,4},{6,7},{7,6},{8,9},{9,8},{10,11... | collective-permute-start | bytes 110600 | tf_op jit(solution)/shard_map/ppermute | solution.py:731
  47.4 3.6 %collective-permute-start.7 = (f32[3,128]{1,0:T(4,128)S(1)}, f32[3,128]{1,0:T(4,128)S(1)}, u32[]{:S(2)}, u32[]{:S(2)}) collective-permute-start(f32[3,128]{1,0:T(4,128)S(1)} %get-tuple-element.94), channel_id=1, source_target_pairs={{0,1},{1,0},{2,3},{3,2},{4,5},{5,4},{6,7},{7,6},{8,9},{9,8},{10,11... | collective-permute-start | bytes 4616 | tf_op jit(solution)/shard_map/ppermute | solution.py:731
  51.1 1.4 %collective-permute-start.8 = (f32[15,128]{1,0:T(8,128)S(1)}, f32[15,128]{1,0:T(8,128)S(1)}, u32[]{:S(2)}, u32[]{:S(2)}) collective-permute-start(f32[15,128]{1,0:T(8,128)S(1)} %get-tuple-element.96), channel_id=1, source_target_pairs={{8,0},{16,8},{24,16},{0,24},{9,1},{17,9},{25,17},{1,25},{10,2},{18... | collective-permute-start | bytes 23048 | tf_op jit(solution)/shard_map/ppermute | solution.py:726
  51.2 3.1 %collective-permute-start.9 = (f32[15,128]{1,0:T(8,128)S(1)}, f32[15,128]{1,0:T(8,128)S(1)}, u32[]{:S(2)}, u32[]{:S(2)}) collective-permute-start(f32[15,128]{1,0:T(8,128)S(1)} %get-tuple-element.97), channel_id=1, source_target_pairs={{24,0},{0,8},{8,16},{16,24},{25,1},{1,9},{9,17},{17,25},{26,2},{2,... | collective-permute-start | bytes 23048 | tf_op jit(solution)/shard_map/ppermute | solution.py:726
  54.3 14.7 %collective-permute-start.10 = (f32[9,128]{1,0:T(8,128)S(1)}, f32[9,128]{1,0:T(8,128)S(1)}, u32[]{:S(2)}, u32[]{:S(2)}) collective-permute-start(f32[9,128]{1,0:T(8,128)S(1)} %get-tuple-element.100), channel_id=1, source_target_pairs={{2,0},{4,2},{6,4},{0,6},{3,1},{5,3},{7,5},{1,7},{10,8},{12,10},{14... | collective-permute-start | bytes 13832 | tf_op jit(solution)/shard_map/ppermute | solution.py:726
  67.7 5.4 %collective-permute-start.11 = (f32[9,128]{1,0:T(8,128)S(1)}, f32[9,128]{1,0:T(8,128)S(1)}, u32[]{:S(2)}, u32[]{:S(2)}) collective-permute-start(f32[9,128]{1,0:T(8,128)S(1)} %get-tuple-element.101), channel_id=1, source_target_pairs={{6,0},{0,2},{2,4},{4,6},{7,1},{1,3},{3,5},{5,7},{14,8},{8,10},{10,... | collective-permute-start | bytes 13832 | tf_op jit(solution)/shard_map/ppermute | solution.py:726

commit v3 on v2

--- a/solution.py
+++ b/solution.py
@@ -278,7 +278,7 @@
 
 
 FIELDS = (
-    ["hot", "extra", "center_hot", "lows", "latent", "slope", "chan"]
+    ["hot", "extra", "center_hot", "edge_hot", "lows", "latent", "slope", "chan"]
     + ["geo", "res", "dlat", "dharm", "tensor", "acc"]
 )
 Scratch = collections.namedtuple("Scratch", FIELDS)
@@ -374,9 +374,11 @@
             lows = jnp.concatenate([hot_o, hot_c], axis=0)
             own_s.lows[at] = lows
             c_high16 = jnp.broadcast_to(c_high, (16, eb))
-            own_s.center_hot[at] = jnp.concatenate(
+            center_hot = jnp.concatenate(
                 [masked(hot_c, c_high16, high) for high in range(span // LANES)], axis=0
             )
+            own_s.center_hot[at] = center_hot
+            own_s.edge_hot[at] = center_hot.T
             both = dot(place_b[...], lows)
             picked = (both[0 : 3 * hpad] + both[3 * hpad : 6 * hpad]).reshape(3, hpad, eb)
             po = jnp.sum(picked * one_hot(o_high, hpad)[None], axis=1)
@@ -489,9 +491,9 @@
         own_s, b, at = side
         return dot(tensor_b[half_of(b)], own_s.center_hot[at])
 
-    def add_tensor(side, products, hot):
-        own_s, b, _ = side
-        own_s.tensor[half_of(b)] += dot_t(products, hot)
+    def add_tensor(side, products):
+        own_s, b, at = side
+        own_s.tensor[half_of(b)] += dot(products, own_s.edge_hot[at])
 
     def first_pass(sides):
         for side in sides:
@@ -504,7 +506,7 @@
         for side, values in zip(sides, mixed):
             products.append(spread(side, activate(side, values)))
         for side, values in zip(sides, products):
-            add_tensor(side, values, side[0].center_hot[side[2]])
+            add_tensor(side, values)
         for side in sides:
             clear_windows(side)
 
@@ -559,7 +561,7 @@
         pre = [hidden(side, invariants(side, g)) for side, g in zip(sides, gathered)]
         back = [dot(w_back_ref[...], readout(side, values)) for side, values in zip(sides, pre)]
         for side, values, g in zip(sides, back, gathered):
-            add_tensor(side, unfold(side, values, g), side[0].center_hot[side[2]])
+            add_tensor(side, unfold(side, values, g))
 
     each_block(second_pass)
     tensor_b[...] = (0.125 * (even.tensor[...] + odd.tensor[...])).astype(bf16)
@@ -764,7 +766,7 @@
     pairs = -(-(edges // eb + atoms // span - 1) // 2)
     slot_rows = -(-(2 * pairs * eb // LANES) // 8) * 8
     lift = (1 - 2 * lax.axis_index("gz")).astype(f32).reshape(1)
-    big = 42 * 1024 * 1024
+    big = 44 * 1024 * 1024
 
     shape = jax.ShapeDtypeStruct
     picks = jnp.concatenate([rim, zr], axis=0)
@@ -873,6 +875,7 @@
             pltpu.VMEM((WINDOW + span + LANES, eb), bf16),
             pltpu.VMEM((features, eb), f32),
             pltpu.VMEM((pairs, span, eb), bf16),
+            pltpu.VMEM((pairs, eb, span), bf16),
             pltpu.VMEM((pairs, 2 * LANES, eb), bf16),
             pltpu.VMEM((pairs, features, eb), bf16),
             pltpu.VMEM((pairs, features, eb), bf16),

time: 74.3 us -> 72.8 us (0.980)
  starting transfers between devices: 25.5 us -> 15.9 us
  waiting for transfers between devices: 12 us -> 17.5 us
  Pallas kernels: 30.3 us -> 33.1 us
    ppermute x10, starting transfers between devices: 22.6 us -> 11.3 us  [shifted(): lax.ppermute(x, axis, [((i + step) % count, i) for i in range(count)])]
    ppermute x10, waiting for transfers between devices: 8.09 us -> 14.4 us  [shifted(): lax.ppermute(x, axis, [((i + step) % count, i) for i in range(count)])]
    pallas_call x10, Pallas kernels: 30.3 us -> 33.1 us  [call(): pl.pallas_call(kernel, out_shape=out_shape, in_specs=[scalar] * smem + [v...]
    ppermute x2, starting transfers between devices: 2.92 us -> 4.64 us  [swapped(): return lax.ppermute(x, 'gz', [(i, i ^ 1) for i in range(count)])]
    ppermute x2, waiting for transfers between devices: 3.92 us -> 3.12 us  [swapped(): return lax.ppermute(x, 'gz', [(i, i ^ 1) for i in range(count)])]
where the time goes in v3:
time: 72.8 us; the launch traced here: 72.7 us
  Pallas kernels  33.1 us (45%)
  waiting for transfers between devices  17.5 us (24%)
  starting transfers between devices  15.9 us (22%)
  other arithmetic  3.19 us (4%)
  local copies, waits for them, and re-layouts  1.59 us (2%)
  between operations  1.4 us (2%)
    pallas_call x10, Pallas kernels, call(): pl.pallas_call(kernel, out_shape=out_shape, in_specs=[scalar] * smem + [v...  33.1 us
    ppermute x10, waiting for transfers between devices, shifted(): lax.ppermute(x, axis, [((i + step) % count, i) for i in range(count)])  14.4 us
    ppermute x10, starting transfers between devices, shifted(): lax.ppermute(x, axis, [((i + step) % count, i) for i in range(count)])  11.3 us
    ppermute x2, starting transfers between devices, swapped(): return lax.ppermute(x, 'gz', [(i, i ^ 1) for i in range(count)])  4.64 us
    ppermute x2, waiting for transfers between devices, swapped(): return lax.ppermute(x, 'gz', [(i, i ^ 1) for i in range(count)])  3.12 us
    unnamed x4, local copies, waits for them, and re-layouts  1.59 us
  transfers between devices with their start and end apart: 12, of which 6 were waited for; matrix products, arithmetic and copies ran while one was open for 3% of the time, Pallas kernels for 5%

profile of v3, /device:TPU:0, one launch (start us, length us, event | category | flops | bytes accessed | tf_op | source)
XLA Modules:
  0.0 72.7 jit_solution(5906354790199220259)
XLA Ops:
  0.6 0.7 pad_add_fusion.1.picks_ref
  1.3 0.9 %copy-done = bf16[1,1,1,512,128]{4,3,2,1,0:T(8,128)(2,1)S(1)} copy-done((bf16[1,1,1,512,128]{4,3,2,1,0:T(8,128)(2,1)S(1)}, bf16[1,1,1,512,128]{4,3,2,1,0:T(8,128)(2,1)}, u32[]{:S(2)}) %copy-start) | copy-done | bytes 131096
  2.2 0.7 copy-done.1
  2.9 0.6 shard_map.140
  3.5 3.1 %collective-permute-start = (bf16[144,384]{1,0:T(8,128)(2,1)S(1)}, bf16[144,384]{1,0:T(8,128)(2,1)S(1)}, u32[]{:S(2)}, u32[]{:S(2)}) collective-permute-start(bf16[144,384]{1,0:T(8,128)(2,1)S(1)} %get-tuple-element.52), channel_id=1, source_target_pairs={{6,0},{0,2},{2,4},{4,6},{7,1},{1,3},{3,5},{5,7},{14,8},{8,10},{10,... | collective-permute-start | bytes 331784 | tf_op jit(solution)/shard_map/ppermute | solution.py:728
  6.6 2.1 %collective-permute-start.1 = (bf16[144,384]{1,0:T(8,128)(2,1)S(1)}, bf16[144,384]{1,0:T(8,128)(2,1)S(1)}, u32[]{:S(2)}, u32[]{:S(2)}) collective-permute-start(bf16[144,384]{1,0:T(8,128)(2,1)S(1)} %get-tuple-element.53), channel_id=1, source_target_pairs={{2,0},{4,2},{6,4},{0,6},{3,1},{5,3},{7,5},{1,7},{10,8},{12,10},{14... | collective-permute-start | bytes 331784 | tf_op jit(solution)/shard_map/ppermute | solution.py:728
  8.7 1.7 %collective-permute-start.3 = (bf16[144,384]{1,0:T(8,128)(2,1)S(1)}, bf16[144,384]{1,0:T(8,128)(2,1)S(1)}, u32[]{:S(2)}, u32[]{:S(2)}) collective-permute-start(bf16[144,384]{1,0:T(8,128)(2,1)S(1)} %get-tuple-element.64), channel_id=1, source_target_pairs={{8,0},{16,8},{24,16},{0,24},{9,1},{17,9},{25,17},{1,25},{10,2},{18... | collective-permute-start | bytes 331784 | tf_op jit(solution)/shard_map/ppermute | solution.py:728
  11.1 0.8 %pad_add_fusion.ends_ref = s32[96,128]{1,0:T(8,128)S(1)} fusion(s32[48,128]{1,0:T(8,128)} %bitcast.22, s32[48,128]{1,0:T(8,128)} %bitcast.23), kind=kLoop, calls=%fused_computation.1 | loop fusion | flops 12288 | bytes 98304 | tf_op jit(solution)/shard_map/concatenate | solution.py:784
  11.9 2.5 %shard_map.141 = (s32[56,128]{1,0:T(8,128)S(1)}, s32[56,128]{1,0:T(8,128)S(1)}, s32[4,128]{1,0:T(4,128)S(1)}) custom-call(s32[1]{0:T(128)} %bitcast.16.count_ref, s32[96,128]{1,0:T(8,128)S(1)} %pad_add_fusion.ends_ref), custom_call_target="tpu_custom_call" | custom-call | tf_op jit(solution)/shard_map/pallas_call | solution.py:716
  14.5 1.7 %collective-permute-start.5 = (bf16[144,256]{1,0:T(8,128)(2,1)S(1)}, bf16[144,256]{1,0:T(8,128)(2,1)S(1)}, u32[]{:S(2)}, u32[]{:S(2)}) collective-permute-start(bf16[144,256]{1,0:T(8,128)(2,1)S(1)} %get-tuple-element.67), channel_id=1, source_target_pairs={{8,0},{16,8},{24,16},{0,24},{9,1},{17,9},{25,17},{1,25},{10,2},{18... | collective-permute-start | bytes 221192 | tf_op jit(solution)/shard_map/ppermute | solution.py:728
  16.2 1.0 %pad_maximum_fusion.stacked_ref = bf16[640,256]{1,0:T(8,128)(2,1)S(1)} fusion(bf16[64,256]{1,0:T(8,128)(2,1)} %bitcast.21, bf16[192,256]{1,0:T(8,128)(2,1)} %param.24, bf16[256,256]{1,0:T(8,128)(2,1)} %param.23, bf16[128,256]{1,0:T(8,128)(2,1)} %param.20), kind=kLoop, calls=%fused_computation | loop fusion | flops 1310720 | bytes 655360 | tf_op jit(solution)/shard_map/concatenate | solution.py:827
  17.2 0.7 pad_maximum_fusion.1.small_ref
  18.7 1.7 %collective-permute-start.6 = (bf16[144,128]{1,0:T(8,128)(2,1)S(1)}, bf16[144,128]{1,0:T(8,128)(2,1)S(1)}, u32[]{:S(2)}, u32[]{:S(2)}) collective-permute-start(bf16[144,128]{1,0:T(8,128)(2,1)S(1)} %get-tuple-element.84), channel_id=1, source_target_pairs={{0,1},{1,0},{2,3},{3,2},{4,5},{5,4},{6,7},{7,6},{8,9},{9,8},{10,11... | collective-permute-start | bytes 110600 | tf_op jit(solution)/shard_map/ppermute | solution.py:733
  20.4 0.8 %shard_map.145 = (bf16[256,2560]{1,0:T(8,128)(2,1)S(1)}, f32[6,24,128]{2,1,0:T(8,128)S(1)}) custom-call(bf16[144,2560]{1,0:T(8,128)(2,1)S(1)} %get-tuple-element.80.inner_ref, bf16[256,128]{1,0:T(8,128)(2,1)S(1)} %get-tuple-element.81.w_emb_ref), custom_call_target="tpu_custom_call" | custom-call | tf_op jit(solution)/shard_map/pallas_call | solution.py:716
  21.1 1.6 %collective-permute-done.6.slab_ref = bf16[144,128]{1,0:T(8,128)(2,1)S(1)} collective-permute-done((bf16[144,128]{1,0:T(8,128)(2,1)S(1)}, bf16[144,128]{1,0:T(8,128)(2,1)S(1)}, u32[]{:S(2)}, u32[]{:S(2)}) %collective-permute-start.6) | collective-permute-done | bytes 36896 | tf_op jit(solution)/shard_map/ppermute | solution.py:733
  22.7 27.4 %shard_map.146 = (f32[3,24,128]{2,1,0:T(8,128)S(1)}, f32[3,128]{1,0:T(4,128)S(1)}, f32[1,512]{1,0:T(1,128)}) custom-call(s32[4,128]{1,0:T(4,128)S(1)} %get-tuple-element.57.meta_ref, f32[1]{0:T(128)} %bitcast.7.lift_ref, s32[14,1,512]{2,1,0:T(1,128)S(1)} %bitcast.18, s32[14,1,512]{2,1,0:T(1,128)S(1)} %bitcast.19, ...), custom_call_target="tpu_custom_call" | custom-call | tf_op jit(solution)/shard_map/pallas_call | solution.py:716
  50.1 2.9 %collective-permute-start.7 = (f32[3,128]{1,0:T(4,128)S(1)}, f32[3,128]{1,0:T(4,128)S(1)}, u32[]{:S(2)}, u32[]{:S(2)}) collective-permute-start(f32[3,128]{1,0:T(4,128)S(1)} %get-tuple-element.94), channel_id=1, source_target_pairs={{0,1},{1,0},{2,3},{3,2},{4,5},{5,4},{6,7},{7,6},{8,9},{9,8},{10,11... | collective-permute-start | bytes 4616 | tf_op jit(solution)/shard_map/ppermute | solution.py:733
  53.1 1.6 %collective-permute-done.7.back_ref = f32[3,128]{1,0:T(4,128)S(1)} collective-permute-done((f32[3,128]{1,0:T(4,128)S(1)}, f32[3,128]{1,0:T(4,128)S(1)}, u32[]{:S(2)}, u32[]{:S(2)}) %collective-permute-start.7) | collective-permute-done | bytes 1568 | tf_op jit(solution)/shard_map/ppermute | solution.py:733
  55.4 0.9 %collective-permute-done.8.from_xp_ref = f32[15,128]{1,0:T(8,128)S(1)} collective-permute-done((f32[15,128]{1,0:T(8,128)S(1)}, f32[15,128]{1,0:T(8,128)S(1)}, u32[]{:S(2)}, u32[]{:S(2)}) %collective-permute-start.8) | collective-permute-done | bytes 7712 | tf_op jit(solution)/shard_map/ppermute | solution.py:728
  56.2 10.0 %collective-permute-done.9.from_xm_ref = f32[15,128]{1,0:T(8,128)S(1)} collective-permute-done((f32[15,128]{1,0:T(8,128)S(1)}, f32[15,128]{1,0:T(8,128)S(1)}, u32[]{:S(2)}, u32[]{:S(2)}) %collective-permute-start.9) | collective-permute-done | bytes 7712 | tf_op jit(solution)/shard_map/ppermute | solution.py:728
  66.3 2.0 %collective-permute-start.11 = (f32[9,128]{1,0:T(8,128)S(1)}, f32[9,128]{1,0:T(8,128)S(1)}, u32[]{:S(2)}, u32[]{:S(2)}) collective-permute-start(f32[9,128]{1,0:T(8,128)S(1)} %get-tuple-element.101), channel_id=1, source_target_pairs={{6,0},{0,2},{2,4},{4,6},{7,1},{1,3},{3,5},{5,7},{14,8},{8,10},{10,... | collective-permute-start | bytes 13832 | tf_op jit(solution)/shard_map/ppermute | solution.py:728
  68.3 1.6 %collective-permute-done.10.from_yp_ref = f32[9,128]{1,0:T(8,128)S(1)} collective-permute-done((f32[9,128]{1,0:T(8,128)S(1)}, f32[9,128]{1,0:T(8,128)S(1)}, u32[]{:S(2)}, u32[]{:S(2)}) %collective-permute-start.10) | collective-permute-done | bytes 4640 | tf_op jit(solution)/shard_map/ppermute | solution.py:728
  69.9 1.9 %collective-permute-done.11.from_ym_ref = f32[9,128]{1,0:T(8,128)S(1)} collective-permute-done((f32[9,128]{1,0:T(8,128)S(1)}, f32[9,128]{1,0:T(8,128)S(1)}, u32[]{:S(2)}, u32[]{:S(2)}) %collective-permute-start.11) | collective-permute-done | bytes 4640 | tf_op jit(solution)/shard_map/ppermute | solution.py:728
  71.8 0.9 %shard_map.149 = f32[3,1,512]{2,1,0:T(1,128)} custom-call(f32[3,8,128]{2,1,0:T(8,128)S(1)} %get-tuple-element.95.own_ref, s32[9,128]{1,0:T(8,128)S(1)} %pad_add_fusion.1.picks_ref, f32[15,128]{1,0:T(8,128)S(1)} %collective-permute-done.8.from_xp_ref, f32[15,128]{1,0:T(8,128)S(1)} %collective-permute-done.9.from_xm_ref, ...), custom_call_target="tpu_custom_call" | custom-call | tf_op jit(solution)/shard_map/pallas_call | solution.py:716
  (18 shorter events, 1.6 us)
Async XLA Ops:
  1.3 0.9 %copy-start = (bf16[1,1,1,512,128]{4,3,2,1,0:T(8,128)(2,1)S(1)}, bf16[1,1,1,512,128]{4,3,2,1,0:T(8,128)(2,1)}, u32[]{:S(2)}) copy-start(bf16[1,1,1,512,128]{4,3,2,1,0:T(8,128)(2,1)} %param.14) | copy-start | bytes 393220
  2.2 0.7 copy-start.1
  3.5 10.8 %collective-permute-start = (bf16[144,384]{1,0:T(8,128)(2,1)S(1)}, bf16[144,384]{1,0:T(8,128)(2,1)S(1)}, u32[]{:S(2)}, u32[]{:S(2)}) collective-permute-start(bf16[144,384]{1,0:T(8,128)(2,1)S(1)} %get-tuple-element.52), channel_id=1, source_target_pairs={{6,0},{0,2},{2,4},{4,6},{7,1},{1,3},{3,5},{5,7},{14,8},{8,10},{10,... | collective-permute-start | bytes 331784 | tf_op jit(solution)/shard_map/ppermute | solution.py:728
  6.6 7.7 %collective-permute-start.1 = (bf16[144,384]{1,0:T(8,128)(2,1)S(1)}, bf16[144,384]{1,0:T(8,128)(2,1)S(1)}, u32[]{:S(2)}, u32[]{:S(2)}) collective-permute-start(bf16[144,384]{1,0:T(8,128)(2,1)S(1)} %get-tuple-element.53), channel_id=1, source_target_pairs={{2,0},{4,2},{6,4},{0,6},{3,1},{5,3},{7,5},{1,7},{10,8},{12,10},{14... | collective-permute-start | bytes 331784 | tf_op jit(solution)/shard_map/ppermute | solution.py:728
  8.7 9.6 %collective-permute-start.2 = (bf16[144,384]{1,0:T(8,128)(2,1)S(1)}, bf16[144,384]{1,0:T(8,128)(2,1)S(1)}, u32[]{:S(2)}, u32[]{:S(2)}) collective-permute-start(bf16[144,384]{1,0:T(8,128)(2,1)S(1)} %get-tuple-element.63), channel_id=1, source_target_pairs={{24,0},{0,8},{8,16},{16,24},{25,1},{1,9},{9,17},{17,25},{26,2},{2,... | collective-permute-start | bytes 331784 | tf_op jit(solution)/shard_map/ppermute | solution.py:728
  8.7 9.6 %collective-permute-start.3 = (bf16[144,384]{1,0:T(8,128)(2,1)S(1)}, bf16[144,384]{1,0:T(8,128)(2,1)S(1)}, u32[]{:S(2)}, u32[]{:S(2)}) collective-permute-start(bf16[144,384]{1,0:T(8,128)(2,1)S(1)} %get-tuple-element.64), channel_id=1, source_target_pairs={{8,0},{16,8},{24,16},{0,24},{9,1},{17,9},{25,17},{1,25},{10,2},{18... | collective-permute-start | bytes 331784 | tf_op jit(solution)/shard_map/ppermute | solution.py:728
  14.4 3.8 %collective-permute-start.4 = (bf16[144,256]{1,0:T(8,128)(2,1)S(1)}, bf16[144,256]{1,0:T(8,128)(2,1)S(1)}, u32[]{:S(2)}, u32[]{:S(2)}) collective-permute-start(bf16[144,256]{1,0:T(8,128)(2,1)S(1)} %get-tuple-element.66), channel_id=1, source_target_pairs={{24,0},{0,8},{8,16},{16,24},{25,1},{1,9},{9,17},{17,25},{26,2},{2,... | collective-permute-start | bytes 221192 | tf_op jit(solution)/shard_map/ppermute | solution.py:728
  14.5 3.8 %collective-permute-start.5 = (bf16[144,256]{1,0:T(8,128)(2,1)S(1)}, bf16[144,256]{1,0:T(8,128)(2,1)S(1)}, u32[]{:S(2)}, u32[]{:S(2)}) collective-permute-start(bf16[144,256]{1,0:T(8,128)(2,1)S(1)} %get-tuple-element.67), channel_id=1, source_target_pairs={{8,0},{16,8},{24,16},{0,24},{9,1},{17,9},{25,17},{1,25},{10,2},{18... | collective-permute-start | bytes 221192 | tf_op jit(solution)/shard_map/ppermute | solution.py:728
  18.7 4.0 %collective-permute-start.6 = (bf16[144,128]{1,0:T(8,128)(2,1)S(1)}, bf16[144,128]{1,0:T(8,128)(2,1)S(1)}, u32[]{:S(2)}, u32[]{:S(2)}) collective-permute-start(bf16[144,128]{1,0:T(8,128)(2,1)S(1)} %get-tuple-element.84), channel_id=1, source_target_pairs={{0,1},{1,0},{2,3},{3,2},{4,5},{5,4},{6,7},{7,6},{8,9},{9,8},{10,11... | collective-permute-start | bytes 110600 | tf_op jit(solution)/shard_map/ppermute | solution.py:733
  50.1 4.5 %collective-permute-start.7 = (f32[3,128]{1,0:T(4,128)S(1)}, f32[3,128]{1,0:T(4,128)S(1)}, u32[]{:S(2)}, u32[]{:S(2)}) collective-permute-start(f32[3,128]{1,0:T(4,128)S(1)} %get-tuple-element.94), channel_id=1, source_target_pairs={{0,1},{1,0},{2,3},{3,2},{4,5},{5,4},{6,7},{7,6},{8,9},{9,8},{10,11... | collective-permute-start | bytes 4616 | tf_op jit(solution)/shard_map/ppermute | solution.py:733
  54.8 1.4 %collective-permute-start.8 = (f32[15,128]{1,0:T(8,128)S(1)}, f32[15,128]{1,0:T(8,128)S(1)}, u32[]{:S(2)}, u32[]{:S(2)}) collective-permute-start(f32[15,128]{1,0:T(8,128)S(1)} %get-tuple-element.96), channel_id=1, source_target_pairs={{8,0},{16,8},{24,16},{0,24},{9,1},{17,9},{25,17},{1,25},{10,2},{18... | collective-permute-start | bytes 23048 | tf_op jit(solution)/shard_map/ppermute | solution.py:728
  54.9 11.4 %collective-permute-start.9 = (f32[15,128]{1,0:T(8,128)S(1)}, f32[15,128]{1,0:T(8,128)S(1)}, u32[]{:S(2)}, u32[]{:S(2)}) collective-permute-start(f32[15,128]{1,0:T(8,128)S(1)} %get-tuple-element.97), channel_id=1, source_target_pairs={{24,0},{0,8},{8,16},{16,24},{25,1},{1,9},{9,17},{17,25},{26,2},{2,... | collective-permute-start | bytes 23048 | tf_op jit(solution)/shard_map/ppermute | solution.py:728
  66.2 3.7 %collective-permute-start.10 = (f32[9,128]{1,0:T(8,128)S(1)}, f32[9,128]{1,0:T(8,128)S(1)}, u32[]{:S(2)}, u32[]{:S(2)}) collective-permute-start(f32[9,128]{1,0:T(8,128)S(1)} %get-tuple-element.100), channel_id=1, source_target_pairs={{2,0},{4,2},{6,4},{0,6},{3,1},{5,3},{7,5},{1,7},{10,8},{12,10},{14... | collective-permute-start | bytes 13832 | tf_op jit(solution)/shard_map/ppermute | solution.py:728
  66.3 5.5 %collective-permute-start.11 = (f32[9,128]{1,0:T(8,128)S(1)}, f32[9,128]{1,0:T(8,128)S(1)}, u32[]{:S(2)}, u32[]{:S(2)}) collective-permute-start(f32[9,128]{1,0:T(8,128)S(1)} %get-tuple-element.101), channel_id=1, source_target_pairs={{6,0},{0,2},{2,4},{4,6},{7,1},{1,3},{3,5},{5,7},{14,8},{8,10},{10,... | collective-permute-start | bytes 13832 | tf_op jit(solution)/shard_map/ppermute | solution.py:728

commit v4 on v2

--- a/solution.py
+++ b/solution.py
@@ -12,6 +12,8 @@
 LANES = 128
 PARTS = 16
 BLOCK = 512
+SETS = 4
+SUMS = 2
 WINDOW = 768
 ROOT3 = 3.0**0.5
 BANDS = (0, 1, 1, 1, 2, 2, 2, 2, 2)
@@ -310,8 +312,12 @@
     tensor_b,
     *scratch,
 ):
-    names = len(scratch) // 2
-    even, odd = (Scratch(*scratch[side * names : (side + 1) * names]) for side in range(2))
+    names = len(FIELDS) - 2
+    sums = [scratch[names * SETS + index :: SUMS] for index in range(SUMS)]
+    sets = [
+        Scratch(*scratch[index * names : (index + 1) * names], *sums[index % SUMS])
+        for index in range(SETS)
+    ]
     eb = centers_ref.shape[2]
     width = w_emb_ref.shape[1]
     features = feat_in_ref.shape[0]
@@ -324,7 +330,7 @@
     hpad = place_in_ref.shape[1]
     first_blocks = meta_ref[0, 0]
     total_blocks = meta_ref[1, 0]
-    pairs = total_blocks // 2
+    rounds = total_blocks // SETS
 
     feat[:, 0:inner_len] = feat_in_ref[...]
     raw = dot(w_emb_ref[...], slab_ref[0:width, :])
@@ -343,7 +349,7 @@
     place_b[...] = jnp.zeros_like(place_b)
     place_b[0 : 6 * hpad, 0:LANES] = place[...].reshape(6 * hpad, LANES).astype(bf16)
     place_b[6 * hpad :, LANES:] = place[:, 0:8, :].reshape(48, LANES).astype(bf16)
-    for own in (even, odd):
+    for own in sets:
         own.hot[WINDOW + span + 32 :, :] = jnp.zeros((LANES - 32, eb), bf16)
         for ref in (own.extra, own.tensor, own.acc):
             ref[...] = jnp.zeros_like(ref)
@@ -352,15 +358,27 @@
         return jnp.where(b >= first_blocks, 1, 0)
 
     def each_block(run):
-        def step(pair, carry):
-            run([(even, 2 * pair, pair), (odd, 2 * pair + 1, pair)])
+        def sides(at, picked):
+            return [(sets[index], SETS * at + index, at) for index in picked]
+
+        def step(at, carry):
+            run(sides(at, range(SETS)))
             return carry
 
-        lax.fori_loop(0, pairs, step, 0)
-
-        @pl.when(total_blocks > 2 * pairs)
+        lax.fori_loop(0, rounds, step, 0)
+        rest = total_blocks - SETS * rounds
+
+        @pl.when(rest == 1)
         def _():
-            run([(even, 2 * pairs, pairs)])
+            run(sides(rounds, [0]))
+
+        @pl.when(rest > 1)
+        def _():
+            run(sides(rounds, [0, 1]))
+
+        @pl.when(rest == 3)
+        def _():
+            run(sides(rounds, [2]))
 
     def locate(sides):
         for own_s, b, at in sides:
@@ -391,7 +409,7 @@
             own_s.geo[6, row, :] = jnp.where(slot_c >= 0, 1.0, 0.0)
 
     each_block(locate)
-    for own in (even, odd):
+    for own in sets:
         rx, ry, rz = own.geo[0], own.geo[1], own.geo[2]
         squared = rx * rx + ry * ry + rz * rz
         inv_d = lax.rsqrt(squared + 0.25)
@@ -509,8 +527,8 @@
             clear_windows(side)
 
     each_block(first_pass)
-    tensor_b[...] = (0.125 * (even.tensor[...] + odd.tensor[...])).astype(bf16)
-    for own in (even, odd):
+    tensor_b[...] = (0.125 * sum(own.tensor[...] for own in sets[:SUMS])).astype(bf16)
+    for own in sets[:SUMS]:
         own.tensor[...] = jnp.zeros_like(own.tensor)
 
     def invariants(side, gathered):
@@ -562,7 +580,7 @@
             add_tensor(side, unfold(side, values, g), side[0].center_hot[side[2]])
 
     each_block(second_pass)
-    tensor_b[...] = (0.125 * (even.tensor[...] + odd.tensor[...])).astype(bf16)
+    tensor_b[...] = (0.125 * sum(own.tensor[...] for own in sets[:SUMS])).astype(bf16)
 
     def channels_back(side, gathered):
         own_s, _, at = side
@@ -594,7 +612,7 @@
 
     each_block(third_pass)
 
-    for own in (even, odd):
+    for own in sets:
         x, y, z = own.geo[8], own.geo[9], own.geo[10]
         inv_d, dist, env = own.geo[3], own.geo[4], own.geo[5]
         live, squared = own.geo[6], own.geo[7]
@@ -630,7 +648,7 @@
             own_s.acc[half_of(b)] += dot_t(rows, own_s.lows[at])
 
     each_block(collect)
-    acc = [even.acc[half] + odd.acc[half] for half in range(halves_n)]
+    acc = [sum(own.acc[half] for own in sets[:SUMS]) for half in range(halves_n)]
     sum_o = sum(value[0 : 6 * hpad, 0:LANES] for value in acc)
     sum_o = sum_o[0 : 3 * hpad] + sum_o[3 * hpad :]
     for d in range(3):
@@ -761,10 +779,11 @@
     hpad = -(-(table // LANES) // 8) * 8
     eb = BLOCK
     span = 2 * LANES
-    pairs = -(-(edges // eb + atoms // span - 1) // 2)
-    slot_rows = -(-(2 * pairs * eb // LANES) // 8) * 8
+    blocks = edges // eb + atoms // span - 1
+    depth = -(-blocks // SETS)
+    slot_rows = -(-(blocks * eb // LANES) // 8) * 8
     lift = (1 - 2 * lax.axis_index("gz")).astype(f32).reshape(1)
-    big = 42 * 1024 * 1024
+    big = 47 * 1024 * 1024
 
     shape = jax.ShapeDtypeStruct
     picks = jnp.concatenate([rim, zr], axis=0)
@@ -872,19 +891,25 @@
         + [
             pltpu.VMEM((WINDOW + span + LANES, eb), bf16),
             pltpu.VMEM((features, eb), f32),
-            pltpu.VMEM((pairs, span, eb), bf16),
-            pltpu.VMEM((pairs, 2 * LANES, eb), bf16),
-            pltpu.VMEM((pairs, features, eb), bf16),
-            pltpu.VMEM((pairs, features, eb), bf16),
-            pltpu.VMEM((pairs, chans, eb), f32),
-            pltpu.VMEM((16, -(-pairs // 8) * 8, eb), f32),
-            pltpu.VMEM((11, -(-pairs // 8) * 8, eb), f32),
-            pltpu.VMEM((pairs, features, eb), bf16),
-            pltpu.VMEM((pairs, 64, eb), f32),
+            pltpu.VMEM((depth, span, eb), bf16),
+            pltpu.VMEM((depth, 2 * LANES, eb), bf16),
+            pltpu.VMEM((depth, features, eb), bf16),
+            pltpu.VMEM((depth, features, eb), bf16),
+            pltpu.VMEM((depth, chans, eb), f32),
+            pltpu.VMEM((16, -(-depth // 8) * 8, eb), f32),
+            pltpu.VMEM((11, -(-depth // 8) * 8, eb), f32),
+            pltpu.VMEM((depth, features, eb), bf16),
+            pltpu.VMEM((depth, 64, eb), f32),
+        ]
+        * SETS
+        + [
             pltpu.VMEM((atoms // span, 9 * chans, span), f32),
+        ]
+        * SUMS
+        + [
             pltpu.VMEM((atoms // span, 6 * hpad + 8 * (span // LANES), 2 * LANES), f32),
         ]
-        * 2,
+        * SUMS,
         smem=2,
         limit=big,
     )

time: 74.3 us -> 67.3 us (0.906)
  Pallas kernels: 30.3 us -> 19.7 us
  starting transfers between devices: 25.5 us -> 33.1 us
  waiting for transfers between devices: 12 us -> 8.8 us
    pallas_call x10, Pallas kernels: 30.3 us -> 19.7 us  [call(): pl.pallas_call(kernel, out_shape=out_shape, in_specs=[scalar] * smem + [v...]
    ppermute x2, starting transfers between devices: 2.92 us -> 8.15 us  [swapped(): return lax.ppermute(x, 'gz', [(i, i ^ 1) for i in range(count)])]
    ppermute x10, waiting for transfers between devices: 8.09 us -> 5.69 us  [shifted(): lax.ppermute(x, axis, [((i + step) % count, i) for i in range(count)])]
    ppermute x10, starting transfers between devices: 22.6 us -> 24.9 us  [shifted(): lax.ppermute(x, axis, [((i + step) % count, i) for i in range(count)])]
    ppermute x2, waiting for transfers between devices: 3.92 us -> 3.11 us  [swapped(): return lax.ppermute(x, 'gz', [(i, i ^ 1) for i in range(count)])]
  transfers between devices with their start and end apart: 12 -> 12, of which waited for: 6 -> 6; matrix products, arithmetic and copies ran while one was open for 3% -> 4% of each run, Pallas kernels for 5% -> 5%
where the time goes in v4:
time: 67.3 us; the launch traced here: 67.8 us
  starting transfers between devices  33.1 us (49%)
  Pallas kernels  19.7 us (29%)
  waiting for transfers between devices  8.8 us (13%)
  other arithmetic  3.19 us (5%)
  local copies, waits for them, and re-layouts  1.59 us (2%)
  between operations  1.39 us (2%)
    ppermute x10, starting transfers between devices, shifted(): lax.ppermute(x, axis, [((i + step) % count, i) for i in range(count)])  24.9 us
    pallas_call x10, Pallas kernels, call(): pl.pallas_call(kernel, out_shape=out_shape, in_specs=[scalar] * smem + [v...  19.7 us
    ppermute x2, starting transfers between devices, swapped(): return lax.ppermute(x, 'gz', [(i, i ^ 1) for i in range(count)])  8.15 us
    ppermute x10, waiting for transfers between devices, shifted(): lax.ppermute(x, axis, [((i + step) % count, i) for i in range(count)])  5.69 us
    ppermute x2, waiting for transfers between devices, swapped(): return lax.ppermute(x, 'gz', [(i, i ^ 1) for i in range(count)])  3.11 us
    unnamed x4, local copies, waits for them, and re-layouts  1.59 us
  transfers between devices with their start and end apart: 12, of which 6 were waited for; matrix products, arithmetic and copies ran while one was open for 4% of the time, Pallas kernels for 5%

profile of v4, /device:TPU:0, one launch (start us, length us, event | category | flops | bytes accessed | tf_op | source)
XLA Modules:
  0.0 67.8 jit_solution(13224446277731139763)
XLA Ops:
  0.6 0.7 %pad_add_fusion.1.picks_ref = s32[9,128]{1,0:T(8,128)S(1)} fusion(s32[1,128]{1,0:T(1,128)} %bitcast.27, s32[8,128]{1,0:T(8,128)} %bitcast.25), kind=kLoop, calls=%fused_computation.3 | loop fusion | flops 1152 | bytes 9216 | tf_op jit(solution)/shard_map/concatenate | solution.py:789
  1.3 0.9 %copy-done = bf16[1,1,1,512,128]{4,3,2,1,0:T(8,128)(2,1)S(1)} copy-done((bf16[1,1,1,512,128]{4,3,2,1,0:T(8,128)(2,1)S(1)}, bf16[1,1,1,512,128]{4,3,2,1,0:T(8,128)(2,1)}, u32[]{:S(2)}) %copy-start) | copy-done | bytes 131096
  2.2 0.7 %copy-done.1 = f32[1,1,1,3,512]{4,2,3,1,0:T(1,128)S(1)} copy-done((f32[1,1,1,3,512]{4,2,3,1,0:T(1,128)S(1)}, f32[1,1,1,3,512]{4,2,3,1,0:T(1,128)}, u32[]{:S(2)}) %copy-start.1) | copy-done | bytes 6168
  3.5 3.1 %collective-permute-start = (bf16[144,384]{1,0:T(8,128)(2,1)S(1)}, bf16[144,384]{1,0:T(8,128)(2,1)S(1)}, u32[]{:S(2)}, u32[]{:S(2)}) collective-permute-start(bf16[144,384]{1,0:T(8,128)(2,1)S(1)} %get-tuple-element.52), channel_id=1, source_target_pairs={{6,0},{0,2},{2,4},{4,6},{7,1},{1,3},{3,5},{5,7},{14,8},{8,10},{10,... | collective-permute-start | bytes 331784 | tf_op jit(solution)/shard_map/ppermute | solution.py:744
  6.6 2.1 %collective-permute-start.1 = (bf16[144,384]{1,0:T(8,128)(2,1)S(1)}, bf16[144,384]{1,0:T(8,128)(2,1)S(1)}, u32[]{:S(2)}, u32[]{:S(2)}) collective-permute-start(bf16[144,384]{1,0:T(8,128)(2,1)S(1)} %get-tuple-element.53), channel_id=1, source_target_pairs={{2,0},{4,2},{6,4},{0,6},{3,1},{5,3},{7,5},{1,7},{10,8},{12,10},{14... | collective-permute-start | bytes 331784 | tf_op jit(solution)/shard_map/ppermute | solution.py:744
  8.7 1.7 %collective-permute-start.3 = (bf16[144,384]{1,0:T(8,128)(2,1)S(1)}, bf16[144,384]{1,0:T(8,128)(2,1)S(1)}, u32[]{:S(2)}, u32[]{:S(2)}) collective-permute-start(bf16[144,384]{1,0:T(8,128)(2,1)S(1)} %get-tuple-element.64), channel_id=1, source_target_pairs={{8,0},{16,8},{24,16},{0,24},{9,1},{17,9},{25,17},{1,25},{10,2},{18... | collective-permute-start | bytes 331784 | tf_op jit(solution)/shard_map/ppermute | solution.py:744
  11.1 0.8 %pad_add_fusion.ends_ref = s32[96,128]{1,0:T(8,128)S(1)} fusion(s32[48,128]{1,0:T(8,128)} %bitcast.22, s32[48,128]{1,0:T(8,128)} %bitcast.23), kind=kLoop, calls=%fused_computation.1 | loop fusion | flops 12288 | bytes 98304 | tf_op jit(solution)/shard_map/concatenate | solution.py:801
  11.9 2.5 %shard_map.141 = (s32[56,128]{1,0:T(8,128)S(1)}, s32[56,128]{1,0:T(8,128)S(1)}, s32[4,128]{1,0:T(4,128)S(1)}) custom-call(s32[1]{0:T(128)} %bitcast.16.count_ref, s32[96,128]{1,0:T(8,128)S(1)} %pad_add_fusion.ends_ref), custom_call_target="tpu_custom_call" | custom-call | tf_op jit(solution)/shard_map/pallas_call | solution.py:732
  14.5 1.7 %collective-permute-start.5 = (bf16[144,256]{1,0:T(8,128)(2,1)S(1)}, bf16[144,256]{1,0:T(8,128)(2,1)S(1)}, u32[]{:S(2)}, u32[]{:S(2)}) collective-permute-start(bf16[144,256]{1,0:T(8,128)(2,1)S(1)} %get-tuple-element.67), channel_id=1, source_target_pairs={{8,0},{16,8},{24,16},{0,24},{9,1},{17,9},{25,17},{1,25},{10,2},{18... | collective-permute-start | bytes 221192 | tf_op jit(solution)/shard_map/ppermute | solution.py:744
  16.2 1.0 %pad_maximum_fusion.stacked_ref = bf16[640,256]{1,0:T(8,128)(2,1)S(1)} fusion(bf16[64,256]{1,0:T(8,128)(2,1)} %bitcast.21, bf16[192,256]{1,0:T(8,128)(2,1)} %param.24, bf16[256,256]{1,0:T(8,128)(2,1)} %param.23, bf16[128,256]{1,0:T(8,128)(2,1)} %param.20), kind=kLoop, calls=%fused_computation | loop fusion | flops 1310720 | bytes 655360 | tf_op jit(solution)/shard_map/concatenate | solution.py:844
  17.2 0.7 %pad_maximum_fusion.1.small_ref = f32[9,256]{1,0:T(8,128)S(1)} fusion(f32[1,256]{1,0:T(1,128)} %bitcast.26, f32[8,256]{1,0:T(8,128)} %param.21), kind=kLoop, calls=%fused_computation.2 | loop fusion | flops 2304 | bytes 18432 | tf_op jit(solution)/shard_map/concatenate | solution.py:845
  18.7 1.7 %collective-permute-start.6 = (bf16[144,128]{1,0:T(8,128)(2,1)S(1)}, bf16[144,128]{1,0:T(8,128)(2,1)S(1)}, u32[]{:S(2)}, u32[]{:S(2)}) collective-permute-start(bf16[144,128]{1,0:T(8,128)(2,1)S(1)} %get-tuple-element.84), channel_id=1, source_target_pairs={{0,1},{1,0},{2,3},{3,2},{4,5},{5,4},{6,7},{7,6},{8,9},{9,8},{10,11... | collective-permute-start | bytes 110600 | tf_op jit(solution)/shard_map/ppermute | solution.py:749
  20.4 0.7 %shard_map.145 = (bf16[256,2560]{1,0:T(8,128)(2,1)S(1)}, f32[6,24,128]{2,1,0:T(8,128)S(1)}) custom-call(bf16[144,2560]{1,0:T(8,128)(2,1)S(1)} %get-tuple-element.80.inner_ref, bf16[256,128]{1,0:T(8,128)(2,1)S(1)} %get-tuple-element.81.w_emb_ref), custom_call_target="tpu_custom_call" | custom-call | tf_op jit(solution)/shard_map/pallas_call | solution.py:732
  21.1 1.5 %collective-permute-done.6.slab_ref = bf16[144,128]{1,0:T(8,128)(2,1)S(1)} collective-permute-done((bf16[144,128]{1,0:T(8,128)(2,1)S(1)}, bf16[144,128]{1,0:T(8,128)(2,1)S(1)}, u32[]{:S(2)}, u32[]{:S(2)}) %collective-permute-start.6) | collective-permute-done | bytes 36896 | tf_op jit(solution)/shard_map/ppermute | solution.py:749
  22.7 14.1 %shard_map.146 = (f32[3,24,128]{2,1,0:T(8,128)S(1)}, f32[3,128]{1,0:T(4,128)S(1)}, f32[1,512]{1,0:T(1,128)}) custom-call(s32[4,128]{1,0:T(4,128)S(1)} %get-tuple-element.57.meta_ref, f32[1]{0:T(128)} %bitcast.7.lift_ref, s32[14,1,512]{2,1,0:T(1,128)S(1)} %bitcast.18, s32[14,1,512]{2,1,0:T(1,128)S(1)} %bitcast.19, ...), custom_call_target="tpu_custom_call" | custom-call | tf_op jit(solution)/shard_map/pallas_call | solution.py:732
  36.8 6.4 %collective-permute-start.7 = (f32[3,128]{1,0:T(4,128)S(1)}, f32[3,128]{1,0:T(4,128)S(1)}, u32[]{:S(2)}, u32[]{:S(2)}) collective-permute-start(f32[3,128]{1,0:T(4,128)S(1)} %get-tuple-element.94), channel_id=1, source_target_pairs={{0,1},{1,0},{2,3},{3,2},{4,5},{5,4},{6,7},{7,6},{8,9},{9,8},{10,11... | collective-permute-start | bytes 4616 | tf_op jit(solution)/shard_map/ppermute | solution.py:749
  43.2 1.6 %collective-permute-done.7.back_ref = f32[3,128]{1,0:T(4,128)S(1)} collective-permute-done((f32[3,128]{1,0:T(4,128)S(1)}, f32[3,128]{1,0:T(4,128)S(1)}, u32[]{:S(2)}, u32[]{:S(2)}) %collective-permute-start.7) | collective-permute-done | bytes 1568 | tf_op jit(solution)/shard_map/ppermute | solution.py:749
  45.0 3.6 %collective-permute-start.8 = (f32[15,128]{1,0:T(8,128)S(1)}, f32[15,128]{1,0:T(8,128)S(1)}, u32[]{:S(2)}, u32[]{:S(2)}) collective-permute-start(f32[15,128]{1,0:T(8,128)S(1)} %get-tuple-element.96), channel_id=1, source_target_pairs={{8,0},{16,8},{24,16},{0,24},{9,1},{17,9},{25,17},{1,25},{10,2},{18... | collective-permute-start | bytes 23048 | tf_op jit(solution)/shard_map/ppermute | solution.py:744
  48.6 10.5 %collective-permute-start.9 = (f32[15,128]{1,0:T(8,128)S(1)}, f32[15,128]{1,0:T(8,128)S(1)}, u32[]{:S(2)}, u32[]{:S(2)}) collective-permute-start(f32[15,128]{1,0:T(8,128)S(1)} %get-tuple-element.97), channel_id=1, source_target_pairs={{24,0},{0,8},{8,16},{16,24},{25,1},{1,9},{9,17},{17,25},{26,2},{2,... | collective-permute-start | bytes 23048 | tf_op jit(solution)/shard_map/ppermute | solution.py:744
  60.0 1.3 %collective-permute-start.10 = (f32[9,128]{1,0:T(8,128)S(1)}, f32[9,128]{1,0:T(8,128)S(1)}, u32[]{:S(2)}, u32[]{:S(2)}) collective-permute-start(f32[9,128]{1,0:T(8,128)S(1)} %get-tuple-element.100), channel_id=1, source_target_pairs={{2,0},{4,2},{6,4},{0,6},{3,1},{5,3},{7,5},{1,7},{10,8},{12,10},{14... | collective-permute-start | bytes 13832 | tf_op jit(solution)/shard_map/ppermute | solution.py:744
  61.3 0.7 %collective-permute-start.11 = (f32[9,128]{1,0:T(8,128)S(1)}, f32[9,128]{1,0:T(8,128)S(1)}, u32[]{:S(2)}, u32[]{:S(2)}) collective-permute-start(f32[9,128]{1,0:T(8,128)S(1)} %get-tuple-element.101), channel_id=1, source_target_pairs={{6,0},{0,2},{2,4},{4,6},{7,1},{1,3},{3,5},{5,7},{14,8},{8,10},{10,... | collective-permute-start | bytes 13832 | tf_op jit(solution)/shard_map/ppermute | solution.py:744
  62.0 1.6 %collective-permute-done.10.from_yp_ref = f32[9,128]{1,0:T(8,128)S(1)} collective-permute-done((f32[9,128]{1,0:T(8,128)S(1)}, f32[9,128]{1,0:T(8,128)S(1)}, u32[]{:S(2)}, u32[]{:S(2)}) %collective-permute-start.10) | collective-permute-done | bytes 4640 | tf_op jit(solution)/shard_map/ppermute | solution.py:744
  63.7 3.2 %collective-permute-done.11.from_ym_ref = f32[9,128]{1,0:T(8,128)S(1)} collective-permute-done((f32[9,128]{1,0:T(8,128)S(1)}, f32[9,128]{1,0:T(8,128)S(1)}, u32[]{:S(2)}, u32[]{:S(2)}) %collective-permute-start.11) | collective-permute-done | bytes 4640 | tf_op jit(solution)/shard_map/ppermute | solution.py:744
  66.9 0.9 %shard_map.149 = f32[3,1,512]{2,1,0:T(1,128)} custom-call(f32[3,8,128]{2,1,0:T(8,128)S(1)} %get-tuple-element.95.own_ref, s32[9,128]{1,0:T(8,128)S(1)} %pad_add_fusion.1.picks_ref, f32[15,128]{1,0:T(8,128)S(1)} %collective-permute-done.8.from_xp_ref, f32[15,128]{1,0:T(8,128)S(1)} %collective-permute-done.9.from_xm_ref, ...), custom_call_target="tpu_custom_call" | custom-call | tf_op jit(solution)/shard_map/pallas_call | solution.py:732
  (18 shorter events, 2.5 us)
Async XLA Ops:
  1.3 0.9 %copy-start = (bf16[1,1,1,512,128]{4,3,2,1,0:T(8,128)(2,1)S(1)}, bf16[1,1,1,512,128]{4,3,2,1,0:T(8,128)(2,1)}, u32[]{:S(2)}) copy-start(bf16[1,1,1,512,128]{4,3,2,1,0:T(8,128)(2,1)} %param.14) | copy-start | bytes 393220
  2.2 0.7 %copy-start.1 = (f32[1,1,1,3,512]{4,2,3,1,0:T(1,128)S(1)}, f32[1,1,1,3,512]{4,2,3,1,0:T(1,128)}, u32[]{:S(2)}) copy-start(f32[1,1,1,3,512]{4,2,3,1,0:T(1,128)} %param.13) | copy-start | bytes 18436
  3.5 10.8 %collective-permute-start = (bf16[144,384]{1,0:T(8,128)(2,1)S(1)}, bf16[144,384]{1,0:T(8,128)(2,1)S(1)}, u32[]{:S(2)}, u32[]{:S(2)}) collective-permute-start(bf16[144,384]{1,0:T(8,128)(2,1)S(1)} %get-tuple-element.52), channel_id=1, source_target_pairs={{6,0},{0,2},{2,4},{4,6},{7,1},{1,3},{3,5},{5,7},{14,8},{8,10},{10,... | collective-permute-start | bytes 331784 | tf_op jit(solution)/shard_map/ppermute | solution.py:744
  6.6 7.7 %collective-permute-start.1 = (bf16[144,384]{1,0:T(8,128)(2,1)S(1)}, bf16[144,384]{1,0:T(8,128)(2,1)S(1)}, u32[]{:S(2)}, u32[]{:S(2)}) collective-permute-start(bf16[144,384]{1,0:T(8,128)(2,1)S(1)} %get-tuple-element.53), channel_id=1, source_target_pairs={{2,0},{4,2},{6,4},{0,6},{3,1},{5,3},{7,5},{1,7},{10,8},{12,10},{14... | collective-permute-start | bytes 331784 | tf_op jit(solution)/shard_map/ppermute | solution.py:744
  8.7 9.6 %collective-permute-start.2 = (bf16[144,384]{1,0:T(8,128)(2,1)S(1)}, bf16[144,384]{1,0:T(8,128)(2,1)S(1)}, u32[]{:S(2)}, u32[]{:S(2)}) collective-permute-start(bf16[144,384]{1,0:T(8,128)(2,1)S(1)} %get-tuple-element.63), channel_id=1, source_target_pairs={{24,0},{0,8},{8,16},{16,24},{25,1},{1,9},{9,17},{17,25},{26,2},{2,... | collective-permute-start | bytes 331784 | tf_op jit(solution)/shard_map/ppermute | solution.py:744
  8.7 9.6 %collective-permute-start.3 = (bf16[144,384]{1,0:T(8,128)(2,1)S(1)}, bf16[144,384]{1,0:T(8,128)(2,1)S(1)}, u32[]{:S(2)}, u32[]{:S(2)}) collective-permute-start(bf16[144,384]{1,0:T(8,128)(2,1)S(1)} %get-tuple-element.64), channel_id=1, source_target_pairs={{8,0},{16,8},{24,16},{0,24},{9,1},{17,9},{25,17},{1,25},{10,2},{18... | collective-permute-start | bytes 331784 | tf_op jit(solution)/shard_map/ppermute | solution.py:744
  14.4 3.8 %collective-permute-start.4 = (bf16[144,256]{1,0:T(8,128)(2,1)S(1)}, bf16[144,256]{1,0:T(8,128)(2,1)S(1)}, u32[]{:S(2)}, u32[]{:S(2)}) collective-permute-start(bf16[144,256]{1,0:T(8,128)(2,1)S(1)} %get-tuple-element.66), channel_id=1, source_target_pairs={{24,0},{0,8},{8,16},{16,24},{25,1},{1,9},{9,17},{17,25},{26,2},{2,... | collective-permute-start | bytes 221192 | tf_op jit(solution)/shard_map/ppermute | solution.py:744
  14.5 3.8 %collective-permute-start.5 = (bf16[144,256]{1,0:T(8,128)(2,1)S(1)}, bf16[144,256]{1,0:T(8,128)(2,1)S(1)}, u32[]{:S(2)}, u32[]{:S(2)}) collective-permute-start(bf16[144,256]{1,0:T(8,128)(2,1)S(1)} %get-tuple-element.67), channel_id=1, source_target_pairs={{8,0},{16,8},{24,16},{0,24},{9,1},{17,9},{25,17},{1,25},{10,2},{18... | collective-permute-start | bytes 221192 | tf_op jit(solution)/shard_map/ppermute | solution.py:744
  18.7 4.0 %collective-permute-start.6 = (bf16[144,128]{1,0:T(8,128)(2,1)S(1)}, bf16[144,128]{1,0:T(8,128)(2,1)S(1)}, u32[]{:S(2)}, u32[]{:S(2)}) collective-permute-start(bf16[144,128]{1,0:T(8,128)(2,1)S(1)} %get-tuple-element.84), channel_id=1, source_target_pairs={{0,1},{1,0},{2,3},{3,2},{4,5},{5,4},{6,7},{7,6},{8,9},{9,8},{10,11... | collective-permute-start | bytes 110600 | tf_op jit(solution)/shard_map/ppermute | solution.py:749
  36.8 8.0 %collective-permute-start.7 = (f32[3,128]{1,0:T(4,128)S(1)}, f32[3,128]{1,0:T(4,128)S(1)}, u32[]{:S(2)}, u32[]{:S(2)}) collective-permute-start(f32[3,128]{1,0:T(4,128)S(1)} %get-tuple-element.94), channel_id=1, source_target_pairs={{0,1},{1,0},{2,3},{3,2},{4,5},{5,4},{6,7},{7,6},{8,9},{9,8},{10,11... | collective-permute-start | bytes 4616 | tf_op jit(solution)/shard_map/ppermute | solution.py:749
  45.0 14.8 %collective-permute-start.8 = (f32[15,128]{1,0:T(8,128)S(1)}, f32[15,128]{1,0:T(8,128)S(1)}, u32[]{:S(2)}, u32[]{:S(2)}) collective-permute-start(f32[15,128]{1,0:T(8,128)S(1)} %get-tuple-element.96), channel_id=1, source_target_pairs={{8,0},{16,8},{24,16},{0,24},{9,1},{17,9},{25,17},{1,25},{10,2},{18... | collective-permute-start | bytes 23048 | tf_op jit(solution)/shard_map/ppermute | solution.py:744
  48.6 11.4 %collective-permute-start.9 = (f32[15,128]{1,0:T(8,128)S(1)}, f32[15,128]{1,0:T(8,128)S(1)}, u32[]{:S(2)}, u32[]{:S(2)}) collective-permute-start(f32[15,128]{1,0:T(8,128)S(1)} %get-tuple-element.97), channel_id=1, source_target_pairs={{24,0},{0,8},{8,16},{16,24},{25,1},{1,9},{9,17},{17,25},{26,2},{2,... | collective-permute-start | bytes 23048 | tf_op jit(solution)/shard_map/ppermute | solution.py:744
  60.0 3.7 %collective-permute-start.10 = (f32[9,128]{1,0:T(8,128)S(1)}, f32[9,128]{1,0:T(8,128)S(1)}, u32[]{:S(2)}, u32[]{:S(2)}) collective-permute-start(f32[9,128]{1,0:T(8,128)S(1)} %get-tuple-element.100), channel_id=1, source_target_pairs={{2,0},{4,2},{6,4},{0,6},{3,1},{5,3},{7,5},{1,7},{10,8},{12,10},{14... | collective-permute-start | bytes 13832 | tf_op jit(solution)/shard_map/ppermute | solution.py:744
  61.3 5.5 %collective-permute-start.11 = (f32[9,128]{1,0:T(8,128)S(1)}, f32[9,128]{1,0:T(8,128)S(1)}, u32[]{:S(2)}, u32[]{:S(2)}) collective-permute-start(f32[9,128]{1,0:T(8,128)S(1)} %get-tuple-element.101), channel_id=1, source_target_pairs={{6,0},{0,2},{2,4},{4,6},{7,1},{1,3},{3,5},{5,7},{14,8},{8,10},{10,... | collective-permute-start | bytes 13832 | tf_op jit(solution)/shard_map/ppermute | solution.py:744

commit v5 on v4

--- a/solution.py
+++ b/solution.py
@@ -255,6 +255,12 @@
     high = jnp.max(jnp.where(line_of, high, -1.0), axis=0, keepdims=True)
     low = jnp.where(high < 0.0, 0.0, low)
     high = jnp.where(high < 0.0, 0.0, high)
+    rest_first = first - (first_blocks - 1.0) * BLOCK
+    rest_second = second - (blocks - first_blocks - 1.0) * BLOCK
+    sparse = jnp.where(rest_first < rest_second, first_blocks, blocks) - 1.0
+    fewest = jnp.minimum(rest_first, rest_second)
+    meta_ref[4:5, :] = jnp.broadcast_to(sparse, (1, LANES)).astype(jnp.int32)
+    meta_ref[5:6, :] = jnp.broadcast_to(fewest, (1, LANES)).astype(jnp.int32)
     meta_ref[0:1, :] = jnp.broadcast_to(first_blocks, (1, LANES)).astype(jnp.int32)
     meta_ref[1:2, :] = jnp.broadcast_to(blocks, (1, LANES)).astype(jnp.int32)
     meta_ref[2:3, :] = low.astype(jnp.int32)
@@ -357,9 +363,17 @@
     def half_of(b):
         return jnp.where(b >= first_blocks, 1, 0)
 
+    sparse, fewest = meta_ref[4, 0], meta_ref[5, 0]
+
     def each_block(run):
-        def sides(at, picked):
-            return [(sets[index], SETS * at + index, at) for index in picked]
+        def sides(at, picked, lanes=eb):
+            listed = []
+            for index in picked:
+                turn = SETS * at + index
+                b = turn + jnp.where(turn >= sparse, 1, 0)
+                b = jnp.where(turn == total_blocks - 1, sparse, b)
+                listed.append((sets[index], b, at, lanes))
+            return listed
 
         def step(at, carry):
             run(sides(at, range(SETS)))
@@ -368,7 +382,11 @@
         lax.fori_loop(0, rounds, step, 0)
         rest = total_blocks - SETS * rounds
 
-        @pl.when(rest == 1)
+        @pl.when(jnp.logical_and(rest == 1, fewest <= LANES))
+        def _():
+            run(sides(rounds, [0], LANES))
+
+        @pl.when(jnp.logical_and(rest == 1, fewest > LANES))
         def _():
             run(sides(rounds, [0]))
 
@@ -380,33 +398,38 @@
         def _():
             run(sides(rounds, [2]))
 
+    def put_row(ref, index, at, value):
+        spare = eb - value.shape[1]
+        if spare:
+            value = jnp.concatenate([value, jnp.zeros((1, spare), f32)], axis=1)
+        ref[index, pl.ds(at, 1), :] = value
+
     def locate(sides):
-        for own_s, b, at in sides:
-            slot_c = centers_ref[b]
-            o = others_ref[b]
+        for own_s, b, at, w in sides:
+            slot_c = centers_ref[b][:, 0:w]
+            o = others_ref[b][:, 0:w]
             c = jnp.maximum(slot_c, 0)
             c_high = lax.shift_right_logical(c, 7)
             o_high = lax.shift_right_logical(o, 7)
             hot_c = one_hot(lax.bitwise_and(c, LANES - 1), LANES).astype(bf16)
             hot_o = one_hot(lax.bitwise_and(o, LANES - 1), LANES).astype(bf16)
             lows = jnp.concatenate([hot_o, hot_c], axis=0)
-            own_s.lows[at] = lows
-            c_high16 = jnp.broadcast_to(c_high, (16, eb))
-            own_s.center_hot[at] = jnp.concatenate(
+            own_s.lows[at, :, 0:w] = lows
+            c_high16 = jnp.broadcast_to(c_high, (16, w))
+            own_s.center_hot[at, :, 0:w] = jnp.concatenate(
                 [masked(hot_c, c_high16, high) for high in range(span // LANES)], axis=0
             )
             both = dot(place_b[...], lows)
-            picked = (both[0 : 3 * hpad] + both[3 * hpad : 6 * hpad]).reshape(3, hpad, eb)
+            picked = (both[0 : 3 * hpad] + both[3 * hpad : 6 * hpad]).reshape(3, hpad, w)
             po = jnp.sum(picked * one_hot(o_high, hpad)[None], axis=1)
             picked = both[6 * hpad :]
-            picked = (picked[0:24] + picked[24:48]).reshape(3, 8, eb)
+            picked = (picked[0:24] + picked[24:48]).reshape(3, 8, w)
             c_whole = c_high + half_of(b) * (span // LANES)
             pc = jnp.sum(picked * one_hot(c_whole, 8)[None], axis=1)
             sep = po - pc
-            row = pl.ds(at, 1)
             for d in range(3):
-                own_s.geo[d, row, :] = sep[d : d + 1]
-            own_s.geo[6, row, :] = jnp.where(slot_c >= 0, 1.0, 0.0)
+                put_row(own_s.geo, d, at, sep[d : d + 1])
+            put_row(own_s.geo, 6, at, jnp.where(slot_c >= 0, 1.0, 0.0))
 
     each_block(locate)
     for own in sets:
@@ -422,28 +445,28 @@
             own.geo[8 + m] = value
 
     def geo_row(side, index):
-        own_s, _, at = side
-        return own_s.geo[index, pl.ds(at, 1), :]
+        own_s, _, at, w = side
+        return own_s.geo[index, pl.ds(at, 1), :][:, 0:w]
 
     def harmonics(side):
         return [None] + [geo_row(side, 8 + m) for m in range(8)]
 
     def prepare(side):
-        own_s, b, at = side
+        own_s, b, at, w = side
         hot = own_s.hot
-        hot_o = own_s.lows[at, 0:LANES, :]
-        o_high = lax.shift_right_logical(others_ref[b], 7) - 2 * meta_ref[2, b]
-        o_high16 = jnp.broadcast_to(o_high, (16, eb))
+        hot_o = own_s.lows[at, 0:LANES, 0:w]
+        o_high = lax.shift_right_logical(others_ref[b][:, 0:w], 7) - 2 * meta_ref[2, b]
+        o_high16 = jnp.broadcast_to(o_high, (16, w))
         for high in range(WINDOW // LANES):
             rows = slice(high * LANES, (high + 1) * LANES)
-            hot[rows, :] = masked(hot_o, o_high16, high)
-        hot[WINDOW : WINDOW + span, :] = own_s.center_hot[at]
-        mu = 0.5 + 0.4 * rows_of((8, eb)).astype(f32)
+            hot[rows, 0:w] = masked(hot_o, o_high16, high)
+        hot[WINDOW : WINDOW + span, 0:w] = own_s.center_hot[at, :, 0:w]
+        mu = 0.5 + 0.4 * rows_of((8, w)).astype(f32)
         u = (geo_row(side, 4) - mu) * 2.0
         upper, lower = halves(jnp.exp(-(u * u)) * geo_row(side, 5))
         radial = jnp.concatenate([upper, lower], axis=0).astype(bf16)
-        hot[WINDOW + span : WINDOW + span + 16, :] = radial
-        hot[WINDOW + span + 16 : WINDOW + span + 32, :] = radial
+        hot[WINDOW + span : WINDOW + span + 16, 0:w] = radial
+        hot[WINDOW + span + 16 : WINDOW + span + 32, 0:w] = radial
 
     def window(group):
         return feat[:, pl.ds(pl.multiple_of(group * 256, 256), WINDOW)]
@@ -453,14 +476,14 @@
         return (meta_ref[3, b] - meta_ref[2, b]) // (WINDOW // 256) + 1
 
     def further_windows(side):
-        own_s, b, _ = side
+        own_s, b, _, w = side
         windows = windows_of(side)
 
         @pl.when(windows > 1)
         def _():
-            o = others_ref[b]
+            o = others_ref[b][:, 0:w]
             hot_o = one_hot(lax.bitwise_and(o, LANES - 1), LANES).astype(bf16)
-            o_high16 = jnp.broadcast_to(lax.shift_right_logical(o, 7), (16, eb))
+            o_high16 = jnp.broadcast_to(lax.shift_right_logical(o, 7), (16, w))
 
             def add(index, carry):
                 group = meta_ref[2, b] + index * (WINDOW // 256)
@@ -471,7 +494,7 @@
                     ],
                     axis=0,
                 )
-                own_s.extra[...] += dot(window(group), hot)
+                own_s.extra[:, 0:w] += dot(window(group), hot)
                 return carry
 
             lax.fori_loop(1, windows, add, 0)
@@ -482,33 +505,33 @@
             side[0].extra[...] = jnp.zeros_like(side[0].extra)
 
     def mix(side):
-        own_s, b, _ = side
+        own_s, b, _, w = side
         tables = jnp.concatenate([window(meta_ref[2, b]), feat_c[half_of(b)]], axis=1)
-        return dot(tables, own_s.hot[...]) + own_s.extra[...]
+        return dot(tables, own_s.hot[:, 0:w]) + own_s.extra[:, 0:w]
 
     def activate(side, mixed):
-        own_s, _, at = side
+        own_s, _, at, w = side
         up = 1.0 + jnp.tanh(mixed)
         value = mixed * up
         latent = value.astype(bf16)
-        own_s.slope[at] = (up + value * (2.0 - up)).astype(bf16)
+        own_s.slope[at, :, 0:w] = (up + value * (2.0 - up)).astype(bf16)
         return latent
 
     def spread(side, latent):
-        own_s, _, at = side
-        own_s.latent[at] = latent
+        own_s, _, at, w = side
+        own_s.latent[at, :, 0:w] = latent
         chan = dot(w_chan_t_ref[...], latent) * geo_row(side, 6)
-        own_s.chan[at] = chan
+        own_s.chan[at, :, 0:w] = chan
         return jnp.concatenate(
             [(chan if h is None else chan * h).astype(bf16) for h in harmonics(side)], axis=0
         )
 
     def gather_tensor(side):
-        own_s, b, at = side
-        return dot(tensor_b[half_of(b)], own_s.center_hot[at])
+        own_s, b, at, w = side
+        return dot(tensor_b[half_of(b)], own_s.center_hot[at, :, 0:w])
 
     def add_tensor(side, products, hot):
-        own_s, b, _ = side
+        own_s, b, _, w = side
         own_s.tensor[half_of(b)] += dot_t(products, hot)
 
     def first_pass(sides):
@@ -522,7 +545,7 @@
         for side, values in zip(sides, mixed):
             products.append(spread(side, activate(side, values)))
         for side, values in zip(sides, products):
-            add_tensor(side, values, side[0].center_hot[side[2]])
+            add_tensor(side, values, side[0].center_hot[side[2], :, 0 : side[3]])
         for side in sides:
             clear_windows(side)
 
@@ -542,28 +565,28 @@
         return jnp.concatenate([band.astype(bf16) for band in bands], axis=0)
 
     def hidden(side, invariant):
-        inputs = jnp.concatenate([side[0].latent[side[2]], invariant], axis=0)
+        inputs = jnp.concatenate([side[0].latent[side[2], :, 0 : side[3]], invariant], axis=0)
         return dot(w_hidden_ref[...], inputs)
 
     def readout(side, pre):
-        own_s, _, at = side
+        own_s, _, at, w = side
         up = 1.0 + jnp.tanh(pre)
         value = pre * up
-        weight = jnp.concatenate([w_out_ref[...]] * (eb // LANES), axis=1)
-        own_s.res[10, pl.ds(at, 1), :] = jnp.sum(value * weight, axis=0, keepdims=True)
+        weight = jnp.concatenate([w_out_ref[...]] * (w // LANES), axis=1)
+        put_row(own_s.res, 10, at, jnp.sum(value * weight, axis=0, keepdims=True))
         scale = 0.5 * geo_row(side, 5) * geo_row(side, 6)
         return ((up + value * (2.0 - up)) * (weight * scale)).astype(bf16)
 
     def unfold(side, back, gathered):
-        own_s, _, at = side
+        own_s, _, at, w = side
         harm = harmonics(side)
-        own_s.dlat[at] = back[0:features].astype(bf16)
+        own_s.dlat[at, :, 0:w] = back[0:features].astype(bf16)
         dbands = [
             back[features + band * chans : features + (band + 1) * chans] for band in range(3)
         ]
         for m in range(1, 9):
             part = gathered[m * chans : (m + 1) * chans]
-            own_s.dharm[at, (m - 1) * 8 : m * 8, :] = fold8(dbands[BANDS[m]] * part)
+            own_s.dharm[at, (m - 1) * 8 : m * 8, 0:w] = fold8(dbands[BANDS[m]] * part)
         return jnp.concatenate(
             [
                 (dbands[BANDS[m]] if harm[m] is None else dbands[BANDS[m]] * harm[m]).astype(bf16)
@@ -577,33 +600,33 @@
         pre = [hidden(side, invariants(side, g)) for side, g in zip(sides, gathered)]
         back = [dot(w_back_ref[...], readout(side, values)) for side, values in zip(sides, pre)]
         for side, values, g in zip(sides, back, gathered):
-            add_tensor(side, unfold(side, values, g), side[0].center_hot[side[2]])
+            add_tensor(side, unfold(side, values, g), side[0].center_hot[side[2], :, 0 : side[3]])
 
     each_block(second_pass)
     tensor_b[...] = (0.125 * sum(own.tensor[...] for own in sets[:SUMS])).astype(bf16)
 
     def channels_back(side, gathered):
-        own_s, _, at = side
+        own_s, _, at, w = side
         harm = harmonics(side)
-        chan = own_s.chan[at]
+        chan = own_s.chan[at, :, 0:w]
         dchan = gathered[0:chans]
         for m in range(1, 9):
             part = gathered[m * chans : (m + 1) * chans]
             dchan = dchan + part * harm[m]
-            total = own_s.dharm[at, (m - 1) * 8 : m * 8, :] + fold8(part * chan)
-            own_s.res[m - 1, pl.ds(at, 1), :] = jnp.sum(total, axis=0, keepdims=True)
+            total = own_s.dharm[at, (m - 1) * 8 : m * 8, 0:w] + fold8(part * chan)
+            put_row(own_s.res, m - 1, at, jnp.sum(total, axis=0, keepdims=True))
         return (dchan * geo_row(side, 6)).astype(bf16)
 
     def radial_back(side, dchan):
-        own_s, _, at = side
-        dlat = own_s.dlat[at] + dot(w_chan_ref[...], dchan).astype(bf16)
-        drad = dot(w_rbf_ref[...], dlat * own_s.slope[at])
+        own_s, _, at, w = side
+        dlat = own_s.dlat[at, :, 0:w] + dot(w_chan_ref[...], dchan).astype(bf16)
+        drad = dot(w_rbf_ref[...], dlat * own_s.slope[at, :, 0:w])
         drad = drad[0:8] + drad[8:16]
-        mu = 0.5 + 0.4 * rows_of((8, eb)).astype(f32)
+        mu = 0.5 + 0.4 * rows_of((8, w)).astype(f32)
         u = (geo_row(side, 4) - mu) * 2.0
         weighted = drad * jnp.exp(-(u * u))
-        own_s.res[8, pl.ds(at, 1), :] = jnp.sum(weighted, axis=0, keepdims=True)
-        own_s.res[9, pl.ds(at, 1), :] = jnp.sum(weighted * u, axis=0, keepdims=True)
+        put_row(own_s.res, 8, at, jnp.sum(weighted, axis=0, keepdims=True))
+        put_row(own_s.res, 9, at, jnp.sum(weighted * u, axis=0, keepdims=True))
 
     def third_pass(sides):
         gathered = [gather_tensor(side) for side in sides]
@@ -632,11 +655,11 @@
             own.res[index], own.res[4 + index] = halves(value)
 
     def collect(sides):
-        for own_s, b, at in sides:
-            split = [own_s.res[index, pl.ds(at, 1), :] for index in range(8)]
-            mask_o = one_hot(lax.shift_right_logical(others_ref[b], 7), hpad)
+        for own_s, b, at, w in sides:
+            split = [own_s.res[index, pl.ds(at, 1), :][:, 0:w] for index in range(8)]
+            mask_o = one_hot(lax.shift_right_logical(others_ref[b][:, 0:w], 7), hpad)
             values = jnp.concatenate(split, axis=0)
-            c_high = lax.shift_right_arithmetic(centers_ref[b], 7)
+            c_high = lax.shift_right_arithmetic(centers_ref[b][:, 0:w], 7)
             rows = jnp.concatenate(
                 [mask_o * split[4 * part + d] for part in range(2) for d in range(3)]
                 + [
@@ -645,7 +668,7 @@
                 ],
                 axis=0,
             ).astype(bf16)
-            own_s.acc[half_of(b)] += dot_t(rows, own_s.lows[at])
+            own_s.acc[half_of(b)] += dot_t(rows, own_s.lows[at, :, 0:w])
 
     each_block(collect)
     acc = [sum(own.acc[half] for own in sets[:SUMS]) for half in range(halves_n)]
@@ -806,7 +829,7 @@
         (
             shape((slot_rows, LANES), jnp.int32),
             shape((slot_rows, LANES), jnp.int32),
-            shape((4, LANES), jnp.int32),
+            shape((6, LANES), jnp.int32),
         ),
         (count, ends),
         [

time: 67.3 us -> 68.2 us (1.013); the launches traced: 67.8 us -> 67.3 us
  starting transfers between devices: 33.1 us -> 24.8 us
  Pallas kernels: 19.7 us -> 24.1 us
  waiting for transfers between devices: 8.8 us -> 12.3 us
    ppermute x2, starting transfers between devices: 8.15 us -> 1.72 us  [swapped(): return lax.ppermute(x, 'gz', [(i, i ^ 1) for i in range(count)])]
    pallas_call x10, Pallas kernels: 19.7 us -> 24.1 us  [call(): pl.pallas_call(kernel, out_shape=out_shape, in_specs=[scalar] * smem + [v...]
    ppermute x2, waiting for transfers between devices: 3.11 us -> 5.13 us  [swapped(): return lax.ppermute(x, 'gz', [(i, i ^ 1) for i in range(count)])]
    ppermute x10, starting transfers between devices: 24.9 us -> 23 us  [shifted(): lax.ppermute(x, axis, [((i + step) % count, i) for i in range(count)])]
    ppermute x10, waiting for transfers between devices: 5.69 us -> 7.12 us  [shifted(): lax.ppermute(x, axis, [((i + step) % count, i) for i in range(count)])]
where the time goes in v5:
time: 68.2 us; the launch traced here: 67.3 us
  starting transfers between devices  24.8 us (36%)
  Pallas kernels  24.1 us (35%)
  waiting for transfers between devices  12.3 us (18%)
  other arithmetic  3.19 us (5%)
  local copies, waits for them, and re-layouts  1.59 us (2%)
  between operations  1.39 us (2%)
    pallas_call x10, Pallas kernels, call(): pl.pallas_call(kernel, out_shape=out_shape, in_specs=[scalar] * smem + [v...  24.1 us
    ppermute x10, starting transfers between devices, shifted(): lax.ppermute(x, axis, [((i + step) % count, i) for i in range(count)])  23 us
    ppermute x10, waiting for transfers between devices, shifted(): lax.ppermute(x, axis, [((i + step) % count, i) for i in range(count)])  7.12 us
    ppermute x2, waiting for transfers between devices, swapped(): return lax.ppermute(x, 'gz', [(i, i ^ 1) for i in range(count)])  5.13 us
    ppermute x2, starting transfers between devices, swapped(): return lax.ppermute(x, 'gz', [(i, i ^ 1) for i in range(count)])  1.72 us
    unnamed x4, local copies, waits for them, and re-layouts  1.59 us
  transfers between devices with their start and end apart: 12, of which 6 were waited for; matrix products, arithmetic and copies ran while one was open for 4% of the time, Pallas kernels for 5%

profile of v5, /device:TPU:0, one launch (start us, length us, event | category | flops | bytes accessed | tf_op | source)
XLA Modules:
  0.0 67.3 jit_solution(6298182065654586969)
XLA Ops:
  0.6 0.7 %pad_add_fusion.1.picks_ref = s32[9,128]{1,0:T(8,128)S(1)} fusion(s32[1,128]{1,0:T(1,128)} %bitcast.27, s32[8,128]{1,0:T(8,128)} %bitcast.25), kind=kLoop, calls=%fused_computation.3 | loop fusion | flops 1152 | bytes 9216 | tf_op jit(solution)/shard_map/concatenate | solution.py:812
  1.3 0.9 %copy-done = bf16[1,1,1,512,128]{4,3,2,1,0:T(8,128)(2,1)S(1)} copy-done((bf16[1,1,1,512,128]{4,3,2,1,0:T(8,128)(2,1)S(1)}, bf16[1,1,1,512,128]{4,3,2,1,0:T(8,128)(2,1)}, u32[]{:S(2)}) %copy-start) | copy-done | bytes 131096
  2.2 0.7 %copy-done.1 = f32[1,1,1,3,512]{4,2,3,1,0:T(1,128)S(1)} copy-done((f32[1,1,1,3,512]{4,2,3,1,0:T(1,128)S(1)}, f32[1,1,1,3,512]{4,2,3,1,0:T(1,128)}, u32[]{:S(2)}) %copy-start.1) | copy-done | bytes 6168
  3.5 3.1 %collective-permute-start = (bf16[144,384]{1,0:T(8,128)(2,1)S(1)}, bf16[144,384]{1,0:T(8,128)(2,1)S(1)}, u32[]{:S(2)}, u32[]{:S(2)}) collective-permute-start(bf16[144,384]{1,0:T(8,128)(2,1)S(1)} %get-tuple-element.52), channel_id=1, source_target_pairs={{6,0},{0,2},{2,4},{4,6},{7,1},{1,3},{3,5},{5,7},{14,8},{8,10},{10,... | collective-permute-start | bytes 331784 | tf_op jit(solution)/shard_map/ppermute | solution.py:767
  6.6 2.1 %collective-permute-start.1 = (bf16[144,384]{1,0:T(8,128)(2,1)S(1)}, bf16[144,384]{1,0:T(8,128)(2,1)S(1)}, u32[]{:S(2)}, u32[]{:S(2)}) collective-permute-start(bf16[144,384]{1,0:T(8,128)(2,1)S(1)} %get-tuple-element.53), channel_id=1, source_target_pairs={{2,0},{4,2},{6,4},{0,6},{3,1},{5,3},{7,5},{1,7},{10,8},{12,10},{14... | collective-permute-start | bytes 331784 | tf_op jit(solution)/shard_map/ppermute | solution.py:767
  8.7 1.7 %collective-permute-start.3 = (bf16[144,384]{1,0:T(8,128)(2,1)S(1)}, bf16[144,384]{1,0:T(8,128)(2,1)S(1)}, u32[]{:S(2)}, u32[]{:S(2)}) collective-permute-start(bf16[144,384]{1,0:T(8,128)(2,1)S(1)} %get-tuple-element.64), channel_id=1, source_target_pairs={{8,0},{16,8},{24,16},{0,24},{9,1},{17,9},{25,17},{1,25},{10,2},{18... | collective-permute-start | bytes 331784 | tf_op jit(solution)/shard_map/ppermute | solution.py:767
  11.1 0.8 %pad_add_fusion.ends_ref = s32[96,128]{1,0:T(8,128)S(1)} fusion(s32[48,128]{1,0:T(8,128)} %bitcast.22, s32[48,128]{1,0:T(8,128)} %bitcast.23), kind=kLoop, calls=%fused_computation.1 | loop fusion | flops 12288 | bytes 98304 | tf_op jit(solution)/shard_map/concatenate | solution.py:824
  11.9 2.5 %shard_map.141 = (s32[56,128]{1,0:T(8,128)S(1)}, s32[56,128]{1,0:T(8,128)S(1)}, s32[6,128]{1,0:T(8,128)S(1)}) custom-call(s32[1]{0:T(128)} %bitcast.16.count_ref, s32[96,128]{1,0:T(8,128)S(1)} %pad_add_fusion.ends_ref), custom_call_target="tpu_custom_call" | custom-call | tf_op jit(solution)/shard_map/pallas_call | solution.py:755
  14.5 1.7 %collective-permute-start.5 = (bf16[144,256]{1,0:T(8,128)(2,1)S(1)}, bf16[144,256]{1,0:T(8,128)(2,1)S(1)}, u32[]{:S(2)}, u32[]{:S(2)}) collective-permute-start(bf16[144,256]{1,0:T(8,128)(2,1)S(1)} %get-tuple-element.67), channel_id=1, source_target_pairs={{8,0},{16,8},{24,16},{0,24},{9,1},{17,9},{25,17},{1,25},{10,2},{18... | collective-permute-start | bytes 221192 | tf_op jit(solution)/shard_map/ppermute | solution.py:767
  16.2 1.0 %pad_maximum_fusion.stacked_ref = bf16[640,256]{1,0:T(8,128)(2,1)S(1)} fusion(bf16[64,256]{1,0:T(8,128)(2,1)} %bitcast.21, bf16[192,256]{1,0:T(8,128)(2,1)} %param.24, bf16[256,256]{1,0:T(8,128)(2,1)} %param.23, bf16[128,256]{1,0:T(8,128)(2,1)} %param.20), kind=kLoop, calls=%fused_computation | loop fusion | flops 1310720 | bytes 655360 | tf_op jit(solution)/shard_map/concatenate | solution.py:867
  17.2 0.7 %pad_maximum_fusion.1.small_ref = f32[9,256]{1,0:T(8,128)S(1)} fusion(f32[1,256]{1,0:T(1,128)} %bitcast.26, f32[8,256]{1,0:T(8,128)} %param.21), kind=kLoop, calls=%fused_computation.2 | loop fusion | flops 2304 | bytes 18432 | tf_op jit(solution)/shard_map/concatenate | solution.py:868
  18.7 1.7 %collective-permute-start.6 = (bf16[144,128]{1,0:T(8,128)(2,1)S(1)}, bf16[144,128]{1,0:T(8,128)(2,1)S(1)}, u32[]{:S(2)}, u32[]{:S(2)}) collective-permute-start(bf16[144,128]{1,0:T(8,128)(2,1)S(1)} %get-tuple-element.84), channel_id=1, source_target_pairs={{0,1},{1,0},{2,3},{3,2},{4,5},{5,4},{6,7},{7,6},{8,9},{9,8},{10,11... | collective-permute-start | bytes 110600 | tf_op jit(solution)/shard_map/ppermute | solution.py:772
  20.4 0.7 %shard_map.145 = (bf16[256,2560]{1,0:T(8,128)(2,1)S(1)}, f32[6,24,128]{2,1,0:T(8,128)S(1)}) custom-call(bf16[144,2560]{1,0:T(8,128)(2,1)S(1)} %get-tuple-element.80.inner_ref, bf16[256,128]{1,0:T(8,128)(2,1)S(1)} %get-tuple-element.81.w_emb_ref), custom_call_target="tpu_custom_call" | custom-call | tf_op jit(solution)/shard_map/pallas_call | solution.py:755
  21.1 1.5 %collective-permute-done.6.slab_ref = bf16[144,128]{1,0:T(8,128)(2,1)S(1)} collective-permute-done((bf16[144,128]{1,0:T(8,128)(2,1)S(1)}, bf16[144,128]{1,0:T(8,128)(2,1)S(1)}, u32[]{:S(2)}, u32[]{:S(2)}) %collective-permute-start.6) | collective-permute-done | bytes 36896 | tf_op jit(solution)/shard_map/ppermute | solution.py:772
  22.7 18.5 %shard_map.146 = (f32[3,24,128]{2,1,0:T(8,128)S(1)}, f32[3,128]{1,0:T(4,128)S(1)}, f32[1,512]{1,0:T(1,128)}) custom-call(s32[6,128]{1,0:T(8,128)S(1)} %get-tuple-element.57.meta_ref, f32[1]{0:T(128)} %bitcast.7.lift_ref, s32[14,1,512]{2,1,0:T(1,128)S(1)} %bitcast.18, s32[14,1,512]{2,1,0:T(1,128)S(1)} %bitcast.19, ...), custom_call_target="tpu_custom_call" | custom-call | tf_op jit(solution)/shard_map/pallas_call | solution.py:755
  41.2 3.6 %collective-permute-done.7.back_ref = f32[3,128]{1,0:T(4,128)S(1)} collective-permute-done((f32[3,128]{1,0:T(4,128)S(1)}, f32[3,128]{1,0:T(4,128)S(1)}, u32[]{:S(2)}, u32[]{:S(2)}) %collective-permute-start.7) | collective-permute-done | bytes 1568 | tf_op jit(solution)/shard_map/ppermute | solution.py:772
  45.0 7.7 %collective-permute-start.8 = (f32[15,128]{1,0:T(8,128)S(1)}, f32[15,128]{1,0:T(8,128)S(1)}, u32[]{:S(2)}, u32[]{:S(2)}) collective-permute-start(f32[15,128]{1,0:T(8,128)S(1)} %get-tuple-element.96), channel_id=1, source_target_pairs={{8,0},{16,8},{24,16},{0,24},{9,1},{17,9},{25,17},{1,25},{10,2},{18... | collective-permute-start | bytes 23048 | tf_op jit(solution)/shard_map/ppermute | solution.py:767
  52.7 1.4 %collective-permute-done.8.from_xp_ref = f32[15,128]{1,0:T(8,128)S(1)} collective-permute-done((f32[15,128]{1,0:T(8,128)S(1)}, f32[15,128]{1,0:T(8,128)S(1)}, u32[]{:S(2)}, u32[]{:S(2)}) %collective-permute-start.8) | collective-permute-done | bytes 7712 | tf_op jit(solution)/shard_map/ppermute | solution.py:767
  54.0 1.7 %collective-permute-done.9.from_xm_ref = f32[15,128]{1,0:T(8,128)S(1)} collective-permute-done((f32[15,128]{1,0:T(8,128)S(1)}, f32[15,128]{1,0:T(8,128)S(1)}, u32[]{:S(2)}, u32[]{:S(2)}) %collective-permute-start.9) | collective-permute-done | bytes 7712 | tf_op jit(solution)/shard_map/ppermute | solution.py:767
  55.7 5.2 %collective-permute-start.10 = (f32[9,128]{1,0:T(8,128)S(1)}, f32[9,128]{1,0:T(8,128)S(1)}, u32[]{:S(2)}, u32[]{:S(2)}) collective-permute-start(f32[9,128]{1,0:T(8,128)S(1)} %get-tuple-element.100), channel_id=1, source_target_pairs={{2,0},{4,2},{6,4},{0,6},{3,1},{5,3},{7,5},{1,7},{10,8},{12,10},{14... | collective-permute-start | bytes 13832 | tf_op jit(solution)/shard_map/ppermute | solution.py:767
  61.0 1.4 %collective-permute-start.11 = (f32[9,128]{1,0:T(8,128)S(1)}, f32[9,128]{1,0:T(8,128)S(1)}, u32[]{:S(2)}, u32[]{:S(2)}) collective-permute-start(f32[9,128]{1,0:T(8,128)S(1)} %get-tuple-element.101), channel_id=1, source_target_pairs={{6,0},{0,2},{2,4},{4,6},{7,1},{1,3},{3,5},{5,7},{14,8},{8,10},{10,... | collective-permute-start | bytes 13832 | tf_op jit(solution)/shard_map/ppermute | solution.py:767
  62.4 1.6 %collective-permute-done.10.from_yp_ref = f32[9,128]{1,0:T(8,128)S(1)} collective-permute-done((f32[9,128]{1,0:T(8,128)S(1)}, f32[9,128]{1,0:T(8,128)S(1)}, u32[]{:S(2)}, u32[]{:S(2)}) %collective-permute-start.10) | collective-permute-done | bytes 4640 | tf_op jit(solution)/shard_map/ppermute | solution.py:767
  64.0 2.5 %collective-permute-done.11.from_ym_ref = f32[9,128]{1,0:T(8,128)S(1)} collective-permute-done((f32[9,128]{1,0:T(8,128)S(1)}, f32[9,128]{1,0:T(8,128)S(1)}, u32[]{:S(2)}, u32[]{:S(2)}) %collective-permute-start.11) | collective-permute-done | bytes 4640 | tf_op jit(solution)/shard_map/ppermute | solution.py:767
  66.4 0.9 %shard_map.149 = f32[3,1,512]{2,1,0:T(1,128)} custom-call(f32[3,8,128]{2,1,0:T(8,128)S(1)} %get-tuple-element.95.own_ref, s32[9,128]{1,0:T(8,128)S(1)} %pad_add_fusion.1.picks_ref, f32[15,128]{1,0:T(8,128)S(1)} %collective-permute-done.8.from_xp_ref, f32[15,128]{1,0:T(8,128)S(1)} %collective-permute-done.9.from_xm_ref, ...), custom_call_target="tpu_custom_call" | custom-call | tf_op jit(solution)/shard_map/pallas_call | solution.py:755
  (18 shorter events, 1.6 us)
Async XLA Ops:
  1.3 0.9 %copy-start = (bf16[1,1,1,512,128]{4,3,2,1,0:T(8,128)(2,1)S(1)}, bf16[1,1,1,512,128]{4,3,2,1,0:T(8,128)(2,1)}, u32[]{:S(2)}) copy-start(bf16[1,1,1,512,128]{4,3,2,1,0:T(8,128)(2,1)} %param.14) | copy-start | bytes 393220
  2.2 0.7 %copy-start.1 = (f32[1,1,1,3,512]{4,2,3,1,0:T(1,128)S(1)}, f32[1,1,1,3,512]{4,2,3,1,0:T(1,128)}, u32[]{:S(2)}) copy-start(f32[1,1,1,3,512]{4,2,3,1,0:T(1,128)} %param.13) | copy-start | bytes 18436
  3.5 10.8 %collective-permute-start = (bf16[144,384]{1,0:T(8,128)(2,1)S(1)}, bf16[144,384]{1,0:T(8,128)(2,1)S(1)}, u32[]{:S(2)}, u32[]{:S(2)}) collective-permute-start(bf16[144,384]{1,0:T(8,128)(2,1)S(1)} %get-tuple-element.52), channel_id=1, source_target_pairs={{6,0},{0,2},{2,4},{4,6},{7,1},{1,3},{3,5},{5,7},{14,8},{8,10},{10,... | collective-permute-start | bytes 331784 | tf_op jit(solution)/shard_map/ppermute | solution.py:767
  6.6 7.7 %collective-permute-start.1 = (bf16[144,384]{1,0:T(8,128)(2,1)S(1)}, bf16[144,384]{1,0:T(8,128)(2,1)S(1)}, u32[]{:S(2)}, u32[]{:S(2)}) collective-permute-start(bf16[144,384]{1,0:T(8,128)(2,1)S(1)} %get-tuple-element.53), channel_id=1, source_target_pairs={{2,0},{4,2},{6,4},{0,6},{3,1},{5,3},{7,5},{1,7},{10,8},{12,10},{14... | collective-permute-start | bytes 331784 | tf_op jit(solution)/shard_map/ppermute | solution.py:767
  8.7 9.5 %collective-permute-start.2 = (bf16[144,384]{1,0:T(8,128)(2,1)S(1)}, bf16[144,384]{1,0:T(8,128)(2,1)S(1)}, u32[]{:S(2)}, u32[]{:S(2)}) collective-permute-start(bf16[144,384]{1,0:T(8,128)(2,1)S(1)} %get-tuple-element.63), channel_id=1, source_target_pairs={{24,0},{0,8},{8,16},{16,24},{25,1},{1,9},{9,17},{17,25},{26,2},{2,... | collective-permute-start | bytes 331784 | tf_op jit(solution)/shard_map/ppermute | solution.py:767
  8.7 9.6 %collective-permute-start.3 = (bf16[144,384]{1,0:T(8,128)(2,1)S(1)}, bf16[144,384]{1,0:T(8,128)(2,1)S(1)}, u32[]{:S(2)}, u32[]{:S(2)}) collective-permute-start(bf16[144,384]{1,0:T(8,128)(2,1)S(1)} %get-tuple-element.64), channel_id=1, source_target_pairs={{8,0},{16,8},{24,16},{0,24},{9,1},{17,9},{25,17},{1,25},{10,2},{18... | collective-permute-start | bytes 331784 | tf_op jit(solution)/shard_map/ppermute | solution.py:767
  14.4 3.8 %collective-permute-start.4 = (bf16[144,256]{1,0:T(8,128)(2,1)S(1)}, bf16[144,256]{1,0:T(8,128)(2,1)S(1)}, u32[]{:S(2)}, u32[]{:S(2)}) collective-permute-start(bf16[144,256]{1,0:T(8,128)(2,1)S(1)} %get-tuple-element.66), channel_id=1, source_target_pairs={{24,0},{0,8},{8,16},{16,24},{25,1},{1,9},{9,17},{17,25},{26,2},{2,... | collective-permute-start | bytes 221192 | tf_op jit(solution)/shard_map/ppermute | solution.py:767
  14.5 3.8 %collective-permute-start.5 = (bf16[144,256]{1,0:T(8,128)(2,1)S(1)}, bf16[144,256]{1,0:T(8,128)(2,1)S(1)}, u32[]{:S(2)}, u32[]{:S(2)}) collective-permute-start(bf16[144,256]{1,0:T(8,128)(2,1)S(1)} %get-tuple-element.67), channel_id=1, source_target_pairs={{8,0},{16,8},{24,16},{0,24},{9,1},{17,9},{25,17},{1,25},{10,2},{18... | collective-permute-start | bytes 221192 | tf_op jit(solution)/shard_map/ppermute | solution.py:767
  18.7 4.0 %collective-permute-start.6 = (bf16[144,128]{1,0:T(8,128)(2,1)S(1)}, bf16[144,128]{1,0:T(8,128)(2,1)S(1)}, u32[]{:S(2)}, u32[]{:S(2)}) collective-permute-start(bf16[144,128]{1,0:T(8,128)(2,1)S(1)} %get-tuple-element.84), channel_id=1, source_target_pairs={{0,1},{1,0},{2,3},{3,2},{4,5},{5,4},{6,7},{7,6},{8,9},{9,8},{10,11... | collective-permute-start | bytes 110600 | tf_op jit(solution)/shard_map/ppermute | solution.py:772
  41.2 3.6 %collective-permute-start.7 = (f32[3,128]{1,0:T(4,128)S(1)}, f32[3,128]{1,0:T(4,128)S(1)}, u32[]{:S(2)}, u32[]{:S(2)}) collective-permute-start(f32[3,128]{1,0:T(4,128)S(1)} %get-tuple-element.94), channel_id=1, source_target_pairs={{0,1},{1,0},{2,3},{3,2},{4,5},{5,4},{6,7},{7,6},{8,9},{9,8},{10,11... | collective-permute-start | bytes 4616 | tf_op jit(solution)/shard_map/ppermute | solution.py:772
  45.0 9.0 %collective-permute-start.8 = (f32[15,128]{1,0:T(8,128)S(1)}, f32[15,128]{1,0:T(8,128)S(1)}, u32[]{:S(2)}, u32[]{:S(2)}) collective-permute-start(f32[15,128]{1,0:T(8,128)S(1)} %get-tuple-element.96), channel_id=1, source_target_pairs={{8,0},{16,8},{24,16},{0,24},{9,1},{17,9},{25,17},{1,25},{10,2},{18... | collective-permute-start | bytes 23048 | tf_op jit(solution)/shard_map/ppermute | solution.py:767
  52.7 3.1 %collective-permute-start.9 = (f32[15,128]{1,0:T(8,128)S(1)}, f32[15,128]{1,0:T(8,128)S(1)}, u32[]{:S(2)}, u32[]{:S(2)}) collective-permute-start(f32[15,128]{1,0:T(8,128)S(1)} %get-tuple-element.97), channel_id=1, source_target_pairs={{24,0},{0,8},{8,16},{16,24},{25,1},{1,9},{9,17},{17,25},{26,2},{2,... | collective-permute-start | bytes 23048 | tf_op jit(solution)/shard_map/ppermute | solution.py:767
  55.7 8.2 %collective-permute-start.10 = (f32[9,128]{1,0:T(8,128)S(1)}, f32[9,128]{1,0:T(8,128)S(1)}, u32[]{:S(2)}, u32[]{:S(2)}) collective-permute-start(f32[9,128]{1,0:T(8,128)S(1)} %get-tuple-element.100), channel_id=1, source_target_pairs={{2,0},{4,2},{6,4},{0,6},{3,1},{5,3},{7,5},{1,7},{10,8},{12,10},{14... | collective-permute-start | bytes 13832 | tf_op jit(solution)/shard_map/ppermute | solution.py:767
  61.0 5.4 %collective-permute-start.11 = (f32[9,128]{1,0:T(8,128)S(1)}, f32[9,128]{1,0:T(8,128)S(1)}, u32[]{:S(2)}, u32[]{:S(2)}) collective-permute-start(f32[9,128]{1,0:T(8,128)S(1)} %get-tuple-element.101), channel_id=1, source_target_pairs={{6,0},{0,2},{2,4},{4,6},{7,1},{1,3},{3,5},{5,7},{14,8},{8,10},{10,... | collective-permute-start | bytes 13832 | tf_op jit(solution)/shard_map/ppermute | solution.py:767
